TPU v7x, 32 devices: a whole 2x2x4 slice. The times are simulated.
32 devices in a mesh: section: 4 (over y, x), dp: 8 (over z, core).
Axes of the slice: x: 2, y: 2, z: 4, core: 2. Of those that a mesh axis runs over, the one named last changes fastest.
Arguments:
- bottom_tier_source: bfloat16 [2, 1024, 1024], P(None, 'dp'), may hold values from -6 to 6
- topmost_emitted_cotangent: bfloat16 [2, 1024, 1024], P(None, 'dp'), may hold values from -6 to 6
- packed_span_sizes: int32 [2, 5], replicated, may hold values from 1 to 1020, as said below
- attention_standardize_scale: float32 [4, 1024], P('section'), may hold values from 0.5 to 1.5
- attention_standardize_offset: float32 [4, 1024], P('section'), may hold values from -1 to 1
- lagged_lookup_mix: float32 [4, 1024], P('section'), may hold values from 0.05 to 0.95
- lagged_payload_mix: float32 [4, 1024], P('section'), may hold values from 0.05 to 0.95
- lagged_sigmoid_mix: float32 [4, 1024], P('section'), may hold values from 0.05 to 0.95
- fading_rate_logarithm: float32 [4, 1024], P('section'), may hold values from -9 to -3.5
- present_element_extra: float32 [4, 1024], P('section'), may hold values from -1 to 1
- lookup_projection: bfloat16 [4, 1024, 1024], P('section'), may hold values from -0.1875 to 0.1875
- payload_projection: bfloat16 [4, 1024, 1024], P('section'), may hold values from -0.1875 to 0.1875
- sigmoid_projection: bfloat16 [4, 1024, 1024], P('section'), may hold values from -0.1875 to 0.1875
- attention_emit_projection: bfloat16 [4, 1024, 1024], P('section'), may hold values from -0.75 to 0.75
- feedforward_standardize_scale: float32 [4, 1024], P('section'), may hold values from 0.5 to 1.5
- feedforward_standardize_offset: float32 [4, 1024], P('section'), may hold values from -1 to 1
- lagged_feedforward_lookup_mix: float32 [4, 1024], P('section'), may hold values from 0.05 to 0.95
- lagged_feedforward_sigmoid_mix: float32 [4, 1024], P('section'), may hold values from 0.05 to 0.95
- feedforward_lookup_projection: bfloat16 [4, 1024, 4096], P('section'), may hold values from -0.1875 to 0.1875
- feedforward_payload_projection: bfloat16 [4, 4096, 1024], P('section'), may hold values from -0.09375 to 0.09375
- feedforward_sigmoid_projection: bfloat16 [4, 1024, 1024], P('section'), may hold values from -0.1875 to 0.1875
Outputs:
- layer_output: bfloat16 [4, 2, 1024, 1024], P('section', None, 'dp')
- input_grad: bfloat16 [4, 2, 1024, 1024], P('section', None, 'dp')
- norm_gain_grad: float32 [4, 1024], P('section', 'dp')
- norm_bias_grad: float32 [4, 1024], P('section', 'dp')
- shift_key_grad: float32 [4, 1024], P('section', 'dp')
- shift_value_grad: float32 [4, 1024], P('section', 'dp')
- shift_gate_grad: float32 [4, 1024], P('section', 'dp')
- decay_rate_grad: float32 [4, 1024], P('section', 'dp')
- first_bonus_grad: float32 [4, 1024], P('section', 'dp')
- key_weight_grad: float32 [4, 1024, 1024], P('section', 'dp')
- value_weight_grad: float32 [4, 1024, 1024], P('section', 'dp')
- gate_weight_grad: float32 [4, 1024, 1024], P('section', 'dp')
- output_weight_grad: float32 [4, 1024, 1024], P('section', 'dp')
- second_gain_grad: float32 [4, 1024], P('section', 'dp')
- second_bias_grad: float32 [4, 1024], P('section', 'dp')
- shift_hidden_grad: float32 [4, 1024], P('section', 'dp')
- shift_filter_grad: float32 [4, 1024], P('section', 'dp')
- hidden_weight_grad: float32 [4, 1024, 4096], P('section', 'dp')
- project_weight_grad: float32 [4, 4096, 1024], P('section', 'dp')
- filter_weight_grad: float32 [4, 1024, 1024], P('section', 'dp')
Inputs may be any that keep to these rules, and one draw needn't show every extreme that they name: `packed_span_sizes`: in each micro-batch the lengths sum to 1024; the second sequence begins within the first 128 tokens and ends within the last 128 tokens; the first micro-batch's lengths are 1, 1020, 1, 1, 1.
All inputs are finite; a program needn't handle non-finite values.
Results may differ from a plain program's by a relative error of at most 0.02.
Values may be sent and summed in bfloat16 or wider, within the bound.
A program may use at most 320 MiB of HBM per device.

v0:
```python
from functools import partial

import jax
import jax.numpy as jnp
from jax import lax
from jax.sharding import PartitionSpec as P

EPS = 1e-05


def entering(x, axis, combine, identity, reverse):
    peers, position = (lax.axis_size(axis), lax.axis_index(axis))
    everything = jax.tree.map(lambda part: lax.all_gather(part, axis), x)
    start = jax.tree.map(
        lambda part, zero: jnp.broadcast_to(jnp.asarray(zero, part.dtype), part.shape), x, identity
    )

    def turn(k, before):
        at = peers - 1 - k if reverse else k
        reached = at > position if reverse else at < position
        new = combine(before, jax.tree.map(lambda part: part[at], everything))
        return jax.tree.map(lambda a, b: jnp.where(reached, a, b), new, before)

    return lax.fori_loop(0, peers, turn, start)


def passed_along(x, axis, by):
    peers = lax.axis_size(axis)
    pairs = [(i, i + by) for i in range(peers) if 0 <= i + by < peers]
    return lax.ppermute(x, axis, pairs)


def layer_norm(source, attention_standardize_scale, attention_standardize_offset):
    average = jnp.mean(source, axis=-1, keepdims=True)
    centred = source - average
    variance = jnp.mean(centred * centred, axis=-1, keepdims=True)
    return (
        centred * lax.rsqrt(variance + EPS) * attention_standardize_scale
        + attention_standardize_offset
    )


def combine_pairs(earlier, later_part):
    return (
        earlier[0] * later_part[0],
        later_part[0] * earlier[1] + later_part[1],
        later_part[0] * earlier[2] + later_part[2],
    )


def matmul_rows(left_rows, weight):
    return jnp.dot(left_rows, weight, preferred_element_type=jnp.float32)


def exact_rows(mixing, rows):
    return jnp.dot(
        mixing, rows, preferred_element_type=jnp.float32, precision=lax.Precision.HIGHEST
    )


def outer_sum(left_rows, right_rows):
    return lax.dot_general(
        left_rows, right_rows, (((0,), (0,)), ((), ())), preferred_element_type=jnp.float32
    )


def back_dot(gradient, weight):
    return lax.dot_general(
        gradient, weight, (((1,), (1,)), ((), ())), preferred_element_type=jnp.float32
    )


def blend_rows(normed, earlier, coefficient):
    return normed * coefficient + earlier * (1.0 - coefficient)


def blend_back(gradient, normed, earlier, coefficient):
    return (
        gradient * coefficient,
        gradient * (1.0 - coefficient),
        jnp.sum(gradient * (normed - earlier), axis=0),
    )


def shift_down(rows, first_row):
    extent = rows.shape[0]
    places = jnp.arange(extent, dtype=jnp.int32)
    mover = (places[:, None] == places[None, :] + 1).astype(jnp.float32)
    opening = (places == 0).astype(jnp.float32)[:, None]
    return exact_rows(mover, rows) + opening * jnp.reshape(first_row, (1, -1))


def shift_up(rows, last_row):
    extent = rows.shape[0]
    places = jnp.arange(extent, dtype=jnp.int32)
    mover = (places[:, None] + 1 == places[None, :]).astype(jnp.float32)
    closing = (places == extent - 1).astype(jnp.float32)[:, None]
    return exact_rows(mover, rows) + closing * jnp.reshape(last_row, (1, -1))


def keep_rows(lengths, offset, row_count):
    starts = jnp.cumsum(lengths) - lengths
    position = offset + jnp.arange(row_count, dtype=jnp.int32)
    hits = jnp.any(position[:, None] == starts[None, :], axis=1)
    return jnp.where(hits, 0.0, 1.0).astype(jnp.float32)


def recurrence_summary(
    lookup_projected_vectors, payload_vectors, fading_rate_logarithm, retain_mask
):
    extent = lookup_projected_vectors.shape[0]
    places = jnp.arange(extent, dtype=jnp.int32)
    lower = places[:, None] >= places[None, :]
    resets = (1.0 - retain_mask)[:, None]
    segment = exact_rows(lower.astype(jnp.float32), resets)[:, 0]
    same_span = (lower & (segment[:, None] == segment[None, :])).astype(jnp.float32)
    rate = jnp.exp(fading_rate_logarithm)[None, :]
    position = places.astype(jnp.float32)[:, None]
    growing = jnp.exp(position * rate)
    shrinking = jnp.exp(-position * rate)
    weight = jnp.exp(lookup_projected_vectors)
    acc_a = shrinking * exact_rows(same_span, growing * weight * payload_vectors)
    acc_b = shrinking * exact_rows(same_span, growing * weight)
    unbroken = (segment == 0.0).astype(jnp.float32)[:, None]
    totals = unbroken * jnp.exp(-(position + 1.0) * rate)
    return (totals, acc_a, acc_b)


def recurrence_result_rows(
    lookup_projected_vectors,
    payload_vectors,
    present_element_extra,
    retain_mask,
    overview_state,
    state_first,
    state_second,
):
    totals, acc_a, acc_b = overview_state
    post_a = acc_a + totals * state_first[None, :]
    post_b = acc_b + totals * state_second[None, :]
    prior_primary_carry = shift_down(post_a, state_first) * retain_mask[:, None]
    prior_auxiliary_carry = shift_down(post_b, state_second) * retain_mask[:, None]
    present_extra_term = jnp.exp(present_element_extra[None, :] + lookup_projected_vectors)
    interpolated_vectors = (prior_primary_carry + present_extra_term * payload_vectors) / (
        prior_auxiliary_carry + present_extra_term
    )
    return (interpolated_vectors, post_a[-1], post_b[-1])


def recurrence_nearby(
    lookup_projected_vectors,
    payload_vectors,
    fading_rate_logarithm,
    present_element_extra,
    state_first,
    state_second,
    retain_mask,
):
    overview_state = recurrence_summary(
        lookup_projected_vectors, payload_vectors, fading_rate_logarithm, retain_mask
    )
    return (
        recurrence_result_rows(
            lookup_projected_vectors,
            payload_vectors,
            present_element_extra,
            retain_mask,
            overview_state,
            state_first,
            state_second,
        ),
        overview_state[0][-1],
    )


def identity_of(sample):
    return (jnp.ones_like(sample), jnp.zeros_like(sample), jnp.zeros_like(sample))


def carry_in(totals_last, last_a, last_b):
    found = entering(
        (totals_last, last_a, last_b), "dp", combine_pairs, identity_of(totals_last), False
    )
    return (found[1], found[2])


def carry_out(totals_last, grad_a, grad_b):
    found = entering(
        (totals_last, grad_a, grad_b), "dp", combine_pairs, identity_of(totals_last), True
    )
    return (found[1], found[2])


def prior_row(normed):
    return passed_along(normed[-1:], "dp", 1)


def later_row(grad_row):
    return passed_along(grad_row, "dp", -1)


def forward_layer(current, retain_mask, weights):
    (
        attention_standardize_scale,
        attention_standardize_offset,
        lagged_lookup_mix,
        lagged_payload_mix,
        lagged_sigmoid_mix,
        fading_rate_logarithm,
        present_element_extra,
        lookup_projection,
        payload_projection,
        sigmoid_projection,
        attention_emit_projection,
        feedforward_standardize_scale,
        feedforward_standardize_offset,
        lagged_feedforward_lookup_mix,
        lagged_feedforward_sigmoid_mix,
        feedforward_lookup_projection,
        feedforward_payload_projection,
        feedforward_sigmoid_projection,
    ) = weights
    normed = layer_norm(current, attention_standardize_scale, attention_standardize_offset)
    row_one = prior_row(normed)
    earlier = shift_down(normed, row_one) * retain_mask[:, None]
    lookup_projected_vectors = matmul_rows(
        blend_rows(normed, earlier, lagged_lookup_mix).astype(jnp.bfloat16), lookup_projection
    )
    payload_vectors = matmul_rows(
        blend_rows(normed, earlier, lagged_payload_mix).astype(jnp.bfloat16), payload_projection
    )
    gate_pre = matmul_rows(
        blend_rows(normed, earlier, lagged_sigmoid_mix).astype(jnp.bfloat16), sigmoid_projection
    )
    overview_state = recurrence_summary(
        lookup_projected_vectors, payload_vectors, fading_rate_logarithm, retain_mask
    )
    entry_state_first, entry_state_second = carry_in(
        overview_state[0][-1], overview_state[1][-1], overview_state[2][-1]
    )
    interpolated_vectors = recurrence_result_rows(
        lookup_projected_vectors,
        payload_vectors,
        present_element_extra,
        retain_mask,
        overview_state,
        entry_state_first,
        entry_state_second,
    )[0]
    gated_rows = jax.nn.sigmoid(gate_pre) * interpolated_vectors
    middle = current + matmul_rows(gated_rows.astype(jnp.bfloat16), attention_emit_projection)
    second = layer_norm(middle, feedforward_standardize_scale, feedforward_standardize_offset)
    row_two = prior_row(second)
    earlier_two = shift_down(second, row_two) * retain_mask[:, None]
    hidden_pre = matmul_rows(
        blend_rows(second, earlier_two, lagged_feedforward_lookup_mix).astype(jnp.bfloat16),
        feedforward_lookup_projection,
    )
    active = jnp.maximum(hidden_pre, 0.0)
    projected = matmul_rows((active * active).astype(jnp.bfloat16), feedforward_payload_projection)
    sieve_rows = jax.nn.sigmoid(
        matmul_rows(
            blend_rows(second, earlier_two, lagged_feedforward_sigmoid_mix).astype(jnp.bfloat16),
            feedforward_sigmoid_projection,
        )
    )
    result = middle + sieve_rows * projected
    return (
        result,
        jnp.concatenate(
            [row_one, entry_state_first[None], entry_state_second[None], row_two], axis=0
        ),
    )


def backward_layer(current, retain_mask, weights, stored, incoming):
    (
        attention_standardize_scale,
        attention_standardize_offset,
        lagged_lookup_mix,
        lagged_payload_mix,
        lagged_sigmoid_mix,
        fading_rate_logarithm,
        present_element_extra,
        lookup_projection,
        payload_projection,
        sigmoid_projection,
        attention_emit_projection,
        feedforward_standardize_scale,
        feedforward_standardize_offset,
        lagged_feedforward_lookup_mix,
        lagged_feedforward_sigmoid_mix,
        feedforward_lookup_projection,
        feedforward_payload_projection,
        feedforward_sigmoid_projection,
    ) = weights
    row_one = stored[0:1]
    entry_state_first = stored[1]
    entry_state_second = stored[2]
    row_two = stored[3:4]
    normed, norm_back = jax.vjp(
        layer_norm, current, attention_standardize_scale, attention_standardize_offset
    )
    earlier = shift_down(normed, row_one) * retain_mask[:, None]
    low_keys = blend_rows(normed, earlier, lagged_lookup_mix).astype(jnp.bfloat16)
    low_values = blend_rows(normed, earlier, lagged_payload_mix).astype(jnp.bfloat16)
    low_gates = blend_rows(normed, earlier, lagged_sigmoid_mix).astype(jnp.bfloat16)
    lookup_projected_vectors = matmul_rows(low_keys, lookup_projection)
    payload_vectors = matmul_rows(low_values, payload_projection)
    gate_pre = matmul_rows(low_gates, sigmoid_projection)
    outcome, recurrence_back, totals_last = jax.vjp(
        partial(recurrence_nearby, retain_mask=retain_mask),
        lookup_projected_vectors,
        payload_vectors,
        fading_rate_logarithm,
        present_element_extra,
        entry_state_first,
        entry_state_second,
        has_aux=True,
    )
    interpolated_vectors = outcome[0]
    gate_rows = jax.nn.sigmoid(gate_pre)
    gated_rows = gate_rows * interpolated_vectors
    low_gated = gated_rows.astype(jnp.bfloat16)
    middle = current + matmul_rows(low_gated, attention_emit_projection)
    second, second_back = jax.vjp(
        layer_norm, middle, feedforward_standardize_scale, feedforward_standardize_offset
    )
    earlier_two = shift_down(second, row_two) * retain_mask[:, None]
    low_hidden = blend_rows(second, earlier_two, lagged_feedforward_lookup_mix).astype(jnp.bfloat16)
    low_sieve = blend_rows(second, earlier_two, lagged_feedforward_sigmoid_mix).astype(jnp.bfloat16)
    hidden_pre = matmul_rows(low_hidden, feedforward_lookup_projection)
    active = jnp.maximum(hidden_pre, 0.0)
    low_squared = (active * active).astype(jnp.bfloat16)
    projected = matmul_rows(low_squared, feedforward_payload_projection)
    sieve_rows = jax.nn.sigmoid(matmul_rows(low_sieve, feedforward_sigmoid_projection))
    d_projected = (incoming * sieve_rows).astype(jnp.bfloat16)
    d_sieve_pre = (incoming * projected * sieve_rows * (1.0 - sieve_rows)).astype(jnp.bfloat16)
    project_grad = outer_sum(low_squared, d_projected)
    filter_grad = outer_sum(low_sieve, d_sieve_pre)
    d_hidden_pre = (back_dot(d_projected, feedforward_payload_projection) * 2.0 * active).astype(
        jnp.bfloat16
    )
    hidden_grad = outer_sum(low_hidden, d_hidden_pre)
    second_one, earlier_one, shift_hidden_grad = blend_back(
        back_dot(d_hidden_pre, feedforward_lookup_projection),
        second,
        earlier_two,
        lagged_feedforward_lookup_mix,
    )
    second_two, earlier_more, shift_filter_grad = blend_back(
        back_dot(d_sieve_pre, feedforward_sigmoid_projection),
        second,
        earlier_two,
        lagged_feedforward_sigmoid_mix,
    )
    d_earlier_two = (earlier_one + earlier_more) * retain_mask[:, None]
    received_two = later_row(d_earlier_two[:1])
    d_second = second_one + second_two + shift_up(d_earlier_two, received_two)
    d_middle_norm, second_gain_grad, second_bias_grad = second_back(d_second)
    d_middle = incoming + d_middle_norm
    d_attended = d_middle.astype(jnp.bfloat16)
    output_grad = outer_sum(low_gated, d_attended)
    d_gated = back_dot(d_attended, attention_emit_projection)
    d_blended = d_gated * gate_rows
    d_gate_pre = (d_gated * interpolated_vectors * gate_rows * (1.0 - gate_rows)).astype(
        jnp.bfloat16
    )
    blank_state = jnp.zeros_like(entry_state_first)
    adjacent_fragments = recurrence_back((d_blended, blank_state, blank_state))
    leave_a, leave_b = carry_out(totals_last, adjacent_fragments[4], adjacent_fragments[5])
    distant_fragments = recurrence_back((jnp.zeros_like(d_blended), leave_a, leave_b))
    d_keys = (adjacent_fragments[0] + distant_fragments[0]).astype(jnp.bfloat16)
    d_values = (adjacent_fragments[1] + distant_fragments[1]).astype(jnp.bfloat16)
    decay_grad = adjacent_fragments[2] + distant_fragments[2]
    present_extra_cotangent = adjacent_fragments[3] + distant_fragments[3]
    key_grad = outer_sum(low_keys, d_keys)
    value_grad = outer_sum(low_values, d_values)
    gate_grad = outer_sum(low_gates, d_gate_pre)
    normed_one, earlier_one, shift_key_grad = blend_back(
        back_dot(d_keys, lookup_projection), normed, earlier, lagged_lookup_mix
    )
    normed_two, earlier_two_part, shift_value_grad = blend_back(
        back_dot(d_values, payload_projection), normed, earlier, lagged_payload_mix
    )
    normed_three, earlier_three, shift_gate_grad = blend_back(
        back_dot(d_gate_pre, sigmoid_projection), normed, earlier, lagged_sigmoid_mix
    )
    d_earlier = (earlier_one + earlier_two_part + earlier_three) * retain_mask[:, None]
    received_one = later_row(d_earlier[:1])
    d_normed = normed_one + normed_two + normed_three + shift_up(d_earlier, received_one)
    d_current_norm, norm_gain_grad, norm_bias_grad = norm_back(d_normed)
    back_input = d_middle + d_current_norm
    gradients = (
        norm_gain_grad,
        norm_bias_grad,
        shift_key_grad,
        shift_value_grad,
        shift_gate_grad,
        decay_grad,
        present_extra_cotangent,
        key_grad,
        value_grad,
        gate_grad,
        output_grad,
        second_gain_grad,
        second_bias_grad,
        shift_hidden_grad,
        shift_filter_grad,
        hidden_grad,
        project_grad,
        filter_grad,
    )
    return (back_input, gradients)


def per_device(
    bottom_tier_source,
    topmost_emitted_cotangent,
    packed_span_sizes,
    attention_standardize_scale,
    attention_standardize_offset,
    lagged_lookup_mix,
    lagged_payload_mix,
    lagged_sigmoid_mix,
    fading_rate_logarithm,
    present_element_extra,
    lookup_projection,
    payload_projection,
    sigmoid_projection,
    attention_emit_projection,
    feedforward_standardize_scale,
    feedforward_standardize_offset,
    lagged_feedforward_lookup_mix,
    lagged_feedforward_sigmoid_mix,
    feedforward_lookup_projection,
    feedforward_payload_projection,
    feedforward_sigmoid_projection,
):
    weights = tuple(
        (
            peer_device_rank[0]
            for peer_device_rank in (
                attention_standardize_scale,
                attention_standardize_offset,
                lagged_lookup_mix,
                lagged_payload_mix,
                lagged_sigmoid_mix,
                fading_rate_logarithm,
                present_element_extra,
                lookup_projection,
                payload_projection,
                sigmoid_projection,
                attention_emit_projection,
                feedforward_standardize_scale,
                feedforward_standardize_offset,
                lagged_feedforward_lookup_mix,
                lagged_feedforward_sigmoid_mix,
                feedforward_lookup_projection,
                feedforward_payload_projection,
                feedforward_sigmoid_projection,
            )
        )
    )
    sections = lax.axis_size("section")
    section_index = lax.axis_index("section")
    dp_index = lax.axis_index("dp")
    batches = bottom_tier_source.shape[0]
    row_count = bottom_tier_source.shape[1]
    width = bottom_tier_source.shape[2]
    step_count = batches + sections - 1
    arrived = jnp.zeros((row_count, width), jnp.bfloat16)
    kept_inputs = jnp.zeros((batches, row_count, width), jnp.bfloat16)
    kept_rows = jnp.zeros((batches, 4, width), jnp.float32)
    outputs = jnp.zeros((batches, row_count, width), jnp.bfloat16)
    for moment in range(step_count):
        batch_index = moment - section_index
        is_valid = (batch_index >= 0) & (batch_index < batches)
        chosen = jnp.clip(batch_index, 0, batches - 1)
        retain_mask = keep_rows(packed_span_sizes[chosen], dp_index * row_count, row_count)
        supplied = lax.dynamic_index_in_dim(bottom_tier_source, chosen, 0, keepdims=False)
        current = jnp.where(section_index == 0, supplied, arrived)
        result, stored = forward_layer(current.astype(jnp.float32), retain_mask, weights)
        low_result = result.astype(jnp.bfloat16)
        kept_inputs = jnp.where(
            is_valid, lax.dynamic_update_index_in_dim(kept_inputs, current, chosen, 0), kept_inputs
        )
        kept_rows = jnp.where(
            is_valid, lax.dynamic_update_index_in_dim(kept_rows, stored, chosen, 0), kept_rows
        )
        outputs = jnp.where(
            is_valid, lax.dynamic_update_index_in_dim(outputs, low_result, chosen, 0), outputs
        )
        arrived = passed_along(low_result, "section", 1)
    summed = tuple((jnp.zeros(peer_device_rank.shape, jnp.float32) for peer_device_rank in weights))
    descended = jnp.zeros((row_count, width), jnp.bfloat16)
    input_grads = jnp.zeros((batches, row_count, width), jnp.bfloat16)
    for moment in range(step_count):
        batch_index = moment - (sections - 1 - section_index)
        is_valid = (batch_index >= 0) & (batch_index < batches)
        chosen = jnp.clip(batch_index, 0, batches - 1)
        retain_mask = keep_rows(packed_span_sizes[chosen], dp_index * row_count, row_count)
        supplied = lax.dynamic_index_in_dim(topmost_emitted_cotangent, chosen, 0, keepdims=False)
        incoming = jnp.where(section_index == sections - 1, supplied, descended).astype(jnp.float32)
        current = lax.dynamic_index_in_dim(kept_inputs, chosen, 0, keepdims=False).astype(
            jnp.float32
        )
        stored = lax.dynamic_index_in_dim(kept_rows, chosen, 0, keepdims=False)
        back_input, gradients = backward_layer(current, retain_mask, weights, stored, incoming)
        low_input = back_input.astype(jnp.bfloat16)
        input_grads = jnp.where(
            is_valid,
            lax.dynamic_update_index_in_dim(input_grads, low_input, chosen, 0),
            input_grads,
        )
        masked = tuple((jnp.where(is_valid, part_grad, 0.0) for part_grad in gradients))
        summed = tuple((running + portion for running, portion in zip(summed, masked)))
        descended = passed_along(low_input, "section", -1)
    summed = lax.psum_scatter(summed, "dp", scatter_dimension=0, tiled=True)
    return (outputs[None], input_grads[None]) + tuple((portion[None] for portion in summed))


def solution(mesh):
    return jax.shard_map(
        per_device,
        mesh=mesh,
        in_specs=(
            P(None, "dp", None),
            P(None, "dp", None),
            P(),
            P("section", None),
            P("section", None),
            P("section", None),
            P("section", None),
            P("section", None),
            P("section", None),
            P("section", None),
            P("section", None, None),
            P("section", None, None),
            P("section", None, None),
            P("section", None, None),
            P("section", None),
            P("section", None),
            P("section", None),
            P("section", None),
            P("section", None, None),
            P("section", None, None),
            P("section", None, None),
        ),
        out_specs=(
            P("section", None, "dp", None),
            P("section", None, "dp", None),
            P("section", "dp"),
            P("section", "dp"),
            P("section", "dp"),
            P("section", "dp"),
            P("section", "dp"),
            P("section", "dp"),
            P("section", "dp"),
            P("section", "dp", None),
            P("section", "dp", None),
            P("section", "dp", None),
            P("section", "dp", None),
            P("section", "dp"),
            P("section", "dp"),
            P("section", "dp"),
            P("section", "dp"),
            P("section", "dp", None),
            P("section", "dp", None),
            P("section", "dp", None),
        ),
        check_vma=False,
    )
```

profile of v0, /device:TPU:0, one launch (start us, length us, event | category | flops | bytes accessed | tf_op | source)
XLA Modules:
  0.0 1632.6 jit_solution(9925031727877144393)
XLA Ops:
  30.7 15.2 all-gather.10
  66.4 14.0 all-gather.12
  109.2 14.0 all-gather.13
  134.5 15.4 all-gather.14
  149.9 14.2 all-gather.15
  222.2 15.1 all-gather.17
  237.4 14.2 all-gather.18
  298.5 14.1 all-gather.22
  323.6 15.1 all-gather.20
  338.7 14.2 all-gather.21
  492.9 14.8 all-gather.25
  507.7 14.0 all-gather
  521.7 14.0 all-gather.1
  652.9 14.8 all-gather.26
  683.0 14.4 all-gather.3
  773.4 15.8 all-gather.27
  889.1 15.2 all-gather.28
  1008.5 15.8 all-gather.29
  1025.3 14.4 all-gather.8
  1040.3 14.6 all-gather.9
  1190.1 15.0 select_add_fusion
  1237.9 32.6 %all-reduce.21 = (f32[1024]{0:T(1024)S(1)}, f32[1024]{0:T(1024)S(1)}, f32[1024]{0:T(1024)S(1)}, f32[1024]{0:T(1024)S(1)}, f32[1024]{0:T(1024)S(1)}, /*index=5*/f...) all-reduce(f32[1024]{0:T(1024)S(1)} %select_add_fusion.16, ...), channel_id=12, replica_groups=mesh['section'=4,'dp'=8] {'dp'}, use_global_device_ids=true, to_apply=%region_125.126.clone | all-reduce | flops 11264 | bytes 90112
  1286.8 169.2 %reduce-scatter.16.cloned.1.call-done = f32[128,4096]{1,0:T(8,128)} async-done(((f32[1024,4096]{1,0:T(8,128)}), f32[128,4096]{1,0:T(8,128)}) %reduce-scatter.16.cloned.1.call-update) | async-done | bytes 2097168 | tf_op jit(solution)/shard_map/reduce_scatter | solution.py:519
  1456.0 169.6 %reduce-scatter.18.cloned.1.call-done = f32[512,1024]{1,0:T(8,128)} async-done(((f32[4096,1024]{1,0:T(8,128)}), f32[512,1024]{1,0:T(8,128)}) %reduce-scatter.18.cloned.1.call-update) | async-done | bytes 2097168 | tf_op jit(solution)/shard_map/reduce_scatter | solution.py:519
  (2076 shorter events, 962.9 us)
Async XLA Ops:
  7.2 1272.0 %reduce-scatter.20.cloned.1.call-start = ((), (), s32[]{:S(2)}) async-start(), calls=%async_computation.13 | async-start | bytes 4718592 | tf_op jit(solution)/shard_map/reduce_scatter | solution.py:519
  10.9 35.0 %collective-permute-start = (f32[1,1024]{1,0:T(1,128)S(1)}, f32[1,1024]{1,0:T(1,128)S(1)}, u32[]{:S(2)}, u32[]{:S(2)}) collective-permute-start(f32[1,1024]{1,0:T(1,128)S(1)} %slice.260), channel_id=1, source_target_pairs={{0,1},{1,2},{2,3},{3,4},{4,5},{5,6},{6,7},{8,9},{9,10},{10,11},{11... | collective-permute-start | bytes 12296 | tf_op jit(solution)/shard_map/ppermute | solution.py:30
  88.6 4.5 collective-permute-start.1
  105.6 18.6 %collective-permute-start.2 = (bf16[128,1024]{1,0:T(8,128)(2,1)}, bf16[128,1024]{1,0:T(8,128)(2,1)S(1)}, u32[]{:S(2)}, u32[]{:S(2)}) collective-permute-start(bf16[128,1024]{1,0:T(8,128)(2,1)} %get-tuple-element.2343), channel_id=1, source_target_pairs={{0,8},{8,16},{16,24},{1,9},{9,17},{17,25},{2,10},{10,18},{18,26},{... | collective-permute-start | bytes 786440 | tf_op jit(solution)/shard_map/ppermute | solution.py:30
  175.3 5.1 collective-permute-start.4
  193.1 18.9 %collective-permute-start.5 = (bf16[128,1024]{1,0:T(8,128)(2,1)}, bf16[128,1024]{1,0:T(8,128)(2,1)S(1)}, u32[]{:S(2)}, u32[]{:S(2)}) collective-permute-start(bf16[128,1024]{1,0:T(8,128)(2,1)} %get-tuple-element.2347), channel_id=1, source_target_pairs={{0,8},{8,16},{16,24},{1,9},{9,17},{17,25},{2,10},{10,18},{18,26},{... | collective-permute-start | bytes 786440 | tf_op jit(solution)/shard_map/ppermute | solution.py:30
  262.8 4.8 collective-permute-start.7
  280.3 32.9 %collective-permute-start.8 = (bf16[128,1024]{1,0:T(8,128)(2,1)}, bf16[128,1024]{1,0:T(8,128)(2,1)S(1)}, u32[]{:S(2)}, u32[]{:S(2)}) collective-permute-start(bf16[128,1024]{1,0:T(8,128)(2,1)} %get-tuple-element.2351), channel_id=1, source_target_pairs={{0,8},{8,16},{16,24},{1,9},{9,17},{17,25},{2,10},{10,18},{18,26},{... | collective-permute-start | bytes 786440 | tf_op jit(solution)/shard_map/ppermute | solution.py:30
  364.1 4.9 collective-permute-start.10
  381.6 8.2 collective-permute-start.11
  392.2 5.7 collective-permute-start.12
  547.3 4.2 collective-permute-start.15
  603.3 17.3 %collective-permute-start.16 = (bf16[128,1024]{1,0:T(8,128)(2,1)S(1)}, bf16[128,1024]{1,0:T(8,128)(2,1)S(1)}, u32[]{:S(2)}, u32[]{:S(2)}) collective-permute-start(bf16[128,1024]{1,0:T(8,128)(2,1)S(1)} %get-tuple-element.2166), channel_id=1, source_target_pairs={{8,0},{16,8},{24,16},{9,1},{17,9},{25,17},{10,2},{18,10},{26,18},{... | collective-permute-start | bytes 786440 | tf_op jit(solution)/shard_map/ppermute | solution.py:30
  731.5 11.5 collective-permute-start.19
  848.2 11.8 collective-permute-start.22
  964.0 11.5 collective-permute-start.25
  987.9 7.1 collective-permute-start.26
  995.0 284.2 %reduce-scatter.8.cloned.1.call-start = ((), (), s32[]{:S(2)}) async-start(), calls=%async_computation.7 | async-start | bytes 4718592 | tf_op jit(solution)/shard_map/reduce_scatter | solution.py:519
  1080.3 198.9 %reduce-scatter.10.cloned.1.call-start = ((), (), s32[]{:S(2)}) async-start(), calls=%async_computation.8 | async-start | bytes 4718592 | tf_op jit(solution)/shard_map/reduce_scatter | solution.py:519
  1088.7 190.6 %reduce-scatter.12.cloned.1.call-start = ((), (), s32[]{:S(2)}) async-start(), calls=%async_computation.9 | async-start | bytes 4718592 | tf_op jit(solution)/shard_map/reduce_scatter | solution.py:519
  1097.1 189.7 %reduce-scatter.14.cloned.1.call-start = ((), (), s32[]{:S(2)}) async-start(), calls=%async_computation.10 | async-start | bytes 4718592 | tf_op jit(solution)/shard_map/reduce_scatter | solution.py:519
  1105.7 350.3 %reduce-scatter.16.cloned.1.call-start = ((), (), s32[]{:S(2)}) async-start(), calls=%async_computation.11 | async-start | bytes 18874368 | tf_op jit(solution)/shard_map/reduce_scatter | solution.py:519
  1154.6 470.9 %reduce-scatter.18.cloned.1.call-start = ((), (), s32[]{:S(2)}) async-start(), calls=%async_computation.12 | async-start | bytes 18874368 | tf_op jit(solution)/shard_map/reduce_scatter | solution.py:519
  1228.2 5.9 collective-permute-start.27
  (602 other events, 6219.5 us)
Sparse Core Ops, SparseCore 0:
  995.1 54.6 reduce-scatter.19
  1080.4 52.2 reduce-scatter.7
  1135.6 48.1 reduce-scatter.9
  1186.5 48.1 reduce-scatter.11
  1237.4 49.3 reduce-scatter.13
  1289.6 166.3 reduce-scatter.15
  1458.9 166.6 reduce-scatter.17
where the time goes:
time: 1650 us; the launch traced here: 1630 us
  matrix products  551 us (33%)
  blocking collectives  466 us (28%)
  waiting for transfers between devices  377 us (23%)
  local copies, waits for them, and re-layouts  90.8 us (6%)
  other arithmetic  62.7 us (4%)
  starting transfers between devices  58.4 us (4%)
  between operations  23.5 us (1%)
    all_gather x30, blocking collectives, entering(): everything = jax.tree.map(lambda part: lax.all_gather(part, axis), x)  433 us
    reduce_scatter x7, waiting for transfers between devices, per_device(): summed = lax.psum_scatter(summed, 'dp', scatter_dimension=0, tiled=True)  346 us
    dot_general x120, matrix products, exact_rows(): jnp.dot(mixing, rows, preferred_element_type=jnp.float32, precision=lax.P...  192 us
    dot_general x35, matrix products, outer_sum(): lax.dot_general(left_rows, right_rows, (((0,), (0,)), ((), ())), preferre...  147 us
    dot_general x60, matrix products, matmul_rows(): return jnp.dot(left_rows, weight, preferred_element_type=jnp.float32)  138 us
    dot_general x35, matrix products, back_dot(): lax.dot_general(gradient, weight, (((1,), (1,)), ((), ())), preferred_ele...  73.8 us
    ppermute x28, starting transfers between devices, passed_along(): return lax.ppermute(x, axis, pairs)  57.3 us
    unnamed x1225, local copies, waits for them, and re-layouts  44.5 us
  transfers between devices with their start and end apart: 35, of which 9 were waited for; matrix products, arithmetic and copies ran while one was open for 17% of the time, Pallas kernels for 0%

commit v1 on v0

v1 whole, which is shorter than its diff:
```python
from functools import partial

import jax
import jax.numpy as jnp
from jax import lax
from jax.experimental import pallas as pl
from jax.experimental.pallas import tpu as pltpu
from jax.sharding import PartitionSpec as P

EPS = 1e-05
MESH = pl.DeviceIdType.MESH
RB = 32
VECTORS = 16
F32 = jnp.float32
BF16 = jnp.bfloat16


def dot_nn(left, right):
    return jnp.dot(left, right, preferred_element_type=F32)


def dot_nt(left, right):
    return lax.dot_general(left, right, (((1,), (1,)), ((), ())), preferred_element_type=F32)


def dot_tn(left, right):
    return lax.dot_general(left, right, (((0,), (0,)), ((), ())), preferred_element_type=F32)


def sigmoid(v):
    return 1.0 / (1.0 + jnp.exp(-v))


def normalise(source):
    centred = source - jnp.mean(source, axis=-1, keepdims=True)
    spread = lax.rsqrt(jnp.mean(centred * centred, axis=-1, keepdims=True) + EPS)
    return centred * spread, spread


def moved_down(rows, first):
    place = lax.broadcasted_iota(jnp.int32, rows.shape, 0)
    return jnp.where(place == 0, first, pltpu.roll(rows, 1, 0))


def moved_up(rows, last):
    count = rows.shape[0]
    place = lax.broadcasted_iota(jnp.int32, rows.shape, 0)
    return jnp.where(place == count - 1, last, pltpu.roll(rows, count - 1, 0))


def fold(rows):
    total = rows[0:8]
    for at in range(8, rows.shape[0], 8):
        total = total + rows[at : at + 8]
    return total


def relay_kernel(sections, peers, split_vectors, *refs):
    (
        spans, x_in, top_in,
        gain1, bias1, mix_k, mix_v, mix_g, log_rate, extra, gain2, bias2, mix_h, mix_f,
        wk_in, wv_in, wg_in, wo_in, wh_in, wp_in, wf_in,
        out, back, vec_out, lk, lv, lg, lgt, lh, lf, sq, dk, dv, dg, datt, dproj, dsv, dh,
        wk, wv, wg, wo, wh, wp, wf,
        xs, hx, dys, kk, vv, sg, sa, sb, mid, hmid, proj, sv, act, halo1, halo2,
        e0, e1, low_mask, up_mask, split, acc, t1, t2, t3,
        states, back_states, de2, de1, sum_row, sum_back, send_de2, send_de1, vg, vgs, vgr,
        w_sem, x_sem, top_sem, s_h0, s_x, s_hx, s_st, s_mid, s_dy, s_de2, s_bst, s_de1, s_vg,
        r_x, r_hx, r_st, r_mid, r_dy, r_de2, r_bst, r_de1, r_vg,
    ) = refs
    me_s = lax.axis_index("section")
    me = lax.axis_index("dp")
    batches, row_count, width = x_in.shape
    hidden = wh.shape[1]
    chunks = row_count // RB
    base = me * row_count

    def at(section, index):
        return (section, index)

    barrier = pltpu.get_barrier_semaphore()

    def greet(section, index):
        pl.semaphore_signal(barrier, inc=1, device_id=at(section, index), device_id_type=MESH)

    def greet_peer(k, carry):
        @pl.when(k != me)
        def _():
            greet(me_s, k)

        return carry

    lax.fori_loop(0, peers, greet_peer, 0)
    has_next = me_s + 1 < sections
    has_prior = me_s > 0
    has_right = me + 1 < peers
    has_left = me > 0

    @pl.when(has_next)
    def _():
        greet(me_s + 1, me)

    @pl.when(has_prior)
    def _():
        greet(me_s - 1, me)

    @pl.when(has_next & has_right)
    def _():
        greet(me_s + 1, me + 1)

    @pl.when(has_prior & has_left)
    def _():
        greet(me_s - 1, me - 1)

    weight_copies = [
        pltpu.make_async_copy(source, target, w_sem.at[index])
        for index, (source, target) in enumerate(
            ((wk_in, wk), (wv_in, wv), (wg_in, wg), (wo_in, wo), (wf_in, wf), (wh_in, wh), (wp_in, wp))
        )
    ]

    @pl.when(me_s == 0)
    def _():
        pltpu.make_async_copy(x_in, xs, x_sem).start()

    for copy in weight_copies:
        copy.start()

    @pl.when(me_s == sections - 1)
    def _():
        pltpu.make_async_copy(top_in, dys, top_sem).start()

    rate = jnp.exp(log_rate[...])
    decay_block = jnp.exp(-rate * row_count)
    grow_block = jnp.exp(rate * row_count)

    def starts_of(m):
        found = []
        total = jnp.int32(0)
        for j in range(spans.shape[1]):
            found.append(total)
            total = total + spans[m, j]
        return found

    def segment(position, starts):
        total = jnp.where(position >= starts[0], 1, 0)
        for start in starts[1:]:
            total = total + jnp.where(position >= start, 1, 0)
        return total

    def column(i):
        return base + i * RB + lax.broadcasted_iota(jnp.int32, (RB, 1), 0)

    def keep_of(position, starts):
        return jnp.where(segment(position, starts) == segment(position - 1, starts), 1.0, 0.0)

    def fill_powers(i, carry):
        place = (i * RB + lax.broadcasted_iota(jnp.int32, (RB, width), 0)).astype(F32)
        e0[pl.ds(pl.multiple_of(i * RB, RB), RB), :] = jnp.exp(-place * rate)
        e1[pl.ds(pl.multiple_of(i * RB, RB), RB), :] = jnp.exp((place - (row_count - 1.0)) * rate)
        return carry

    lax.fori_loop(0, chunks, fill_powers, 0)
    for m in range(batches):
        starts = starts_of(m)
        row_at = lax.broadcasted_iota(jnp.int32, (row_count, row_count), 0)
        column_at = lax.broadcasted_iota(jnp.int32, (row_count, row_count), 1)
        same = segment(base + row_at, starts) == segment(base + column_at, starts)
        lower = jnp.where(same & (column_at < row_at), 1.0, 0.0).astype(BF16)
        upper = jnp.where(same & (column_at > row_at), 1.0, 0.0).astype(BF16)
        low_mask[m, :, 0:row_count] = lower
        low_mask[m, :, row_count:] = lower
        up_mask[m, :, 0:row_count] = upper
        up_mask[m, :, row_count:] = upper
    vg[...] = jnp.zeros_like(vg)

    @pl.when(me == 0)
    def _():
        hx[...] = jnp.zeros_like(hx)
        hmid[...] = jnp.zeros_like(hmid)

    @pl.when(me == peers - 1)
    def _():
        de1[...] = jnp.zeros_like(de1)
        de2[...] = jnp.zeros_like(de2)

    greeted = (
        peers - 1
        + jnp.where(has_next, 1, 0)
        + jnp.where(has_prior, 1, 0)
        + jnp.where(has_next & has_right, 1, 0)
        + jnp.where(has_prior & has_left, 1, 0)
    )
    pl.semaphore_wait(barrier, greeted)

    def remote(source, target, send, receive, section, index):
        return pltpu.make_async_remote_copy(
            src_ref=source, dst_ref=target, send_sem=send, recv_sem=receive,
            device_id=at(section, index), device_id_type=MESH,
        )

    right = jnp.minimum(me + 1, peers - 1)
    left = jnp.maximum(me - 1, 0)
    above = jnp.minimum(me_s + 1, sections - 1)
    below = jnp.maximum(me_s - 1, 0)
    tail = pl.ds(row_count - 16, 16)
    tail8 = pl.ds(row_count - 8, 8)

    def start_halo(m):
        return remote(x_in.at[m, tail], hx.at[m], s_h0.at[m], r_hx.at[m], me_s, right)

    def result_copy(m):
        return remote(out.at[m], xs.at[m], s_x.at[m], r_x.at[m], above, me)

    def result_halo(m):
        return remote(out.at[m, tail], hx.at[m], s_hx.at[m], r_hx.at[m], above, right)

    def middle_halo(m):
        return remote(mid.at[m, tail8], hmid.at[m], s_mid.at[m], r_mid.at[m], me_s, right)

    def state_copy(m, k, slot):
        return remote(sum_row.at[m], states.at[m, slot], s_st.at[m, k], r_st.at[m, slot], me_s, k)

    def back_copy(m):
        return remote(back.at[m], dys.at[m], s_dy.at[m], r_dy.at[m], below, me)

    def second_copy(m):
        return remote(send_de2.at[m], de2.at[m], s_de2.at[m], r_de2.at[m], me_s, left)

    def first_copy(m):
        return remote(send_de1.at[m], de1.at[m], s_de1.at[m], r_de1.at[m], me_s, left)

    def back_state_copy(m, k, slot):
        return remote(
            sum_back.at[m], back_states.at[m, slot], s_bst.at[m, k], r_bst.at[m, slot], me_s, k
        )

    @pl.when((me_s == 0) & has_right)
    def _():
        for m in range(batches):
            start_halo(m).start()

    @pl.when(me_s == 0)
    def _():
        pltpu.make_async_copy(x_in, xs, x_sem).wait()

    def span_of(i):
        return pl.ds(pl.multiple_of(i * RB, RB), RB)

    def forward(m, carry):
        starts = starts_of(m)

        @pl.when(has_prior)
        def _():
            result_copy(m).wait_recv()

        @pl.when(has_left)
        def _():
            start_halo(m).wait_recv()

        halo_rows, _ = normalise(hx[m].astype(F32))
        halo_rows = halo_rows * gain1[...] + bias1[...]
        halo1[m] = halo_rows[8:16]

        def mix_in(i, last):
            rows = span_of(i)
            normed, _ = normalise(xs[m, rows, :].astype(F32))
            normed = normed * gain1[...] + bias1[...]
            earlier = moved_down(normed, last) * keep_of(column(i), starts)
            gap = normed - earlier
            lk[m, rows, :] = (earlier + gap * mix_k[...]).astype(BF16)
            lv[m, rows, :] = (earlier + gap * mix_v[...]).astype(BF16)
            lg[m, rows, :] = (earlier + gap * mix_g[...]).astype(BF16)
            return normed[RB - 1 : RB]

        lax.fori_loop(0, chunks, mix_in, halo_rows[15:16])

        @pl.when(m == 0)
        def _():
            for copy in weight_copies[0:2]:
                copy.wait()

        kk[m] = dot_nn(lk[m], wk[...])
        vv[m] = dot_nn(lv[m], wv[...])
        end_segment = segment(base + row_count - 1, starts)

        def spread_in(i, totals):
            rows = span_of(i)
            weight = jnp.exp(kk[m, rows, :]) * e1[rows, :]
            weighted = weight * vv[m, rows, :]
            high_a = weighted.astype(BF16)
            high_b = weight.astype(BF16)
            split[rows, 0:width] = high_a
            split[rows, width:] = high_b
            low = pl.ds(pl.multiple_of(row_count + i * RB, RB), RB)
            split[low, 0:width] = (weighted - high_a.astype(F32)).astype(BF16)
            split[low, width:] = (weight - high_b.astype(F32)).astype(BF16)
            chosen = segment(column(i), starts) == end_segment
            return (
                totals[0] + fold(jnp.where(chosen, weighted, 0.0)),
                totals[1] + fold(jnp.where(chosen, weight, 0.0)),
            )

        nothing = jnp.zeros((8, width), F32)
        total_a, total_b = lax.fori_loop(0, chunks, spread_in, (nothing, nothing))
        sum_row[m, 0:1] = jnp.sum(total_a, axis=0, keepdims=True)
        sum_row[m, 1:2] = jnp.sum(total_b, axis=0, keepdims=True)

        def send_state(k, carry):
            state_copy(m, k, me).start()
            return carry

        lax.fori_loop(me + 1, peers, send_state, 0)

        @pl.when(m == 0)
        def _():
            weight_copies[2].wait()

        sg[m] = dot_nn(lg[m], wg[...])
        acc[...] = dot_nn(low_mask[m], split[...])

        def receive_state(k, held):
            state_copy(m, k, k).wait_recv()
            unbroken = segment(k * row_count - 1, starts) == segment(
                (k + 1) * row_count - 1, starts
            )
            passing = jnp.where(unbroken, 1.0, 0.0) * decay_block
            return (
                passing * held[0] + states[m, k, 0:1],
                passing * held[1] + states[m, k, 1:2],
            )

        none = jnp.zeros((1, width), F32)
        enter_a, enter_b = lax.fori_loop(0, me, receive_state, (none, none))
        prior_segment = segment(base - 1, starts)

        def mix_states(i, carry):
            rows = span_of(i)
            falling = e0[rows, :]
            chosen = jnp.where(segment(column(i), starts) == prior_segment, 1.0, 0.0)
            grown = falling * grow_block
            held = falling * chosen
            state_a = grown * acc[rows, 0:width] + held * enter_a
            state_b = grown * acc[rows, width:] + held * enter_b
            sa[m, rows, :] = state_a
            sb[m, rows, :] = state_b
            present = jnp.exp(extra[...] + kk[m, rows, :])
            gate = sigmoid(sg[m, rows, :])
            sg[m, rows, :] = gate
            found = (state_a + present * vv[m, rows, :]) / (state_b + present)
            lgt[m, rows, :] = (gate * found).astype(BF16)
            return carry

        lax.fori_loop(0, chunks, mix_states, 0)

        @pl.when(m == 0)
        def _():
            weight_copies[3].wait()

        mid[m] = xs[m].astype(F32) + dot_nn(lgt[m], wo[...])

        @pl.when(has_right)
        def _():
            middle_halo(m).start()

        def mix_second(i, last):
            rows = span_of(i)
            normed, _ = normalise(mid[m, rows, :])
            normed = normed * gain2[...] + bias2[...]
            earlier = moved_down(normed, last) * keep_of(column(i), starts)
            gap = normed - earlier
            lh[m, rows, :] = (earlier + gap * mix_h[...]).astype(BF16)
            lf[m, rows, :] = (earlier + gap * mix_f[...]).astype(BF16)
            return normed[RB - 1 : RB]

        lax.fori_loop(0, chunks, mix_second, none)

        @pl.when(has_left)
        def _():
            middle_halo(m).wait_recv()

        halo_rows, _ = normalise(hmid[m])
        halo_rows = halo_rows * gain2[...] + bias2[...]
        halo2[m] = halo_rows
        mix_second(0, halo_rows[7:8])

        @pl.when(m == 0)
        def _():
            for copy in weight_copies[4:7]:
                copy.wait()

        sv[m] = dot_nn(lf[m], wf[...])

        def widen(j, carry):
            columns = pl.ds(pl.multiple_of(j * width, width), width)
            active = jnp.maximum(dot_nn(lh[m], wh[:, columns]), 0.0)
            act[m, :, columns] = active.astype(BF16)
            sq[m, :, columns] = (active * active).astype(BF16)
            return carry

        lax.fori_loop(0, hidden // width, widen, 0)
        proj[m] = dot_nn(sq[m], wp[...])

        def finish(i, carry):
            rows = span_of(i)
            sieve = sigmoid(sv[m, rows, :])
            sv[m, rows, :] = sieve
            out[m, rows, :] = (mid[m, rows, :] + sieve * proj[m, rows, :]).astype(BF16)
            return carry

        lax.fori_loop(0, chunks, finish, 0)

        @pl.when(has_next)
        def _():
            result_copy(m).start()

        @pl.when(has_next & has_right)
        def _():
            result_halo(m).start()

        return carry

    lax.fori_loop(0, batches, forward, 0)

    def add_vector(index, value):
        vg[index] += fold(value)

    @pl.when(me_s == sections - 1)
    def _():
        pltpu.make_async_copy(top_in, dys, top_sem).wait()

    def backward(m, carry):
        starts = starts_of(m)
        none = jnp.zeros((1, width), F32)

        @pl.when(has_next)
        def _():
            back_copy(m).wait_recv()

        def open_back(i, carry):
            rows = span_of(i)
            incoming = dys[m, rows, :].astype(F32)
            sieve = sv[m, rows, :]
            gained = incoming * sieve
            dproj[m, rows, :] = gained.astype(BF16)
            dsv[m, rows, :] = (gained * proj[m, rows, :] * (1.0 - sieve)).astype(BF16)
            return carry

        lax.fori_loop(0, chunks, open_back, 0)
        t1[...] = jnp.zeros_like(t1)

        def narrow(j, carry):
            columns = pl.ds(pl.multiple_of(j * width, width), width)
            grown = dot_nt(dproj[m], wp[columns, :])
            dh[m, :, columns] = (grown * 2.0 * act[m, :, columns].astype(F32)).astype(BF16)
            t1[...] += dot_nt(dh[m, :, columns], wh[:, columns])
            return carry

        lax.fori_loop(0, hidden // width, narrow, 0)
        t2[...] = dot_nt(dsv[m], wf[...])

        def second_earlier(rows, position):
            whole = t1[rows, :] * (1.0 - mix_h[...]) + t2[rows, :] * (1.0 - mix_f[...])
            return whole * keep_of(position, starts)

        eight = lax.broadcasted_iota(jnp.int32, (8, 1), 0)
        send_de2[m] = second_earlier(pl.ds(0, 8), base + eight)

        @pl.when(has_left)
        def _():
            second_copy(m).start()

        def back_second(i, last, following):
            rows = span_of(i)
            spare, spread = normalise(mid[m, rows, :])
            normed = spare * gain2[...] + bias2[...]
            kept = keep_of(column(i), starts)
            gap = normed - moved_down(normed, last) * kept
            from_h = t1[rows, :]
            from_f = t2[rows, :]
            add_vector(9, from_h * gap)
            add_vector(10, from_f * gap)
            straight = from_h * mix_h[...] + from_f * mix_f[...]
            earlier = (from_h + from_f - straight) * kept
            d_normed = straight + moved_up(earlier, following)
            add_vector(7, d_normed * spare)
            add_vector(8, d_normed)
            scaled = d_normed * gain2[...]
            mean_one = jnp.mean(scaled, axis=-1, keepdims=True)
            mean_two = jnp.mean(scaled * spare, axis=-1, keepdims=True)
            d_mid = dys[m, rows, :].astype(F32) + spread * (scaled - mean_one - spare * mean_two)
            t3[rows, :] = d_mid
            datt[m, rows, :] = d_mid.astype(BF16)
            return normed[RB - 1 : RB]

        def following_second(i):
            start = pl.multiple_of((i + 1) * RB, RB)
            return second_earlier(pl.ds(start, 8), base + start + eight)[0:1]

        last = lax.fori_loop(
            0, chunks - 1,
            lambda i, last: back_second(i, last, following_second(i)),
            halo2[m, 7:8],
        )

        @pl.when(has_right)
        def _():
            second_copy(m).wait_recv()

        back_second(chunks - 1, last, de2[m, 0:1])
        t1[...] = dot_nt(datt[m], wo[...])
        open_segment = segment(base, starts)

        def back_states_in(i, totals):
            rows = span_of(i)
            d_gated = t1[rows, :]
            gate = sg[m, rows, :]
            keys = kk[m, rows, :]
            values = vv[m, rows, :]
            present = jnp.exp(extra[...] + keys)
            inverse = 1.0 / (sb[m, rows, :] + present)
            found = (sa[m, rows, :] + present * values) * inverse
            d_found = d_gated * gate
            dg[m, rows, :] = (d_found * found * (1.0 - gate)).astype(BF16)
            d_a = d_found * inverse
            d_b = -d_a * found
            d_key = (d_a * values + d_b) * present
            add_vector(6, d_key)
            t1[rows, :] = d_key
            t2[rows, :] = d_a * present
            falling = e0[rows, :]
            scaled_a = d_a * falling
            scaled_b = d_b * falling
            high_a = scaled_a.astype(BF16)
            high_b = scaled_b.astype(BF16)
            split[rows, 0:width] = high_a
            split[rows, width:] = high_b
            low = pl.ds(pl.multiple_of(row_count + i * RB, RB), RB)
            split[low, 0:width] = (scaled_a - high_a.astype(F32)).astype(BF16)
            split[low, width:] = (scaled_b - high_b.astype(F32)).astype(BF16)
            chosen = segment(column(i), starts) == open_segment
            return (
                totals[0] + fold(jnp.where(chosen, scaled_a, 0.0)),
                totals[1] + fold(jnp.where(chosen, scaled_b, 0.0)),
            )

        nothing = jnp.zeros((8, width), F32)
        total_a, total_b = lax.fori_loop(0, chunks, back_states_in, (nothing, nothing))
        sum_back[m, 0:1] = jnp.sum(total_a, axis=0, keepdims=True)
        sum_back[m, 1:2] = jnp.sum(total_b, axis=0, keepdims=True)

        def send_state(k, carry):
            back_state_copy(m, k, me).start()
            return carry

        lax.fori_loop(0, me, send_state, 0)
        acc[...] = dot_nn(up_mask[m], split[...])

        def receive_state(turn, held):
            k = peers - 1 - turn
            back_state_copy(m, k, k).wait_recv()
            first = segment(k * row_count, starts)
            unbroken = first == segment((k + 1) * row_count - 1, starts)
            joined = jnp.where(first == segment(k * row_count - 1, starts), 1.0, 0.0)
            passing = jnp.where(unbroken, 1.0, 0.0) * decay_block
            return (
                joined * (passing * held[0] + back_states[m, k, 0:1]),
                joined * (passing * held[1] + back_states[m, k, 1:2]),
            )

        enter_a, enter_b = lax.fori_loop(0, peers - 1 - me, receive_state, (none, none))
        end_segment = segment(base + row_count - 1, starts)

        def back_keys(i, carry):
            rows = span_of(i)
            rising = e1[rows, :]
            chosen = jnp.where(segment(column(i), starts) == end_segment, 1.0, 0.0)
            grown = rising * grow_block
            held = rising * chosen
            d_a = grown * acc[rows, 0:width] + held * enter_a
            d_b = grown * acc[rows, width:] + held * enter_b
            add_vector(5, d_a * sa[m, rows, :] + d_b * sb[m, rows, :])
            weight = jnp.exp(kk[m, rows, :])
            dv[m, rows, :] = (t2[rows, :] + d_a * weight).astype(BF16)
            dk[m, rows, :] = (t1[rows, :] + (d_a * vv[m, rows, :] + d_b) * weight).astype(BF16)
            return carry

        lax.fori_loop(0, chunks, back_keys, 0)
        t1[...] = dot_nt(dk[m], wk[...])
        t2[...] = dot_nt(dv[m], wv[...])
        acc[:, 0:width] = dot_nt(dg[m], wg[...])

        def first_earlier(rows, position):
            whole = (
                t1[rows, :] * (1.0 - mix_k[...])
                + t2[rows, :] * (1.0 - mix_v[...])
                + acc[rows, 0:width] * (1.0 - mix_g[...])
            )
            return whole * keep_of(position, starts)

        send_de1[m] = first_earlier(pl.ds(0, 8), base + eight)

        @pl.when(has_left)
        def _():
            first_copy(m).start()

        def back_first(i, last, following):
            rows = span_of(i)
            spare, spread = normalise(xs[m, rows, :].astype(F32))
            normed = spare * gain1[...] + bias1[...]
            kept = keep_of(column(i), starts)
            gap = normed - moved_down(normed, last) * kept
            from_k = t1[rows, :]
            from_v = t2[rows, :]
            from_g = acc[rows, 0:width]
            add_vector(2, from_k * gap)
            add_vector(3, from_v * gap)
            add_vector(4, from_g * gap)
            straight = from_k * mix_k[...] + from_v * mix_v[...] + from_g * mix_g[...]
            earlier = (from_k + from_v + from_g - straight) * kept
            d_normed = straight + moved_up(earlier, following)
            add_vector(0, d_normed * spare)
            add_vector(1, d_normed)
            scaled = d_normed * gain1[...]
            mean_one = jnp.mean(scaled, axis=-1, keepdims=True)
            mean_two = jnp.mean(scaled * spare, axis=-1, keepdims=True)
            found = t3[rows, :] + spread * (scaled - mean_one - spare * mean_two)
            back[m, rows, :] = found.astype(BF16)
            return normed[RB - 1 : RB]

        def following_first(i):
            start = pl.multiple_of((i + 1) * RB, RB)
            return first_earlier(pl.ds(start, 8), base + start + eight)[0:1]

        last = lax.fori_loop(
            0, chunks - 1,
            lambda i, last: back_first(i, last, following_first(i)),
            halo1[m, 7:8],
        )

        @pl.when(has_right)
        def _():
            first_copy(m).wait_recv()

        back_first(chunks - 1, last, de1[m, 0:1])

        @pl.when(has_prior)
        def _():
            back_copy(m).start()

        return carry

    lax.fori_loop(0, batches, backward, 0)

    vgs[...] = jnp.sum(vg[...], axis=1)
    vgs[5:6] = vgs[5:6] * (-rate * jnp.exp(-rate))
    share = vgr.shape[2]

    def part(k):
        if split_vectors:
            return vgs.at[:, pl.ds(pl.multiple_of(k * share, share), share)]
        return vgs

    def vector_copy(k, slot):
        return remote(part(k), vgr.at[slot], s_vg.at[k], r_vg.at[slot], me_s, k)

    def each_peer(action):
        def turn(k, carry):
            @pl.when(k != me)
            def _():
                action(k)

            return carry

        lax.fori_loop(0, peers, turn, 0)

    each_peer(lambda k: vector_copy(k, me).start())
    if split_vectors:
        vec_out[...] = vgs[:, pl.ds(pl.multiple_of(me * share, share), share)]
    else:
        vec_out[...] = vgs[...]

    def collect(k):
        vector_copy(k, k).wait_recv()
        vec_out[...] += vgr[k]

    each_peer(collect)

    each_peer(lambda k: vector_copy(k, me).wait_send())

    def close(m, carry):
        @pl.when((me_s == 0) & has_right)
        def _():
            start_halo(m).wait_send()

        @pl.when(has_next)
        def _():
            result_copy(m).wait_send()

        @pl.when(has_next & has_right)
        def _():
            result_halo(m).wait_send()

        @pl.when(has_right)
        def _():
            middle_halo(m).wait_send()

        @pl.when(has_left)
        def _():
            second_copy(m).wait_send()
            first_copy(m).wait_send()

        @pl.when(has_prior)
        def _():
            back_copy(m).wait_send()

        def ended(k, carry):
            state_copy(m, k, me).wait_send()
            return carry

        lax.fori_loop(me + 1, peers, ended, 0)

        def ended_back(k, carry):
            back_state_copy(m, k, me).wait_send()
            return carry

        lax.fori_loop(0, me, ended_back, 0)
        return carry

    lax.fori_loop(0, batches, close, 0)


def relay(sections, peers, x, top, spans, vectors, matrices):
    batches, rows, width = x.shape
    hidden = matrices[4].shape[1]
    share = width // peers
    split_vectors = share % 128 == 0
    if not split_vectors:
        share = width
    shape = jax.ShapeDtypeStruct
    low = shape((batches, rows, width), BF16)
    low_wide = shape((batches, rows, hidden), BF16)
    vmem = pl.BlockSpec(memory_space=pltpu.VMEM)
    anywhere = pl.BlockSpec(memory_space=pl.ANY)
    dma = pltpu.SemaphoreType.DMA

    def narrow(kind):
        return pltpu.VMEM((batches, rows, width), kind)

    return pl.pallas_call(
        partial(relay_kernel, sections, peers, split_vectors),
        out_shape=(
            low, low, shape((VECTORS, share), F32),
            low, low, low, low, low, low, low_wide,
            low, low, low, low, low, low, low_wide,
        ),
        in_specs=[pl.BlockSpec(memory_space=pltpu.SMEM), anywhere, anywhere]
        + [vmem] * 11
        + [anywhere] * 7,
        out_specs=[vmem] * 17,
        scratch_shapes=[pltpu.VMEM(matrix.shape, BF16) for matrix in matrices_order(matrices)]
        + [
            narrow(BF16), pltpu.VMEM((batches, 16, width), BF16), narrow(BF16),
            narrow(F32), narrow(F32), narrow(F32), narrow(F32), narrow(F32), narrow(F32),
            pltpu.VMEM((batches, 8, width), F32), narrow(F32), narrow(F32),
            pltpu.VMEM((batches, rows, hidden), BF16),
            pltpu.VMEM((batches, 8, width), F32), pltpu.VMEM((batches, 8, width), F32),
            pltpu.VMEM((rows, width), F32), pltpu.VMEM((rows, width), F32),
            pltpu.VMEM((batches, rows, 2 * rows), BF16), pltpu.VMEM((batches, rows, 2 * rows), BF16),
            pltpu.VMEM((2 * rows, 2 * width), BF16), pltpu.VMEM((rows, 2 * width), F32),
            pltpu.VMEM((rows, width), F32), pltpu.VMEM((rows, width), F32), pltpu.VMEM((rows, width), F32),
            pltpu.VMEM((batches, peers, 2, width), F32), pltpu.VMEM((batches, peers, 2, width), F32),
            pltpu.VMEM((batches, 8, width), F32), pltpu.VMEM((batches, 8, width), F32),
            pltpu.VMEM((batches, 2, width), F32), pltpu.VMEM((batches, 2, width), F32),
            pltpu.VMEM((batches, 8, width), F32), pltpu.VMEM((batches, 8, width), F32),
            pltpu.VMEM((VECTORS, 8, width), F32), pltpu.VMEM((VECTORS, width), F32),
            pltpu.VMEM((peers, VECTORS, share), F32),
            dma((7,)), dma, dma,
            dma((batches,)), dma((batches,)), dma((batches,)), dma((batches, peers)), dma((batches,)),
            dma((batches,)), dma((batches,)), dma((batches, peers)), dma((batches,)), dma((peers,)),
            dma((batches,)), dma((batches,)), dma((batches, peers)), dma((batches,)),
            dma((batches,)), dma((batches,)), dma((batches, peers)), dma((batches,)), dma((peers,)),
        ],
        compiler_params=pltpu.CompilerParams(
            collective_id=0, has_side_effects=True, vmem_limit_bytes=63 * 2**20
        ),
        name="relay",
    )(spans, x, top, *vectors, *matrices_order(matrices))


def matrices_order(matrices):
    wk, wv, wg, wo, wh, wp, wf = matrices
    return (wk, wv, wg, wo, wh, wp, wf)


def per_device(x, top, spans, *parameters):
    sections = lax.axis_size("section")
    peers = lax.axis_size("dp")
    gain1, bias1, mix_k, mix_v, mix_g, log_rate, extra = parameters[0:7]
    wk, wv, wg, wo = parameters[7:11]
    gain2, bias2, mix_h, mix_f = parameters[11:15]
    wh, wp, wf = parameters[15:18]
    vectors = (gain1, bias1, mix_k, mix_v, mix_g, log_rate, extra, gain2, bias2, mix_h, mix_f)
    matrices = tuple(w[0] for w in (wk, wv, wg, wo, wh, wp, wf))
    found = relay(sections, peers, x, top, spans, vectors, matrices)
    out, back, vec = found[0:3]
    lk, lv, lg, lgt, lh, lf, sq = found[3:10]
    dk, dv, dg, datt, dproj, dsv, dh = found[10:17]
    share = x.shape[2] // peers
    if vec.shape[1] != share:
        vec = lax.dynamic_slice_in_dim(vec, lax.axis_index("dp") * share, share, 1)

    def weight_grad(left, right):
        local = lax.dot_general(
            left, right, (((0, 1), (0, 1)), ((), ())), preferred_element_type=F32
        )
        whole = lax.psum_scatter(local.astype(BF16), "dp", scatter_dimension=0, tiled=True)
        return whole.astype(F32)[None]

    def row(index):
        return vec[index : index + 1]

    return (
        out[None], back[None],
        row(0), row(1), row(2), row(3), row(4), row(5), row(6),
        weight_grad(lk, dk), weight_grad(lv, dv), weight_grad(lg, dg), weight_grad(lgt, datt),
        row(7), row(8), row(9), row(10),
        weight_grad(lh, dh), weight_grad(sq, dproj), weight_grad(lf, dsv),
    )


def solution(mesh):
    tokens = P(None, "dp", None)
    vector = P("section", None)
    matrix = P("section", None, None)
    result = P("section", None, "dp", None)
    vector_grad = P("section", "dp")
    matrix_grad = P("section", "dp", None)
    return jax.shard_map(
        per_device,
        mesh=mesh,
        in_specs=(tokens, tokens, P())
        + (vector,) * 7 + (matrix,) * 4 + (vector,) * 4 + (matrix,) * 3,
        out_specs=(result, result)
        + (vector_grad,) * 7 + (matrix_grad,) * 4 + (vector_grad,) * 4 + (matrix_grad,) * 3,
        check_vma=False,
    )
```

time: 1650 us -> 580 us (0.35); the launches traced: 1630 us -> 579 us
  matrix products: 551 us -> 22.9 us
  blocking collectives: 466 us -> 0 us
  Pallas kernels: 0 us -> 193 us
  local copies, waits for them, and re-layouts: 90.8 us -> 5.43 us
  starting transfers between devices: 58.4 us -> 0.47 us
  waiting for transfers between devices: 377 us -> 328 us
  other arithmetic: 62.7 us -> 14.5 us
    dot_general x250 -> x7, matrix products: 551 us -> 22.9 us  [weight_grad(): lax.dot_general(left, right, (((0, 1), (0, 1)), ((), ())), preferred_elem...]
    all_gather x30 -> x0, blocking collectives: 433 us -> none  [entering(): everything = jax.tree.map(lambda part: lax.all_gather(part, axis), x)]
    pallas_call x0 -> x1, Pallas kernels: none -> 193 us  [relay(): pl.pallas_call(partial(relay_kernel, sections, peers, split_vectors), out...]
    ppermute x28 -> x0, starting transfers between devices: 57.3 us -> none  [passed_along(): return lax.ppermute(x, axis, pairs)]
    unnamed x1225 -> x32, local copies, waits for them, and re-layouts: 44.5 us -> 4.88 us
    dynamic_slice x161 -> x0, local copies, waits for them, and re-layouts: 33.8 us -> none  [the longest x160 32.8 us: turn(): new = combine(before, jax.tree.map(lambda part: part[at], everything))]
    unnamed x1 -> x0, blocking collectives: 32.6 us -> none
    ppermute x28 -> x0, waiting for transfers between devices: 30.2 us -> none  [passed_along(): return lax.ppermute(x, axis, pairs)]
  transfers between devices with their start and end apart: 35 -> 7, of which waited for: 9 -> 7; matrix products, arithmetic and copies ran while one was open for 17% -> 5% of each run, Pallas kernels for 0% -> 0%
where the time goes in v1:
time: 580 us; the launch traced here: 579 us
  waiting for transfers between devices  328 us (57%)
  Pallas kernels  193 us (33%)
  matrix products  22.9 us (4%)
  other arithmetic  14.5 us (2%)
  between operations  14.3 us (2%)
    reduce_scatter x7, waiting for transfers between devices, weight_grad(): lax.psum_scatter(local.astype(BF16), 'dp', scatter_dimension=0, tiled=True)  328 us
    pallas_call x1, Pallas kernels, relay(): pl.pallas_call(partial(relay_kernel, sections, peers, split_vectors), out...  193 us
    dot_general x7, matrix products, weight_grad(): lax.dot_general(left, right, (((0, 1), (0, 1)), ((), ())), preferred_elem...  22.9 us
    broadcast_in_dim x7, other arithmetic, weight_grad(): return whole.astype(F32)[None]  14.5 us
  transfers between devices with their start and end apart: 7, of which 7 were waited for; matrix products, arithmetic and copies ran while one was open for 5% of the time, Pallas kernels for 0%

profile of v1, /device:TPU:0, one launch (start us, length us, event | category | flops | bytes accessed | tf_op | source)
XLA Modules:
  0.0 579.1 jit_solution(14711986086437008904)
XLA Ops:
  7.2 193.1 %relay.1 = (bf16[2,128,1024]{2,1,0:T(8,128)(2,1)}, bf16[2,128,1024]{2,1,0:T(8,128)(2,1)}, f32[16,128]{1,0:T(8,128)}, bf16[2,128,1024]{2,1,0:T(8,128)(2,1)}, bf16...) custom-call(s32[2,5]{1,0:T(2,128)} %refs_0_.1, ...), custom_call_target="tpu_custom_call" | custom-call | tf_op jit(solution)/shard_map/relay/pallas_call | solution.py:750
  200.3 3.4 bitcast_convert_fusion.6
  203.8 2.1 bitcast_convert_fusion.5
  206.0 2.1 bitcast_convert_fusion.4
  208.4 2.1 bitcast_convert_fusion.3
  210.5 2.1 bitcast_convert_fusion.2
  212.7 1.0 copy-done.13
  213.7 5.6 bitcast_convert_fusion.1
  219.4 1.5 copy-done
  221.0 5.6 bitcast_convert_fusion
  227.9 11.7 %reduce-scatter.8.cloned.1.call-done = bf16[128,1024]{1,0:T(8,128)(2,1)} async-done(((bf16[1024,1024]{1,0:T(8,128)(2,1)}), bf16[128,1024]{1,0:T(8,128)(2,1)}) %reduce-scatter.8.cloned.1.call-update) | async-done | bytes 262160 | tf_op jit(solution)/shard_map/reduce_scatter | solution.py:817
  239.6 1.8 bitcast_convert_fusion.13
  241.4 35.6 %reduce-scatter.10.cloned.1.call-done = bf16[128,1024]{1,0:T(8,128)(2,1)} async-done(((bf16[1024,1024]{1,0:T(8,128)(2,1)}), bf16[128,1024]{1,0:T(8,128)(2,1)}) %reduce-scatter.10.cloned.1.call-update) | async-done | bytes 262160 | tf_op jit(solution)/shard_map/reduce_scatter | solution.py:817
  276.9 1.8 bitcast_convert_fusion.12
  278.7 35.0 %reduce-scatter.12.cloned.1.call-done = bf16[128,1024]{1,0:T(8,128)(2,1)} async-done(((bf16[1024,1024]{1,0:T(8,128)(2,1)}), bf16[128,1024]{1,0:T(8,128)(2,1)}) %reduce-scatter.12.cloned.1.call-update) | async-done | bytes 262160 | tf_op jit(solution)/shard_map/reduce_scatter | solution.py:817
  313.7 1.8 bitcast_convert_fusion.11
  315.5 34.9 %reduce-scatter.14.cloned.1.call-done = bf16[128,1024]{1,0:T(8,128)(2,1)} async-done(((bf16[1024,1024]{1,0:T(8,128)(2,1)}), bf16[128,1024]{1,0:T(8,128)(2,1)}) %reduce-scatter.14.cloned.1.call-update) | async-done | bytes 262160 | tf_op jit(solution)/shard_map/reduce_scatter | solution.py:817
  350.4 1.8 bitcast_convert_fusion.10
  352.2 34.9 %reduce-scatter.20.cloned.1.call-done = bf16[128,1024]{1,0:T(8,128)(2,1)} async-done(((bf16[1024,1024]{1,0:T(8,128)(2,1)}), bf16[128,1024]{1,0:T(8,128)(2,1)}) %reduce-scatter.20.cloned.1.call-update) | async-done | bytes 262160 | tf_op jit(solution)/shard_map/reduce_scatter | solution.py:817
  387.1 1.8 bitcast_convert_fusion.9
  388.9 88.7 %reduce-scatter.16.cloned.1.call-done = bf16[128,4096]{1,0:T(8,128)(2,1)} async-done(((bf16[1024,4096]{1,0:T(8,128)(2,1)}), bf16[128,4096]{1,0:T(8,128)(2,1)}) %reduce-scatter.16.cloned.1.call-update) | async-done | bytes 1048592 | tf_op jit(solution)/shard_map/reduce_scatter | solution.py:817
  477.6 2.8 bitcast_convert_fusion.8
  480.4 87.5 %reduce-scatter.18.cloned.1.call-done = bf16[512,1024]{1,0:T(8,128)(2,1)} async-done(((bf16[4096,1024]{1,0:T(8,128)(2,1)}), bf16[512,1024]{1,0:T(8,128)(2,1)}) %reduce-scatter.18.cloned.1.call-update) | async-done | bytes 1048592 | tf_op jit(solution)/shard_map/reduce_scatter | solution.py:817
  567.9 2.8 bitcast_convert_fusion.7
  (45 shorter events, 3.5 us)
Async XLA Ops:
  7.2 232.4 %reduce-scatter.8.cloned.1.call-start = ((), (), s32[]{:S(2)}) async-start(), calls=%async_computation.7 | async-start | bytes 2359296 | tf_op jit(solution)/shard_map/reduce_scatter | solution.py:817
  200.3 3.4 copy-start.11
  200.3 3.4 copy-start.12
  203.7 73.2 %reduce-scatter.10.cloned.1.call-start = ((), (), s32[]{:S(2)}) async-start(), calls=%async_computation.8 | async-start | bytes 2359296 | tf_op jit(solution)/shard_map/reduce_scatter | solution.py:817
  203.8 2.2 copy-start.9
  203.8 2.2 copy-start.10
  205.9 107.8 %reduce-scatter.12.cloned.1.call-start = ((), (), s32[]{:S(2)}) async-start(), calls=%async_computation.9 | async-start | bytes 2359296 | tf_op jit(solution)/shard_map/reduce_scatter | solution.py:817
  206.0 2.4 copy-start.7
  206.0 2.4 copy-start.8
  208.1 142.3 %reduce-scatter.14.cloned.1.call-start = ((), (), s32[]{:S(2)}) async-start(), calls=%async_computation.10 | async-start | bytes 2359296 | tf_op jit(solution)/shard_map/reduce_scatter | solution.py:817
  208.3 2.2 copy-start.5
  208.4 2.2 copy-start.6
  210.5 176.6 %reduce-scatter.20.cloned.1.call-start = ((), (), s32[]{:S(2)}) async-start(), calls=%async_computation.13 | async-start | bytes 2359296 | tf_op jit(solution)/shard_map/reduce_scatter | solution.py:817
  210.5 2.2 copy-start.1
  212.6 1.0 copy-start.13
  212.7 264.9 %reduce-scatter.16.cloned.1.call-start = ((), (), s32[]{:S(2)}) async-start(), calls=%async_computation.11 | async-start | bytes 9437184 | tf_op jit(solution)/shard_map/reduce_scatter | solution.py:817
  219.3 1.6 copy-start
  219.3 1.7 copy-start.2
  219.3 348.5 %reduce-scatter.18.cloned.1.call-start = ((), (), s32[]{:S(2)}) async-start(), calls=%async_computation.12 | async-start | bytes 9437184 | tf_op jit(solution)/shard_map/reduce_scatter | solution.py:817
  226.6 0.7 copy-start.14
  480.3 90.3 %copy-start.4 = (bf16[2,128,1024]{2,1,0:T(8,128)(2,1)S(1)}, bf16[2,128,1024]{2,1,0:T(8,128)(2,1)}, u32[]{:S(2)}) copy-start(bf16[2,128,1024]{2,1,0:T(8,128)(2,1)} %get-tuple-element.37) | copy-start | bytes 1572868
  480.4 91.1 %copy-start.3 = (bf16[2,128,1024]{2,1,0:T(8,128)(2,1)S(1)}, bf16[2,128,1024]{2,1,0:T(8,128)(2,1)}, u32[]{:S(2)}) copy-start(bf16[2,128,1024]{2,1,0:T(8,128)(2,1)} %get-tuple-element.38) | copy-start | bytes 1572868
Sparse Core Ops, SparseCore 0:
  203.8 35.7 reduce-scatter.7
  242.5 34.4 reduce-scatter.9
  279.2 34.4 reduce-scatter.11
  315.9 34.5 reduce-scatter.13
  352.6 34.4 reduce-scatter.19
  389.2 88.3 reduce-scatter.15
  479.9 87.9 reduce-scatter.17

commit v2 on v1

--- a/solution.py
+++ b/solution.py
@@ -60,13 +60,15 @@
         spans, x_in, top_in,
         gain1, bias1, mix_k, mix_v, mix_g, log_rate, extra, gain2, bias2, mix_h, mix_f,
         wk_in, wv_in, wg_in, wo_in, wh_in, wp_in, wf_in,
-        out, back, vec_out, lk, lv, lg, lgt, lh, lf, sq, dk, dv, dg, datt, dproj, dsv, dh,
+        out, back, vec_out, lk, lv, lg, lgt, lf, dk, dv, dg, datt, dsv, lh_all, dproj_all,
+        lh, sq, dproj, dh,
         wk, wv, wg, wo, wh, wp, wf,
         xs, hx, dys, kk, vv, sg, sa, sb, mid, hmid, proj, sv, act, halo1, halo2,
         e0, e1, low_mask, up_mask, split, acc, t1, t2, t3,
         states, back_states, de2, de1, sum_row, sum_back, send_de2, send_de1, vg, vgs, vgr,
         w_sem, x_sem, top_sem, s_h0, s_x, s_hx, s_st, s_mid, s_dy, s_de2, s_bst, s_de1, s_vg,
         r_x, r_hx, r_st, r_mid, r_dy, r_de2, r_bst, r_de1, r_vg,
+        s_lh, r_lh, s_dp, r_dp, own_sem,
     ) = refs
     me_s = lax.axis_index("section")
     me = lax.axis_index("dp")
@@ -234,6 +236,41 @@
         return remote(
             sum_back.at[m], back_states.at[m, slot], s_bst.at[m, k], r_bst.at[m, slot], me_s, k
         )
+
+    chip, core = me // 2, me % 2
+    chips = peers // 2
+
+    def gather_copy(which, m, k, slot):
+        source, target, send, receive = (
+            (lh, lh_all, s_lh, r_lh) if which == 0 else (dproj, dproj_all, s_dp, r_dp)
+        )
+        return remote(
+            source.at[m], target.at[m, slot], send.at[m, k], receive.at[m, slot],
+            me_s, 2 * k + core,
+        )
+
+    def own_copy(which, m):
+        source, target = (lh, lh_all) if which == 0 else (dproj, dproj_all)
+        return pltpu.make_async_copy(source.at[m], target.at[m, chip], own_sem.at[which, m])
+
+    def each_chip(action):
+        def turn(k, carry):
+            @pl.when(k != chip)
+            def _():
+                action(k)
+
+            return carry
+
+        lax.fori_loop(0, chips, turn, 0)
+
+    def start_gather(which, m):
+        own_copy(which, m).start()
+        each_chip(lambda k: gather_copy(which, m, k, chip).start())
+
+    def end_gather(which, m):
+        own_copy(which, m).wait()
+        each_chip(lambda k: gather_copy(which, m, k, chip).wait_send())
+        each_chip(lambda k: gather_copy(which, m, k, k).wait_recv())
 
     @pl.when((me_s == 0) & has_right)
     def _():
@@ -383,6 +420,7 @@
         halo_rows = halo_rows * gain2[...] + bias2[...]
         halo2[m] = halo_rows
         mix_second(0, halo_rows[7:8])
+        start_gather(0, m)
 
         @pl.when(m == 0)
         def _():
@@ -447,6 +485,7 @@
             return carry
 
         lax.fori_loop(0, chunks, open_back, 0)
+        start_gather(1, m)
         t1[...] = jnp.zeros_like(t1)
 
         def narrow(j, carry):
@@ -719,6 +758,8 @@
             return carry
 
         lax.fori_loop(me + 1, peers, ended, 0)
+        end_gather(0, m)
+        end_gather(1, m)
 
         def ended_back(k, carry):
             back_state_copy(m, k, me).wait_send()
@@ -739,7 +780,6 @@
         share = width
     shape = jax.ShapeDtypeStruct
     low = shape((batches, rows, width), BF16)
-    low_wide = shape((batches, rows, hidden), BF16)
     vmem = pl.BlockSpec(memory_space=pltpu.VMEM)
     anywhere = pl.BlockSpec(memory_space=pl.ANY)
     dma = pltpu.SemaphoreType.DMA
@@ -751,14 +791,20 @@
         partial(relay_kernel, sections, peers, split_vectors),
         out_shape=(
             low, low, shape((VECTORS, share), F32),
-            low, low, low, low, low, low, low_wide,
-            low, low, low, low, low, low, low_wide,
+            low, low, low, low, low,
+            low, low, low, low, low,
+            shape((batches, peers // 2, rows, width), BF16),
+            shape((batches, peers // 2, rows, width), BF16),
         ),
         in_specs=[pl.BlockSpec(memory_space=pltpu.SMEM), anywhere, anywhere]
         + [vmem] * 11
         + [anywhere] * 7,
-        out_specs=[vmem] * 17,
-        scratch_shapes=[pltpu.VMEM(matrix.shape, BF16) for matrix in matrices_order(matrices)]
+        out_specs=[vmem] * 13 + [anywhere] * 2,
+        scratch_shapes=[
+            narrow(BF16), pltpu.VMEM((batches, rows, hidden), BF16),
+            narrow(BF16), pltpu.VMEM((batches, rows, hidden), BF16),
+        ]
+        + [pltpu.VMEM(matrix.shape, BF16) for matrix in matrices_order(matrices)]
         + [
             narrow(BF16), pltpu.VMEM((batches, 16, width), BF16), narrow(BF16),
             narrow(F32), narrow(F32), narrow(F32), narrow(F32), narrow(F32), narrow(F32),
@@ -780,6 +826,8 @@
             dma((batches,)), dma((batches,)), dma((batches, peers)), dma((batches,)), dma((peers,)),
             dma((batches,)), dma((batches,)), dma((batches, peers)), dma((batches,)),
             dma((batches,)), dma((batches,)), dma((batches, peers)), dma((batches,)), dma((peers,)),
+            dma((batches, peers // 2)), dma((batches, peers // 2)),
+            dma((batches, peers // 2)), dma((batches, peers // 2)), dma((2, batches)),
         ],
         compiler_params=pltpu.CompilerParams(
             collective_id=0, has_side_effects=True, vmem_limit_bytes=63 * 2**20
@@ -791,6 +839,312 @@
 def matrices_order(matrices):
     wk, wv, wg, wo, wh, wp, wf = matrices
     return (wk, wv, wg, wo, wh, wp, wf)
+
+
+def sum_kernel(peers, *refs):
+    left_in, right_in = refs[0:5], refs[5:10]
+    lh_in, dp_in, wh_in, wp_in = refs[10:14]
+    outs, wh_out, wp_out = refs[14:19], refs[19], refs[20]
+    (
+        lefts, rights, whole, own, pair_out, going_right, going_left,
+        lh, dp, wh, wp, act, wide, hid_out, hid_in, proj_out, proj_in,
+        left_sem, right_sem, lh_sem, dp_sem, wh_sem, wp_sem,
+        s_pair, r_pair, s_right, r_right, s_left, r_left, s_hid, r_hid, s_proj, r_proj,
+    ) = refs[21:]
+    count = len(left_in)
+    me_s = lax.axis_index("section")
+    me = lax.axis_index("dp")
+    chips = peers // 2
+    chip, core = me // 2, me % 2
+    sibling = me + 1 - 2 * core
+    blocks, share = chips, own.shape[2]
+    columns = wh.shape[2]
+    has_right = chip + 1 < chips
+    has_left = chip > 0
+    after = jnp.minimum(me + 2, peers - 1)
+    before = jnp.maximum(me - 2, 0)
+
+    barrier = pltpu.get_barrier_semaphore()
+
+    def greet(index):
+        pl.semaphore_signal(barrier, inc=1, device_id=(me_s, index), device_id_type=MESH)
+
+    greet(sibling)
+
+    @pl.when(has_right)
+    def _():
+        greet(after)
+
+    @pl.when(has_left)
+    def _():
+        greet(before)
+
+    for w in range(count):
+        pltpu.make_async_copy(left_in[w], lefts.at[w], left_sem.at[w]).start()
+        pltpu.make_async_copy(right_in[w], rights.at[w], right_sem.at[w]).start()
+    lh_copy = pltpu.make_async_copy(lh_in, lh, lh_sem)
+    dp_copy = pltpu.make_async_copy(dp_in, dp, dp_sem)
+    lh_copy.start()
+    dp_copy.start()
+
+    def wh_copy(j, slot):
+        return pltpu.make_async_copy(
+            wh_in.at[:, pl.ds(pl.multiple_of(j * columns, columns), columns)],
+            wh.at[slot], wh_sem.at[slot],
+        )
+
+    def wp_copy(j, slot):
+        return pltpu.make_async_copy(
+            wp_in.at[pl.ds(pl.multiple_of(j * columns, columns), columns)],
+            wp.at[slot], wp_sem.at[slot],
+        )
+
+    wh_copy(0, 0).start()
+    wp_copy(0, 0).start()
+    pl.semaphore_wait(
+        barrier, 1 + jnp.where(has_right, 1, 0) + jnp.where(has_left, 1, 0)
+    )
+
+    def remote(source, target, send, receive, index):
+        return pltpu.make_async_remote_copy(
+            src_ref=source, dst_ref=target, send_sem=send, recv_sem=receive,
+            device_id=(me_s, index), device_id_type=MESH,
+        )
+
+    def pair_copy(w):
+        return remote(pair_out.at[w], own.at[w], s_pair.at[w], r_pair.at[w], sibling)
+
+    def rows_of(block, parity):
+        return pl.ds(pl.multiple_of((2 * block + parity) * share, share), share)
+
+    def prepare(w):
+        pltpu.make_async_copy(lefts.at[w], lefts.at[w], left_sem.at[w]).wait()
+        pltpu.make_async_copy(rights.at[w], rights.at[w], right_sem.at[w]).wait()
+        slot = w % 2
+        whole[slot] = dot_tn(lefts[w], rights[w])
+
+        def divide(q, carry):
+            pair_out[w, q] = whole[slot, rows_of(q, 1 - core), :].astype(BF16)
+            return carry
+
+        lax.fori_loop(0, blocks, divide, 0)
+        pair_copy(w).start()
+
+    def combine(w):
+        slot = w % 2
+        pair_copy(w).wait_recv()
+
+        def add(q, carry):
+            own[w, q] = (
+                whole[slot, rows_of(q, core), :] + own[w, q].astype(F32)
+            ).astype(BF16)
+            return carry
+
+        lax.fori_loop(0, blocks, add, 0)
+
+    def right_copy(source, w, r):
+        return remote(source, going_right.at[w, r], s_right.at[w, r], r_right.at[w, r], after)
+
+    def left_copy(source, w, r):
+        return remote(source, going_left.at[w, r], s_left.at[w, r], r_left.at[w, r], before)
+
+    from_end = chips - 1 - chip
+
+    def travel(w, r):
+        prior = jnp.maximum(r - 1, 0)
+
+        @pl.when(has_right & (chip == 0))
+        def _():
+            right_copy(own.at[w, chips - 1 - r], w, r).start()
+
+        @pl.when(has_left & (from_end == 0))
+        def _():
+            left_copy(own.at[w, r], w, r).start()
+
+        @pl.when(has_right & (chip > 0) & (chip <= r))
+        def _():
+            slot = going_right.at[w, prior]
+            right_copy(slot, w, prior).wait_recv()
+            slot[...] = (
+                slot[...].astype(F32) + own[w, chips - 1 - r + chip].astype(F32)
+            ).astype(BF16)
+            right_copy(slot, w, r).start()
+
+        @pl.when(has_left & (from_end > 0) & (from_end <= r))
+        def _():
+            slot = going_left.at[w, prior]
+            left_copy(slot, w, prior).wait_recv()
+            slot[...] = (
+                slot[...].astype(F32) + own[w, r - from_end].astype(F32)
+            ).astype(BF16)
+            left_copy(slot, w, r).start()
+
+    def hid_copy(j):
+        place = pl.ds(pl.multiple_of(j * columns, columns), columns)
+        return remote(
+            hid_out.at[:, place], hid_in.at[:, place], s_hid.at[j], r_hid.at[j], sibling
+        )
+
+    proj_copy = remote(proj_out, proj_in, s_proj, r_proj, sibling)
+    group = wide.shape[0]
+    first = chip * 2 * share
+    start = pl.multiple_of(first // group * group, group)
+    inside = first - first // group * group
+
+    def feed(j):
+        slot = j % 2
+        place = pl.ds(pl.multiple_of(j * columns, columns), columns)
+
+        @pl.when(j == 0)
+        def _():
+            lh_copy.wait()
+            dp_copy.wait()
+
+        wh_copy(j, slot).wait()
+        wp_copy(j, slot).wait()
+
+        @pl.when(j + 1 < peers)
+        def _():
+            wh_copy(j + 1, 1 - slot).start()
+            wp_copy(j + 1, 1 - slot).start()
+
+        active = jnp.maximum(dot_nn(lh[...], wh[slot]), 0.0)
+        act[...] = active
+        grown = (dot_nt(dp[...], wp[slot]) * 2.0 * act[...]).astype(BF16)
+        wide[...] = dot_tn(lh[:, pl.ds(start, group)], grown)
+        mine = pl.ds(pl.multiple_of(inside + core * share, 16), share)
+        other = pl.ds(pl.multiple_of(inside + (1 - core) * share, 16), share)
+        wh_out[:, place] = wide[mine, :]
+        hid_out[:, place] = wide[other, :].astype(BF16)
+        hid_copy(j).start()
+
+        @pl.when(j == 2 * chip + core)
+        def _():
+            squared = (act[...] * act[...]).astype(BF16)
+            wp_out[...] = dot_tn(squared, dp[...])
+
+        @pl.when(j == 2 * chip + 1 - core)
+        def _():
+            squared = (act[...] * act[...]).astype(BF16)
+            proj_out[...] = dot_tn(squared, dp[...]).astype(BF16)
+            proj_copy.start()
+
+    prepare(0)
+    prepare(1)
+    combine(0)
+    rounds = chips - 1
+
+    def step(t, carry):
+        w, r = t // rounds, t % rounds
+        travel(w, r)
+
+        @pl.when((r == 1) & (w + 2 < count))
+        def _():
+            prepare(w + 2)
+
+        @pl.when((r == 1) & (w + 1 < count))
+        def _():
+            combine(w + 1)
+
+        @pl.when((t % 2 == 0) & (t // 2 < peers))
+        def _():
+            feed(t // 2)
+
+        return carry
+
+    lax.fori_loop(0, count * rounds, step, 0)
+
+    for w in range(count):
+        outs[w][...] = own[w, chip].astype(F32)
+
+        @pl.when(has_left)
+        def _():
+            right_copy(own.at[w, 0], w, rounds - 1).wait_recv()
+            outs[w][...] += going_right[w, rounds - 1].astype(F32)
+
+        @pl.when(has_right)
+        def _():
+            left_copy(own.at[w, 0], w, rounds - 1).wait_recv()
+            outs[w][...] += going_left[w, rounds - 1].astype(F32)
+
+    def gather_hidden(j, carry):
+        hid_copy(j).wait_recv()
+        place = pl.ds(pl.multiple_of(j * columns, columns), columns)
+        wh_out[:, place] += hid_in[:, place].astype(F32)
+        return carry
+
+    lax.fori_loop(0, peers, gather_hidden, 0)
+    proj_copy.wait_recv()
+    wp_out[...] += proj_in[...].astype(F32)
+
+    def sent_hidden(j, carry):
+        hid_copy(j).wait_send()
+        return carry
+
+    lax.fori_loop(0, peers, sent_hidden, 0)
+    proj_copy.wait_send()
+
+    def sent(w, carry):
+        pair_copy(w).wait_send()
+
+        def sent_round(r, inner):
+            @pl.when(has_right & (chip <= r))
+            def _():
+                right_copy(own.at[w, 0], w, r).wait_send()
+
+            @pl.when(has_left & (from_end <= r))
+            def _():
+                left_copy(own.at[w, 0], w, r).wait_send()
+
+            return inner
+
+        lax.fori_loop(0, rounds, sent_round, 0)
+        return carry
+
+    lax.fori_loop(0, count, sent, 0)
+
+
+def gradient_sums(peers, lefts, rights, lh, dp, wh, wp):
+    count = len(lefts)
+    rows, width = lefts[0].shape
+    hidden = wh.shape[1]
+    tokens = lh.shape[0]
+    chips = peers // 2
+    share = width // peers
+    columns = hidden // peers
+    group = max(128, 2 * share)
+    shape = jax.ShapeDtypeStruct
+    vmem = pl.BlockSpec(memory_space=pltpu.VMEM)
+    anywhere = pl.BlockSpec(memory_space=pl.ANY)
+    dma = pltpu.SemaphoreType.DMA
+    blocks = pltpu.VMEM((count, chips, share, width), BF16)
+    slots = pltpu.VMEM((count, chips - 1, share, width), BF16)
+    return pl.pallas_call(
+        partial(sum_kernel, peers),
+        out_shape=(shape((share, width), F32),) * count
+        + (shape((share, hidden), F32), shape((columns, width), F32)),
+        in_specs=[anywhere] * (2 * count + 4),
+        out_specs=[vmem] * (count + 2),
+        scratch_shapes=[
+            pltpu.VMEM((count, rows, width), BF16), pltpu.VMEM((count, rows, width), BF16),
+            pltpu.VMEM((2, width, width), F32),
+            blocks, blocks, slots, slots,
+            pltpu.VMEM((tokens, width), BF16), pltpu.VMEM((tokens, width), BF16),
+            pltpu.VMEM((2, width, columns), BF16), pltpu.VMEM((2, columns, width), BF16),
+            pltpu.VMEM((tokens, columns), F32), pltpu.VMEM((group, columns), F32),
+            pltpu.VMEM((share, hidden), BF16), pltpu.VMEM((share, hidden), BF16),
+            pltpu.VMEM((columns, width), BF16), pltpu.VMEM((columns, width), BF16),
+            dma((count,)), dma((count,)), dma, dma, dma((2,)), dma((2,)),
+            dma((count,)), dma((count,)),
+            dma((count, chips - 1)), dma((count, chips - 1)),
+            dma((count, chips - 1)), dma((count, chips - 1)),
+            dma((peers,)), dma((peers,)), dma, dma,
+        ],
+        compiler_params=pltpu.CompilerParams(
+            collective_id=1, has_side_effects=True, vmem_limit_bytes=63 * 2**20
+        ),
+        name="gradient_sums",
+    )(*lefts, *rights, lh, dp, wh, wp)
 
 
 def per_device(x, top, spans, *parameters):
@@ -804,18 +1158,16 @@
     matrices = tuple(w[0] for w in (wk, wv, wg, wo, wh, wp, wf))
     found = relay(sections, peers, x, top, spans, vectors, matrices)
     out, back, vec = found[0:3]
-    lk, lv, lg, lgt, lh, lf, sq = found[3:10]
-    dk, dv, dg, datt, dproj, dsv, dh = found[10:17]
+    flat = (x.shape[0] * x.shape[1], x.shape[2])
+    lk, lv, lg, lgt, lf, dk, dv, dg, datt, dsv = (part.reshape(flat) for part in found[3:13])
+    lh, dproj = (part.reshape(-1, x.shape[2]) for part in found[13:15])
     share = x.shape[2] // peers
     if vec.shape[1] != share:
         vec = lax.dynamic_slice_in_dim(vec, lax.axis_index("dp") * share, share, 1)
-
-    def weight_grad(left, right):
-        local = lax.dot_general(
-            left, right, (((0, 1), (0, 1)), ((), ())), preferred_element_type=F32
-        )
-        whole = lax.psum_scatter(local.astype(BF16), "dp", scatter_dimension=0, tiled=True)
-        return whole.astype(F32)[None]
+    summed = gradient_sums(
+        peers, (lf, lgt, lg, lk, lv), (dsv, datt, dg, dk, dv), lh, dproj, matrices[4], matrices[5]
+    )
+    d_wf, d_wo, d_wg, d_wk, d_wv, d_wh, d_wp = (part[None] for part in summed)
 
     def row(index):
         return vec[index : index + 1]
@@ -823,9 +1175,9 @@
     return (
         out[None], back[None],
         row(0), row(1), row(2), row(3), row(4), row(5), row(6),
-        weight_grad(lk, dk), weight_grad(lv, dv), weight_grad(lg, dg), weight_grad(lgt, datt),
+        d_wk, d_wv, d_wg, d_wo,
         row(7), row(8), row(9), row(10),
-        weight_grad(lh, dh), weight_grad(sq, dproj), weight_grad(lf, dsv),
+        d_wh, d_wp, d_wf,
     )
 
 

time: 580 us -> 403 us (0.69)
  waiting for transfers between devices: 328 us -> 0 us
  Pallas kernels: 193 us -> 390 us
  matrix products: 22.9 us -> 0 us
  other arithmetic: 14.5 us -> 0 us
  between operations: 14.3 us -> 0.72 us
  local copies, waits for them, and re-layouts: 5.43 us -> 12 us
    reduce_scatter x7 -> x0, waiting for transfers between devices: 328 us -> none  [weight_grad(): lax.psum_scatter(local.astype(BF16), 'dp', scatter_dimension=0, tiled=True)]
    pallas_call x0 -> x1, Pallas kernels: none -> 106 us  [gradient_sums(): pl.pallas_call(partial(sum_kernel, peers), out_shape=(shape((share, width...]
    pallas_call x1, Pallas kernels: 193 us -> 284 us  [relay(): pl.pallas_call(partial(relay_kernel, sections, peers, split_vectors), out...]
    dot_general x7 -> x0, matrix products: 22.9 us -> none  [weight_grad(): lax.dot_general(left, right, (((0, 1), (0, 1)), ((), ())), preferred_elem...]
    broadcast_in_dim x7 -> x0, other arithmetic: 14.5 us -> none  [weight_grad(): return whole.astype(F32)[None]]
  transfers between devices with their start and end apart: 7 -> 0, of which waited for: 7 -> 0; matrix products, arithmetic and copies ran while one was open for 5% -> 0% of each run, Pallas kernels for 0% -> 0%
where the time goes in v2:
time: 403 us
  Pallas kernels  390 us (97%)
  local copies, waits for them, and re-layouts  12 us (3%)
    pallas_call x1, Pallas kernels, relay(): pl.pallas_call(partial(relay_kernel, sections, peers, split_vectors), out...  284 us
    pallas_call x1, Pallas kernels, gradient_sums(): pl.pallas_call(partial(sum_kernel, peers), out_shape=(shape((share, width...  106 us
    unnamed x25, local copies, waits for them, and re-layouts  10.5 us

profile of v2, /device:TPU:0, one launch (start us, length us, event | category | flops | bytes accessed | tf_op | source)
XLA Modules:
  0.0 402.7 jit_solution(5326356210341168288)
XLA Ops:
  0.7 283.8 %relay.1 = (bf16[2,128,1024]{2,1,0:T(8,128)(2,1)}, bf16[2,128,1024]{2,1,0:T(8,128)(2,1)}, f32[16,128]{1,0:T(8,128)}, bf16[2,128,1024]{2,1,0:T(8,128)(2,1)}, bf16...) custom-call(s32[2,5]{1,0:T(2,128)} %refs_0_.1, ...), custom_call_target="tpu_custom_call" | custom-call | tf_op jit(solution)/shard_map/relay/pallas_call | solution.py:790
  284.5 1.5 fusion
  286.0 106.1 %gradient_sums.1 = (f32[128,1024]{1,0:T(8,128)}, f32[128,1024]{1,0:T(8,128)}, f32[128,1024]{1,0:T(8,128)}, f32[128,1024]{1,0:T(8,128)}, f32[128,1024]{1,0:T(8,12...) custom-call(bf16[256,1024]{1,0:T(8,128)(2,1)} %bitcast.45, bf16[256,1024]{1,0:T(8,128)(2,1)} %bitcast.44, ...), custom_call_target="tpu_custom_call" | custom-call | tf_op jit(solution)/shard_map/gradient_sums/pallas_call | solution.py:1122
  392.2 0.0 copy-start.7
  392.2 0.0 copy-start.6
  392.2 0.0 copy-start.5
  392.2 2.0 copy.50
  394.2 0.0 copy-done.2
  394.2 0.0 copy-start.4
  394.2 0.8 copy.51
  395.0 0.0 copy-done.7
  395.0 0.8 copy.52
  395.8 0.0 copy-done.6
  395.8 0.8 copy.53
  396.6 0.0 copy-done.5
  396.6 0.8 copy.54
  397.4 0.0 copy-done.4
  397.4 0.8 copy.55
  398.2 0.0 copy-done.1
  398.2 1.3 copy.56
  399.5 1.0 copy-done
  400.5 1.3 copy.57
  401.8 0.1 copy-done.3
  401.9 0.8 copy.58
  (4 shorter events, 0.0 us)
Async XLA Ops:
  286.0 108.1 %copy-start.2 = (bf16[2,128,1024]{2,1,0:T(8,128)(2,1)S(1)}, bf16[2,128,1024]{2,1,0:T(8,128)(2,1)}, u32[]{:S(2)}) copy-start(bf16[2,128,1024]{2,1,0:T(8,128)(2,1)} %get-tuple-element.43) | copy-start | bytes 1572868
  392.2 2.8 copy-start.7
  392.2 3.6 copy-start.6
  392.2 4.4 %copy-start.5 = (f32[128,1024]{1,0:T(8,128)S(1)}, f32[128,1024]{1,0:T(8,128)}, u32[]{:S(2)}) copy-start(f32[128,1024]{1,0:T(8,128)} %get-tuple-element.59) | copy-start | bytes 1572868
  394.2 3.2 copy-start.4
  395.0 3.2 copy-start.1
  398.2 2.3 copy-start
  400.5 1.4 copy-start.3

commit v3 on v2

--- a/solution.py
+++ b/solution.py
@@ -9,7 +9,7 @@
 
 EPS = 1e-05
 MESH = pl.DeviceIdType.MESH
-RB = 32
+RB = 64
 VECTORS = 16
 F32 = jnp.float32
 BF16 = jnp.bfloat16
@@ -60,15 +60,15 @@
         spans, x_in, top_in,
         gain1, bias1, mix_k, mix_v, mix_g, log_rate, extra, gain2, bias2, mix_h, mix_f,
         wk_in, wv_in, wg_in, wo_in, wh_in, wp_in, wf_in,
-        out, back, vec_out, lk, lv, lg, lgt, lf, dk, dv, dg, datt, dsv, lh_all, dproj_all,
-        lh, sq, dproj, dh,
+        out, back, vec_out, lk, lv, lg, lgt, lf, dk, dv, dg, datt, dsv, dproj, lh_all,
+        lh, sq, dh,
         wk, wv, wg, wo, wh, wp, wf,
         xs, hx, dys, kk, vv, sg, sa, sb, mid, hmid, proj, sv, act, halo1, halo2,
         e0, e1, low_mask, up_mask, split, acc, t1, t2, t3,
         states, back_states, de2, de1, sum_row, sum_back, send_de2, send_de1, vg, vgs, vgr,
         w_sem, x_sem, top_sem, s_h0, s_x, s_hx, s_st, s_mid, s_dy, s_de2, s_bst, s_de1, s_vg,
         r_x, r_hx, r_st, r_mid, r_dy, r_de2, r_bst, r_de1, r_vg,
-        s_lh, r_lh, s_dp, r_dp, own_sem,
+        s_lh, r_lh, own_sem,
     ) = refs
     me_s = lax.axis_index("section")
     me = lax.axis_index("dp")
@@ -240,18 +240,13 @@
     chip, core = me // 2, me % 2
     chips = peers // 2
 
-    def gather_copy(which, m, k, slot):
-        source, target, send, receive = (
-            (lh, lh_all, s_lh, r_lh) if which == 0 else (dproj, dproj_all, s_dp, r_dp)
+    def gather_copy(m, k, slot):
+        return remote(
+            lh.at[m], lh_all.at[slot, m], s_lh.at[m, k], r_lh.at[m, slot], me_s, 2 * k + core
         )
-        return remote(
-            source.at[m], target.at[m, slot], send.at[m, k], receive.at[m, slot],
-            me_s, 2 * k + core,
-        )
-
-    def own_copy(which, m):
-        source, target = (lh, lh_all) if which == 0 else (dproj, dproj_all)
-        return pltpu.make_async_copy(source.at[m], target.at[m, chip], own_sem.at[which, m])
+
+    def own_copy(m):
+        return pltpu.make_async_copy(lh.at[m], lh_all.at[chip, m], own_sem.at[m])
 
     def each_chip(action):
         def turn(k, carry):
@@ -263,14 +258,22 @@
 
         lax.fori_loop(0, chips, turn, 0)
 
-    def start_gather(which, m):
-        own_copy(which, m).start()
-        each_chip(lambda k: gather_copy(which, m, k, chip).start())
-
-    def end_gather(which, m):
-        own_copy(which, m).wait()
-        each_chip(lambda k: gather_copy(which, m, k, chip).wait_send())
-        each_chip(lambda k: gather_copy(which, m, k, k).wait_recv())
+    def start_gather(m):
+        own_copy(m).start()
+        each_chip(lambda k: gather_copy(m, k, chip).start())
+
+    def start_gathers(early):
+        for m in range(batches):
+            in_gap = me_s + 1 + m < sections
+
+            @pl.when(in_gap if early else jnp.logical_not(in_gap))
+            def _(m=m):
+                start_gather(m)
+
+    def end_gather(m):
+        own_copy(m).wait()
+        each_chip(lambda k: gather_copy(m, k, chip).wait_send())
+        each_chip(lambda k: gather_copy(m, k, k).wait_recv())
 
     @pl.when((me_s == 0) & has_right)
     def _():
@@ -420,7 +423,6 @@
         halo_rows = halo_rows * gain2[...] + bias2[...]
         halo2[m] = halo_rows
         mix_second(0, halo_rows[7:8])
-        start_gather(0, m)
 
         @pl.when(m == 0)
         def _():
@@ -459,6 +461,7 @@
         return carry
 
     lax.fori_loop(0, batches, forward, 0)
+    start_gathers(True)
 
     def add_vector(index, value):
         vg[index] += fold(value)
@@ -485,7 +488,6 @@
             return carry
 
         lax.fori_loop(0, chunks, open_back, 0)
-        start_gather(1, m)
         t1[...] = jnp.zeros_like(t1)
 
         def narrow(j, carry):
@@ -690,6 +692,7 @@
         return carry
 
     lax.fori_loop(0, batches, backward, 0)
+    start_gathers(False)
 
     vgs[...] = jnp.sum(vg[...], axis=1)
     vgs[5:6] = vgs[5:6] * (-rate * jnp.exp(-rate))
@@ -758,8 +761,7 @@
             return carry
 
         lax.fori_loop(me + 1, peers, ended, 0)
-        end_gather(0, m)
-        end_gather(1, m)
+        end_gather(m)
 
         def ended_back(k, carry):
             back_state_copy(m, k, me).wait_send()
@@ -792,17 +794,16 @@
         out_shape=(
             low, low, shape((VECTORS, share), F32),
             low, low, low, low, low,
-            low, low, low, low, low,
-            shape((batches, peers // 2, rows, width), BF16),
-            shape((batches, peers // 2, rows, width), BF16),
+            low, low, low, low, low, low,
+            shape((peers // 2, batches, rows, width), BF16),
         ),
         in_specs=[pl.BlockSpec(memory_space=pltpu.SMEM), anywhere, anywhere]
         + [vmem] * 11
         + [anywhere] * 7,
-        out_specs=[vmem] * 13 + [anywhere] * 2,
+        out_specs=[vmem] * 14 + [anywhere],
         scratch_shapes=[
             narrow(BF16), pltpu.VMEM((batches, rows, hidden), BF16),
-            narrow(BF16), pltpu.VMEM((batches, rows, hidden), BF16),
+            pltpu.VMEM((batches, rows, hidden), BF16),
         ]
         + [pltpu.VMEM(matrix.shape, BF16) for matrix in matrices_order(matrices)]
         + [
@@ -826,8 +827,7 @@
             dma((batches,)), dma((batches,)), dma((batches, peers)), dma((batches,)), dma((peers,)),
             dma((batches,)), dma((batches,)), dma((batches, peers)), dma((batches,)),
             dma((batches,)), dma((batches,)), dma((batches, peers)), dma((batches,)), dma((peers,)),
-            dma((batches, peers // 2)), dma((batches, peers // 2)),
-            dma((batches, peers // 2)), dma((batches, peers // 2)), dma((2, batches)),
+            dma((batches, peers // 2)), dma((batches, peers // 2)), dma((batches,)),
         ],
         compiler_params=pltpu.CompilerParams(
             collective_id=0, has_side_effects=True, vmem_limit_bytes=63 * 2**20
@@ -850,6 +850,7 @@
         lh, dp, wh, wp, act, wide, hid_out, hid_in, proj_out, proj_in,
         left_sem, right_sem, lh_sem, dp_sem, wh_sem, wp_sem,
         s_pair, r_pair, s_right, r_right, s_left, r_left, s_hid, r_hid, s_proj, r_proj,
+        s_ahead, s_behind, r_rows,
     ) = refs[21:]
     count = len(left_in)
     me_s = lax.axis_index("section")
@@ -883,9 +884,11 @@
         pltpu.make_async_copy(left_in[w], lefts.at[w], left_sem.at[w]).start()
         pltpu.make_async_copy(right_in[w], rights.at[w], right_sem.at[w]).start()
     lh_copy = pltpu.make_async_copy(lh_in, lh, lh_sem)
-    dp_copy = pltpu.make_async_copy(dp_in, dp, dp_sem)
+    rows = dp_in.shape[0]
+    own_rows = pl.ds(pl.multiple_of(chip * rows, rows), rows)
+    dp_copy = pltpu.make_async_copy(dp_in, dp.at[own_rows], dp_sem)
+    dp_copy.start()
     lh_copy.start()
-    dp_copy.start()
 
     def wh_copy(j, slot):
         return pltpu.make_async_copy(
@@ -979,6 +982,28 @@
             ).astype(BF16)
             left_copy(slot, w, r).start()
 
+    def rows_copy(origin, send, index):
+        block = dp.at[pl.ds(pl.multiple_of(origin * rows, rows), rows)]
+        return remote(block, block, send.at[origin], r_rows.at[origin], index)
+
+    def each_origin(low, high):
+        def turn(origin, carry):
+            rows_copy(origin, s_ahead, after).wait_recv()
+            return carry
+
+        lax.fori_loop(low, high, turn, 0)
+
+    def spread(r):
+        @pl.when(has_right & (chip >= r))
+        def _():
+            pl.when(r > 0)(lambda: rows_copy(chip - r, s_ahead, after).wait_recv())
+            rows_copy(chip - r, s_ahead, after).start()
+
+        @pl.when(has_left & (from_end >= r))
+        def _():
+            pl.when(r > 0)(lambda: rows_copy(chip + r, s_behind, before).wait_recv())
+            rows_copy(chip + r, s_behind, before).start()
+
     def hid_copy(j):
         place = pl.ds(pl.multiple_of(j * columns, columns), columns)
         return remote(
@@ -998,7 +1023,8 @@
         @pl.when(j == 0)
         def _():
             lh_copy.wait()
-            dp_copy.wait()
+            pl.when(chip == 0)(lambda: each_origin(1, chips))
+            pl.when(from_end == 0)(lambda: each_origin(0, chips - 1))
 
         wh_copy(j, slot).wait()
         wp_copy(j, slot).wait()
@@ -1029,10 +1055,13 @@
             proj_out[...] = dot_tn(squared, dp[...]).astype(BF16)
             proj_copy.start()
 
+    rounds = chips - 1
+    dp_copy.wait()
+    spread(0)
     prepare(0)
     prepare(1)
     combine(0)
-    rounds = chips - 1
+    opening = count * rounds - peers
 
     def step(t, carry):
         w, r = t // rounds, t % rounds
@@ -1046,9 +1075,13 @@
         def _():
             combine(w + 1)
 
-        @pl.when((t % 2 == 0) & (t // 2 < peers))
-        def _():
-            feed(t // 2)
+        @pl.when(t + 1 < rounds)
+        def _():
+            spread(t + 1)
+
+        @pl.when(t >= opening)
+        def _():
+            feed(t - opening)
 
         return carry
 
@@ -1083,6 +1116,19 @@
 
     lax.fori_loop(0, peers, sent_hidden, 0)
     proj_copy.wait_send()
+
+    def sent_rows(origin, carry):
+        @pl.when(has_right & (origin <= chip))
+        def _():
+            rows_copy(origin, s_ahead, after).wait_send()
+
+        @pl.when(has_left & (origin >= chip))
+        def _():
+            rows_copy(origin, s_behind, before).wait_send()
+
+        return carry
+
+    lax.fori_loop(0, chips, sent_rows, 0)
 
     def sent(w, carry):
         pair_copy(w).wait_send()
@@ -1139,6 +1185,7 @@
             dma((count, chips - 1)), dma((count, chips - 1)),
             dma((count, chips - 1)), dma((count, chips - 1)),
             dma((peers,)), dma((peers,)), dma, dma,
+            dma((chips,)), dma((chips,)), dma((chips,)),
         ],
         compiler_params=pltpu.CompilerParams(
             collective_id=1, has_side_effects=True, vmem_limit_bytes=63 * 2**20
@@ -1159,8 +1206,10 @@
     found = relay(sections, peers, x, top, spans, vectors, matrices)
     out, back, vec = found[0:3]
     flat = (x.shape[0] * x.shape[1], x.shape[2])
-    lk, lv, lg, lgt, lf, dk, dv, dg, datt, dsv = (part.reshape(flat) for part in found[3:13])
-    lh, dproj = (part.reshape(-1, x.shape[2]) for part in found[13:15])
+    lk, lv, lg, lgt, lf, dk, dv, dg, datt, dsv, dproj = (
+        part.reshape(flat) for part in found[3:14]
+    )
+    lh = found[14].reshape(-1, x.shape[2])
     share = x.shape[2] // peers
     if vec.shape[1] != share:
         vec = lax.dynamic_slice_in_dim(vec, lax.axis_index("dp") * share, share, 1)

time: 403 us -> 316 us (0.78)
  Pallas kernels: 390 us -> 303 us
    pallas_call x1, Pallas kernels: 284 us -> 194 us  [relay(): pl.pallas_call(partial(relay_kernel, sections, peers, split_vectors), out...]
where the time goes in v3:
time: 316 us
  Pallas kernels  303 us (96%)
  local copies, waits for them, and re-layouts  12 us (4%)
    pallas_call x1, Pallas kernels, relay(): pl.pallas_call(partial(relay_kernel, sections, peers, split_vectors), out...  194 us
    pallas_call x1, Pallas kernels, gradient_sums(): pl.pallas_call(partial(sum_kernel, peers), out_shape=(shape((share, width...  109 us
    unnamed x25, local copies, waits for them, and re-layouts  10.5 us

profile of v3, /device:TPU:0, one launch (start us, length us, event | category | flops | bytes accessed | tf_op | source)
XLA Modules:
  0.0 315.5 jit_solution(12997656301853215542)
XLA Ops:
  0.7 193.8 %relay.1 = (bf16[2,128,1024]{2,1,0:T(8,128)(2,1)}, bf16[2,128,1024]{2,1,0:T(8,128)(2,1)}, f32[16,128]{1,0:T(8,128)}, bf16[2,128,1024]{2,1,0:T(8,128)(2,1)}, bf16...) custom-call(s32[2,5]{1,0:T(2,128)} %refs_0_.1, ...), custom_call_target="tpu_custom_call" | custom-call | tf_op jit(solution)/shard_map/relay/pallas_call | solution.py:792
  194.4 1.5 fusion
  196.0 0.0 copy-start.2
  196.0 109.0 %gradient_sums.1 = (f32[128,1024]{1,0:T(8,128)}, f32[128,1024]{1,0:T(8,128)}, f32[128,1024]{1,0:T(8,128)}, f32[128,1024]{1,0:T(8,128)}, f32[128,1024]{1,0:T(8,12...) custom-call(bf16[256,1024]{1,0:T(8,128)(2,1)} %bitcast.44, bf16[256,1024]{1,0:T(8,128)(2,1)} %bitcast.43, ...), custom_call_target="tpu_custom_call" | custom-call | tf_op jit(solution)/shard_map/gradient_sums/pallas_call | solution.py:1168
  305.0 0.0 copy-start.7
  305.0 0.0 copy-start.6
  305.0 0.0 copy-start.5
  305.0 2.0 copy.50
  307.0 0.0 copy-done.2
  307.0 0.8 copy.51
  307.8 0.0 copy-done.7
  307.8 0.8 copy.52
  308.6 0.0 copy-done.6
  308.6 0.8 copy.53
  309.4 0.0 copy-done.5
  309.4 0.8 copy.54
  310.2 0.0 copy-done.4
  310.2 0.8 copy.55
  311.0 0.0 copy-done.1
  311.0 1.3 copy.56
  312.3 1.0 copy-done
  313.3 1.3 copy.57
  314.7 0.1 copy-done.3
  314.7 0.8 copy.58
  (4 shorter events, 0.0 us)
Async XLA Ops:
  196.0 111.0 %copy-start.2 = (bf16[2,128,1024]{2,1,0:T(8,128)(2,1)S(1)}, bf16[2,128,1024]{2,1,0:T(8,128)(2,1)}, u32[]{:S(2)}) copy-start(bf16[2,128,1024]{2,1,0:T(8,128)(2,1)} %get-tuple-element.43) | copy-start | bytes 1572868
  305.0 2.8 copy-start.7
  305.0 3.6 %copy-start.6 = (f32[128,1024]{1,0:T(8,128)S(1)}, f32[128,1024]{1,0:T(8,128)}, u32[]{:S(2)}) copy-start(f32[128,1024]{1,0:T(8,128)} %get-tuple-element.58) | copy-start | bytes 1572868
  305.0 4.4 %copy-start.5 = (f32[128,1024]{1,0:T(8,128)S(1)}, f32[128,1024]{1,0:T(8,128)}, u32[]{:S(2)}) copy-start(f32[128,1024]{1,0:T(8,128)} %get-tuple-element.59) | copy-start | bytes 1572868
  307.0 3.2 %copy-start.4 = (f32[128,1024]{1,0:T(8,128)S(1)}, f32[128,1024]{1,0:T(8,128)}, u32[]{:S(2)}) copy-start(f32[128,1024]{1,0:T(8,128)} %get-tuple-element.60) | copy-start | bytes 1572868
  307.8 3.2 %copy-start.1 = (f32[128,4096]{1,0:T(8,128)S(1)}, f32[128,4096]{1,0:T(8,128)}, u32[]{:S(2)}) copy-start(f32[128,4096]{1,0:T(8,128)} %get-tuple-element.61) | copy-start | bytes 6291460
  311.0 2.3 copy-start
  313.3 1.4 copy-start.3

commit v4 on v3

--- a/solution.py
+++ b/solution.py
@@ -10,6 +10,7 @@
 EPS = 1e-05
 MESH = pl.DeviceIdType.MESH
 RB = 64
+PARTS = 1
 VECTORS = 16
 F32 = jnp.float32
 BF16 = jnp.bfloat16
@@ -61,14 +62,15 @@
         gain1, bias1, mix_k, mix_v, mix_g, log_rate, extra, gain2, bias2, mix_h, mix_f,
         wk_in, wv_in, wg_in, wo_in, wh_in, wp_in, wf_in,
         out, back, vec_out, lk, lv, lg, lgt, lf, dk, dv, dg, datt, dsv, dproj, lh_all,
-        lh, sq, dh,
+        wk_t, wv_t, wg_t, wo_t, wf_t, wp_t, wh_t,
+        lh, sq, dh, turned,
         wk, wv, wg, wo, wh, wp, wf,
         xs, hx, dys, kk, vv, sg, sa, sb, mid, hmid, proj, sv, act, halo1, halo2,
         e0, e1, low_mask, up_mask, split, acc, t1, t2, t3,
         states, back_states, de2, de1, sum_row, sum_back, send_de2, send_de1, vg, vgs, vgr,
         w_sem, x_sem, top_sem, s_h0, s_x, s_hx, s_st, s_mid, s_dy, s_de2, s_bst, s_de1, s_vg,
         r_x, r_hx, r_st, r_mid, r_dy, r_de2, r_bst, r_de1, r_vg,
-        s_lh, r_lh, own_sem,
+        s_lh, r_lh, own_sem, turn_sem, back_sem,
     ) = refs
     me_s = lax.axis_index("section")
     me = lax.axis_index("dp")
@@ -211,8 +213,21 @@
     def start_halo(m):
         return remote(x_in.at[m, tail], hx.at[m], s_h0.at[m], r_hx.at[m], me_s, right)
 
-    def result_copy(m):
-        return remote(out.at[m], xs.at[m], s_x.at[m], r_x.at[m], above, me)
+    def part_of(j):
+        return pl.ds(pl.multiple_of(j * (width // PARTS), width // PARTS), width // PARTS)
+
+    def result_copy(m, j):
+        return remote(
+            out.at[m, :, part_of(j)], xs.at[m, :, part_of(j)],
+            s_x.at[m, j], r_x.at[m, j], above, me,
+        )
+
+    def each_part(action):
+        def turn(j, carry):
+            action(j)
+            return carry
+
+        lax.fori_loop(0, PARTS, turn, 0)
 
     def result_halo(m):
         return remote(out.at[m, tail], hx.at[m], s_hx.at[m], r_hx.at[m], above, right)
@@ -223,8 +238,18 @@
     def state_copy(m, k, slot):
         return remote(sum_row.at[m], states.at[m, slot], s_st.at[m, k], r_st.at[m, slot], me_s, k)
 
-    def back_copy(m):
-        return remote(back.at[m], dys.at[m], s_dy.at[m], r_dy.at[m], below, me)
+    def back_copy(m, i):
+        rows = pl.ds(pl.multiple_of(i * RB, RB), RB)
+        return remote(
+            back.at[m, rows], dys.at[m, rows], s_dy.at[m, i], r_dy.at[m, i], below, me
+        )
+
+    def each_chunk(action):
+        def turn(i, carry):
+            action(i)
+            return carry
+
+        lax.fori_loop(0, chunks, turn, 0)
 
     def second_copy(m):
         return remote(send_de2.at[m], de2.at[m], s_de2.at[m], r_de2.at[m], me_s, left)
@@ -284,6 +309,58 @@
     def _():
         pltpu.make_async_copy(x_in, xs, x_sem).wait()
 
+    turns = (
+        (wk, wk_t), (wv, wv_t), (wg, wg_t), (wo, wo_t), (wf, wf_t), (wh, wh_t), (wp, wp_t)
+    )
+    returns = (
+        (wk_t, wk), (wv_t, wv), (wg_t, wg), (wo_t, wo), (wf_t, wf), (wp_t, wh), (wh_t, wp)
+    )
+    edge = turned.shape[1]
+
+    def transpose_all(fresh):
+        for index, (source, target) in enumerate(turns):
+            if fresh:
+                weight_copies[index].wait()
+            tall = source.shape[0] // edge
+            blocks = tall * (source.shape[1] // edge)
+
+            def place(n, source=source, target=target, tall=tall):
+                down = pl.ds(pl.multiple_of(n % tall * edge, edge), edge)
+                along = pl.ds(pl.multiple_of(n // tall * edge, edge), edge)
+                slot = n % 2
+                return (
+                    source.at[down, along],
+                    turned.at[slot],
+                    pltpu.make_async_copy(turned.at[slot], target.at[along, down], turn_sem.at[slot]),
+                )
+
+            def turn(n, carry, place=place):
+                piece, buffer, copy = place(n)
+                pl.when(n >= 2)(copy.wait)
+                buffer[...] = piece[...].T
+                copy.start()
+                return carry
+
+            lax.fori_loop(0, blocks, turn, 0)
+            for n in range(blocks - 2, blocks):
+                place(n)[2].wait()
+
+    def return_copy(index):
+        source, target = returns[index]
+        return pltpu.make_async_copy(source, target, back_sem.at[index])
+
+    is_late = 2 * me_s >= sections
+
+    def release(m, index):
+        @pl.when(is_late & (m == batches - 1))
+        def _():
+            return_copy(index).start()
+
+    def weight_ready(m, index, fresh=True):
+        @pl.when((m == 0) & jnp.logical_not(is_late))
+        def _():
+            weight_copies[index].wait()
+
     def span_of(i):
         return pl.ds(pl.multiple_of(i * RB, RB), RB)
 
@@ -292,7 +369,7 @@
 
         @pl.when(has_prior)
         def _():
-            result_copy(m).wait_recv()
+            each_part(lambda j: result_copy(m, j).wait_recv())
 
         @pl.when(has_left)
         def _():
@@ -315,13 +392,12 @@
 
         lax.fori_loop(0, chunks, mix_in, halo_rows[15:16])
 
-        @pl.when(m == 0)
-        def _():
-            for copy in weight_copies[0:2]:
-                copy.wait()
-
+        weight_ready(m, 0)
+        weight_ready(m, 1)
         kk[m] = dot_nn(lk[m], wk[...])
+        release(m, 0)
         vv[m] = dot_nn(lv[m], wv[...])
+        release(m, 1)
         end_segment = segment(base + row_count - 1, starts)
 
         def spread_in(i, totals):
@@ -352,11 +428,9 @@
 
         lax.fori_loop(me + 1, peers, send_state, 0)
 
-        @pl.when(m == 0)
-        def _():
-            weight_copies[2].wait()
-
+        weight_ready(m, 2)
         sg[m] = dot_nn(lg[m], wg[...])
+        release(m, 2)
         acc[...] = dot_nn(low_mask[m], split[...])
 
         def receive_state(k, held):
@@ -393,11 +467,9 @@
 
         lax.fori_loop(0, chunks, mix_states, 0)
 
-        @pl.when(m == 0)
-        def _():
-            weight_copies[3].wait()
-
+        weight_ready(m, 3)
         mid[m] = xs[m].astype(F32) + dot_nn(lgt[m], wo[...])
+        release(m, 3)
 
         @pl.when(has_right)
         def _():
@@ -424,12 +496,10 @@
         halo2[m] = halo_rows
         mix_second(0, halo_rows[7:8])
 
-        @pl.when(m == 0)
-        def _():
-            for copy in weight_copies[4:7]:
-                copy.wait()
-
+        for index in range(4, 7):
+            weight_ready(m, index)
         sv[m] = dot_nn(lf[m], wf[...])
+        release(m, 4)
 
         def widen(j, carry):
             columns = pl.ds(pl.multiple_of(j * width, width), width)
@@ -439,20 +509,24 @@
             return carry
 
         lax.fori_loop(0, hidden // width, widen, 0)
-        proj[m] = dot_nn(sq[m], wp[...])
-
-        def finish(i, carry):
-            rows = span_of(i)
-            sieve = sigmoid(sv[m, rows, :])
-            sv[m, rows, :] = sieve
-            out[m, rows, :] = (mid[m, rows, :] + sieve * proj[m, rows, :]).astype(BF16)
-            return carry
-
-        lax.fori_loop(0, chunks, finish, 0)
-
-        @pl.when(has_next)
-        def _():
-            result_copy(m).start()
+        release(m, 5)
+
+        def finish(j, carry):
+            columns = part_of(j)
+            found = dot_nn(sq[m], wp[:, columns])
+            proj[m, :, columns] = found
+            sieve = sigmoid(sv[m, :, columns])
+            sv[m, :, columns] = sieve
+            out[m, :, columns] = (mid[m, :, columns] + sieve * found).astype(BF16)
+
+            @pl.when(has_next)
+            def _():
+                result_copy(m, j).start()
+
+            return carry
+
+        lax.fori_loop(0, PARTS, finish, 0)
+        release(m, 6)
 
         @pl.when(has_next & has_right)
         def _():
@@ -460,7 +534,15 @@
 
         return carry
 
+    pl.when(is_late)(lambda: transpose_all(True))
     lax.fori_loop(0, batches, forward, 0)
+
+    @pl.when(jnp.logical_not(is_late))
+    def _():
+        transpose_all(False)
+        for index in range(7):
+            return_copy(index).start()
+
     start_gathers(True)
 
     def add_vector(index, value):
@@ -470,13 +552,18 @@
     def _():
         pltpu.make_async_copy(top_in, dys, top_sem).wait()
 
+    def turned_ready(m, index):
+        @pl.when(m == 0)
+        def _():
+            return_copy(index).wait()
+
     def backward(m, carry):
         starts = starts_of(m)
         none = jnp.zeros((1, width), F32)
 
         @pl.when(has_next)
         def _():
-            back_copy(m).wait_recv()
+            each_chunk(lambda i: back_copy(m, i).wait_recv())
 
         def open_back(i, carry):
             rows = span_of(i)
@@ -489,16 +576,19 @@
 
         lax.fori_loop(0, chunks, open_back, 0)
         t1[...] = jnp.zeros_like(t1)
+        turned_ready(m, 5)
+        turned_ready(m, 6)
 
         def narrow(j, carry):
             columns = pl.ds(pl.multiple_of(j * width, width), width)
-            grown = dot_nt(dproj[m], wp[columns, :])
+            grown = dot_nn(dproj[m], wh[:, columns])
             dh[m, :, columns] = (grown * 2.0 * act[m, :, columns].astype(F32)).astype(BF16)
-            t1[...] += dot_nt(dh[m, :, columns], wh[:, columns])
+            t1[...] += dot_nn(dh[m, :, columns], wp[columns, :])
             return carry
 
         lax.fori_loop(0, hidden // width, narrow, 0)
-        t2[...] = dot_nt(dsv[m], wf[...])
+        turned_ready(m, 4)
+        t2[...] = dot_nn(dsv[m], wf[...])
 
         def second_earlier(rows, position):
             whole = t1[rows, :] * (1.0 - mix_h[...]) + t2[rows, :] * (1.0 - mix_f[...])
@@ -549,7 +639,8 @@
             second_copy(m).wait_recv()
 
         back_second(chunks - 1, last, de2[m, 0:1])
-        t1[...] = dot_nt(datt[m], wo[...])
+        turned_ready(m, 3)
+        t1[...] = dot_nn(datt[m], wo[...])
         open_segment = segment(base, starts)
 
         def back_states_in(i, totals):
@@ -627,9 +718,11 @@
             return carry
 
         lax.fori_loop(0, chunks, back_keys, 0)
-        t1[...] = dot_nt(dk[m], wk[...])
-        t2[...] = dot_nt(dv[m], wv[...])
-        acc[:, 0:width] = dot_nt(dg[m], wg[...])
+        for index in range(3):
+            turned_ready(m, index)
+        t1[...] = dot_nn(dk[m], wk[...])
+        t2[...] = dot_nn(dv[m], wv[...])
+        acc[:, 0:width] = dot_nn(dg[m], wg[...])
 
         def first_earlier(rows, position):
             whole = (
@@ -667,6 +760,11 @@
             mean_two = jnp.mean(scaled * spare, axis=-1, keepdims=True)
             found = t3[rows, :] + spread * (scaled - mean_one - spare * mean_two)
             back[m, rows, :] = found.astype(BF16)
+
+            @pl.when(has_prior)
+            def _():
+                back_copy(m, i).start()
+
             return normed[RB - 1 : RB]
 
         def following_first(i):
@@ -685,13 +783,10 @@
 
         back_first(chunks - 1, last, de1[m, 0:1])
 
-        @pl.when(has_prior)
-        def _():
-            back_copy(m).start()
-
         return carry
 
     lax.fori_loop(0, batches, backward, 0)
+    pl.when(has_prior)(lambda: each_chunk(lambda i: back_copy(batches - 1, i).wait_send()))
     start_gathers(False)
 
     vgs[...] = jnp.sum(vg[...], axis=1)
@@ -737,7 +832,7 @@
 
         @pl.when(has_next)
         def _():
-            result_copy(m).wait_send()
+            each_part(lambda j: result_copy(m, j).wait_send())
 
         @pl.when(has_next & has_right)
         def _():
@@ -754,7 +849,7 @@
 
         @pl.when(has_prior)
         def _():
-            back_copy(m).wait_send()
+            pl.when(m + 1 < batches)(lambda: each_chunk(lambda i: back_copy(m, i).wait_send()))
 
         def ended(k, carry):
             state_copy(m, k, me).wait_send()
@@ -782,6 +877,7 @@
         share = width
     shape = jax.ShapeDtypeStruct
     low = shape((batches, rows, width), BF16)
+    square = shape((width, width), BF16)
     vmem = pl.BlockSpec(memory_space=pltpu.VMEM)
     anywhere = pl.BlockSpec(memory_space=pl.ANY)
     dma = pltpu.SemaphoreType.DMA
@@ -796,14 +892,16 @@
             low, low, low, low, low,
             low, low, low, low, low, low,
             shape((peers // 2, batches, rows, width), BF16),
+            square, square, square, square, square,
+            shape((width, hidden), BF16), shape((hidden, width), BF16),
         ),
         in_specs=[pl.BlockSpec(memory_space=pltpu.SMEM), anywhere, anywhere]
         + [vmem] * 11
         + [anywhere] * 7,
-        out_specs=[vmem] * 14 + [anywhere],
+        out_specs=[vmem] * 14 + [anywhere] * 8,
         scratch_shapes=[
             narrow(BF16), pltpu.VMEM((batches, rows, hidden), BF16),
-            pltpu.VMEM((batches, rows, hidden), BF16),
+            pltpu.VMEM((batches, rows, hidden), BF16), pltpu.VMEM((2, 512, 512), BF16),
         ]
         + [pltpu.VMEM(matrix.shape, BF16) for matrix in matrices_order(matrices)]
         + [
@@ -823,11 +921,14 @@
             pltpu.VMEM((VECTORS, 8, width), F32), pltpu.VMEM((VECTORS, width), F32),
             pltpu.VMEM((peers, VECTORS, share), F32),
             dma((7,)), dma, dma,
-            dma((batches,)), dma((batches,)), dma((batches,)), dma((batches, peers)), dma((batches,)),
-            dma((batches,)), dma((batches,)), dma((batches, peers)), dma((batches,)), dma((peers,)),
-            dma((batches,)), dma((batches,)), dma((batches, peers)), dma((batches,)),
-            dma((batches,)), dma((batches,)), dma((batches, peers)), dma((batches,)), dma((peers,)),
+            dma((batches,)), dma((batches, PARTS)), dma((batches,)), dma((batches, peers)),
+            dma((batches,)), dma((batches, rows // RB)), dma((batches,)), dma((batches, peers)),
+            dma((batches,)), dma((peers,)),
+            dma((batches, PARTS)), dma((batches,)), dma((batches, peers)), dma((batches,)),
+            dma((batches, rows // RB)), dma((batches,)), dma((batches, peers)), dma((batches,)),
+            dma((peers,)),
             dma((batches, peers // 2)), dma((batches, peers // 2)), dma((batches,)),
+            dma((2,)), dma((7,)),
         ],
         compiler_params=pltpu.CompilerParams(
             collective_id=0, has_side_effects=True, vmem_limit_bytes=63 * 2**20

time: 316 us -> 287 us (0.908)
  Pallas kernels: 303 us -> 274 us
    pallas_call x1, Pallas kernels: 194 us -> 165 us  [relay(): pl.pallas_call(partial(relay_kernel, sections, peers, split_vectors), out...]
where the time goes in v4:
time: 287 us
  Pallas kernels  274 us (95%)
  local copies, waits for them, and re-layouts  12 us (4%)
    pallas_call x1, Pallas kernels, relay(): pl.pallas_call(partial(relay_kernel, sections, peers, split_vectors), out...  165 us
    pallas_call x1, Pallas kernels, gradient_sums(): pl.pallas_call(partial(sum_kernel, peers), out_shape=(shape((share, width...  109 us
    unnamed x25, local copies, waits for them, and re-layouts  10.5 us

profile of v4, /device:TPU:0, one launch (start us, length us, event | category | flops | bytes accessed | tf_op | source)
XLA Modules:
  0.0 287.0 jit_solution(4424292944579206734)
XLA Ops:
  0.7 165.3 %relay.1 = (bf16[2,128,1024]{2,1,0:T(8,128)(2,1)}, bf16[2,128,1024]{2,1,0:T(8,128)(2,1)}, f32[16,128]{1,0:T(8,128)}, bf16[2,128,1024]{2,1,0:T(8,128)(2,1)}, bf16...) custom-call(s32[2,5]{1,0:T(2,128)} %refs_0_.1, ...), custom_call_target="tpu_custom_call" | custom-call | tf_op jit(solution)/shard_map/relay/pallas_call | solution.py:888
  166.0 1.5 fusion
  167.5 0.0 copy-start.2
  167.5 108.9 %gradient_sums.1 = (f32[128,1024]{1,0:T(8,128)}, f32[128,1024]{1,0:T(8,128)}, f32[128,1024]{1,0:T(8,128)}, f32[128,1024]{1,0:T(8,128)}, f32[128,1024]{1,0:T(8,12...) custom-call(bf16[256,1024]{1,0:T(8,128)(2,1)} %bitcast.44, bf16[256,1024]{1,0:T(8,128)(2,1)} %bitcast.43, ...), custom_call_target="tpu_custom_call" | custom-call | tf_op jit(solution)/shard_map/gradient_sums/pallas_call | solution.py:1269
  276.4 0.0 copy-start.7
  276.4 0.0 copy-start.6
  276.4 0.0 copy-start.5
  276.5 2.0 copy.50
  278.4 0.0 copy-done.2
  278.4 0.8 copy.51
  279.2 0.0 copy-done.7
  279.2 0.8 copy.52
  280.0 0.0 copy-done.6
  280.0 0.8 copy.53
  280.8 0.0 copy-done.5
  280.8 0.8 copy.54
  281.6 0.0 copy-done.4
  281.6 0.8 copy.55
  282.4 0.0 copy-done.1
  282.4 1.3 copy.56
  283.8 1.0 copy-done
  284.8 1.3 copy.57
  286.1 0.1 copy-done.3
  286.2 0.8 copy.58
  (4 shorter events, 0.0 us)
Async XLA Ops:
  167.5 111.0 %copy-start.2 = (bf16[2,128,1024]{2,1,0:T(8,128)(2,1)S(1)}, bf16[2,128,1024]{2,1,0:T(8,128)(2,1)}, u32[]{:S(2)}) copy-start(bf16[2,128,1024]{2,1,0:T(8,128)(2,1)} %get-tuple-element.43) | copy-start | bytes 1572868
  276.4 2.8 copy-start.7
  276.4 3.6 %copy-start.6 = (f32[128,1024]{1,0:T(8,128)S(1)}, f32[128,1024]{1,0:T(8,128)}, u32[]{:S(2)}) copy-start(f32[128,1024]{1,0:T(8,128)} %get-tuple-element.58) | copy-start | bytes 1572868
  276.4 4.4 %copy-start.5 = (f32[128,1024]{1,0:T(8,128)S(1)}, f32[128,1024]{1,0:T(8,128)}, u32[]{:S(2)}) copy-start(f32[128,1024]{1,0:T(8,128)} %get-tuple-element.59) | copy-start | bytes 1572868
  278.4 3.2 %copy-start.4 = (f32[128,1024]{1,0:T(8,128)S(1)}, f32[128,1024]{1,0:T(8,128)}, u32[]{:S(2)}) copy-start(f32[128,1024]{1,0:T(8,128)} %get-tuple-element.60) | copy-start | bytes 1572868
  279.2 3.2 %copy-start.1 = (f32[128,4096]{1,0:T(8,128)S(1)}, f32[128,4096]{1,0:T(8,128)}, u32[]{:S(2)}) copy-start(f32[128,4096]{1,0:T(8,128)} %get-tuple-element.61) | copy-start | bytes 6291460
  282.4 2.3 copy-start
  284.8 1.4 copy-start.3

commit v5 on v4

--- a/solution.py
+++ b/solution.py
@@ -56,20 +56,22 @@
     return total
 
 
-def relay_kernel(sections, peers, split_vectors, *refs):
+def relay_kernel(sections, peers, *refs):
     (
         spans, x_in, top_in,
         gain1, bias1, mix_k, mix_v, mix_g, log_rate, extra, gain2, bias2, mix_h, mix_f,
         wk_in, wv_in, wg_in, wo_in, wh_in, wp_in, wf_in,
-        out, back, vec_out, lk, lv, lg, lgt, lf, dk, dv, dg, datt, dsv, dproj, lh_all,
+        out_hbm, back_hbm, lk_hbm, lv_hbm, lg_hbm, lgt_hbm, lf_hbm,
+        dk_hbm, dv_hbm, dg_hbm, datt_hbm, dsv_hbm, dproj_hbm, vgs, lh_all,
         wk_t, wv_t, wg_t, wo_t, wf_t, wp_t, wh_t,
+        out, back, lk, lv, lg, lgt, lf, dk, dv, dg, datt, dsv, dproj,
         lh, sq, dh, turned,
         wk, wv, wg, wo, wh, wp, wf,
         xs, hx, dys, kk, vv, sg, sa, sb, mid, hmid, proj, sv, act, halo1, halo2,
         e0, e1, low_mask, up_mask, split, acc, t1, t2, t3,
-        states, back_states, de2, de1, sum_row, sum_back, send_de2, send_de1, vg, vgs, vgr,
-        w_sem, x_sem, top_sem, s_h0, s_x, s_hx, s_st, s_mid, s_dy, s_de2, s_bst, s_de1, s_vg,
-        r_x, r_hx, r_st, r_mid, r_dy, r_de2, r_bst, r_de1, r_vg,
+        states, back_states, de2, de1, sum_row, sum_back, send_de2, send_de1, vg,
+        w_sem, x_sem, top_sem, s_h0, s_x, s_hx, s_st, s_mid, s_dy, s_de2, s_bst, s_de1,
+        r_x, r_hx, r_st, r_mid, r_dy, r_de2, r_bst, r_de1, store_sem,
         s_lh, r_lh, own_sem, turn_sem, back_sem,
     ) = refs
     me_s = lax.axis_index("section")
@@ -127,7 +129,7 @@
     def _():
         pltpu.make_async_copy(x_in, xs, x_sem).start()
 
-    for copy in weight_copies:
+    for copy in weight_copies[0:2]:
         copy.start()
 
     @pl.when(me_s == sections - 1)
@@ -137,6 +139,20 @@
     rate = jnp.exp(log_rate[...])
     decay_block = jnp.exp(-rate * row_count)
     grow_block = jnp.exp(rate * row_count)
+
+    half = width // 128
+
+    def packed(row_a, row_b):
+        return jnp.concatenate(
+            [row[:, j * 128 : (j + 1) * 128] for row in (row_a, row_b) for j in range(half)], axis=0
+        )
+
+    def unpacked(tile, part):
+        return jnp.concatenate(
+            [tile[part * half + j : part * half + j + 1] for j in range(half)], axis=1
+        )
+
+    decay_tile = packed(decay_block, decay_block)
 
     def starts_of(m):
         found = []
@@ -196,6 +212,8 @@
         + jnp.where(has_prior & has_left, 1, 0)
     )
     pl.semaphore_wait(barrier, greeted)
+    for copy in weight_copies[2:7]:
+        copy.start()
 
     def remote(source, target, send, receive, section, index):
         return pltpu.make_async_remote_copy(
@@ -208,7 +226,17 @@
     above = jnp.minimum(me_s + 1, sections - 1)
     below = jnp.maximum(me_s - 1, 0)
     tail = pl.ds(row_count - 16, 16)
-    tail8 = pl.ds(row_count - 8, 8)
+    final = pl.ds(row_count - 1, 1)
+
+    stored = (
+        (out, out_hbm), (lk, lk_hbm), (lv, lv_hbm), (lg, lg_hbm), (lgt, lgt_hbm), (lf, lf_hbm),
+        (dproj, dproj_hbm), (dsv, dsv_hbm), (datt, datt_hbm), (dg, dg_hbm), (dk, dk_hbm),
+        (dv, dv_hbm), (back, back_hbm),
+    )
+
+    def store_copy(index, m):
+        source, target = stored[index]
+        return pltpu.make_async_copy(source.at[m], target.at[m], store_sem.at[index, m])
 
     def start_halo(m):
         return remote(x_in.at[m, tail], hx.at[m], s_h0.at[m], r_hx.at[m], me_s, right)
@@ -233,7 +261,7 @@
         return remote(out.at[m, tail], hx.at[m], s_hx.at[m], r_hx.at[m], above, right)
 
     def middle_halo(m):
-        return remote(mid.at[m, tail8], hmid.at[m], s_mid.at[m], r_mid.at[m], me_s, right)
+        return remote(mid.at[m, final], hmid.at[m], s_mid.at[m], r_mid.at[m], me_s, right)
 
     def state_copy(m, k, slot):
         return remote(sum_row.at[m], states.at[m, slot], s_st.at[m, k], r_st.at[m, slot], me_s, k)
@@ -390,13 +418,13 @@
             lg[m, rows, :] = (earlier + gap * mix_g[...]).astype(BF16)
             return normed[RB - 1 : RB]
 
-        lax.fori_loop(0, chunks, mix_in, halo_rows[15:16])
+        lax.fori_loop(0, chunks, mix_in, halo_rows[15:16], unroll=True)
 
         weight_ready(m, 0)
         weight_ready(m, 1)
         kk[m] = dot_nn(lk[m], wk[...])
+        vv[m] = dot_nn(lv[m], wv[...])
         release(m, 0)
-        vv[m] = dot_nn(lv[m], wv[...])
         release(m, 1)
         end_segment = segment(base + row_count - 1, starts)
 
@@ -418,9 +446,10 @@
             )
 
         nothing = jnp.zeros((8, width), F32)
-        total_a, total_b = lax.fori_loop(0, chunks, spread_in, (nothing, nothing))
-        sum_row[m, 0:1] = jnp.sum(total_a, axis=0, keepdims=True)
-        sum_row[m, 1:2] = jnp.sum(total_b, axis=0, keepdims=True)
+        total_a, total_b = lax.fori_loop(0, chunks, spread_in, (nothing, nothing), unroll=True)
+        sum_row[m] = packed(
+            jnp.sum(total_a, axis=0, keepdims=True), jnp.sum(total_b, axis=0, keepdims=True)
+        )
 
         def send_state(k, carry):
             state_copy(m, k, me).start()
@@ -430,22 +459,20 @@
 
         weight_ready(m, 2)
         sg[m] = dot_nn(lg[m], wg[...])
+        acc[...] = dot_nn(low_mask[m], split[...])
         release(m, 2)
-        acc[...] = dot_nn(low_mask[m], split[...])
 
         def receive_state(k, held):
             state_copy(m, k, k).wait_recv()
             unbroken = segment(k * row_count - 1, starts) == segment(
                 (k + 1) * row_count - 1, starts
             )
-            passing = jnp.where(unbroken, 1.0, 0.0) * decay_block
-            return (
-                passing * held[0] + states[m, k, 0:1],
-                passing * held[1] + states[m, k, 1:2],
-            )
+            passing = jnp.where(unbroken, 1.0, 0.0) * decay_tile
+            return passing * held + states[m, k]
 
         none = jnp.zeros((1, width), F32)
-        enter_a, enter_b = lax.fori_loop(0, me, receive_state, (none, none))
+        entered = lax.fori_loop(0, me, receive_state, jnp.zeros_like(decay_tile))
+        enter_a, enter_b = unpacked(entered, 0), unpacked(entered, 1)
         prior_segment = segment(base - 1, starts)
 
         def mix_states(i, carry):
@@ -465,7 +492,7 @@
             lgt[m, rows, :] = (gate * found).astype(BF16)
             return carry
 
-        lax.fori_loop(0, chunks, mix_states, 0)
+        lax.fori_loop(0, chunks, mix_states, 0, unroll=True)
 
         weight_ready(m, 3)
         mid[m] = xs[m].astype(F32) + dot_nn(lgt[m], wo[...])
@@ -485,7 +512,7 @@
             lf[m, rows, :] = (earlier + gap * mix_f[...]).astype(BF16)
             return normed[RB - 1 : RB]
 
-        lax.fori_loop(0, chunks, mix_second, none)
+        lax.fori_loop(0, chunks, mix_second, none, unroll=True)
 
         @pl.when(has_left)
         def _():
@@ -494,12 +521,11 @@
         halo_rows, _ = normalise(hmid[m])
         halo_rows = halo_rows * gain2[...] + bias2[...]
         halo2[m] = halo_rows
-        mix_second(0, halo_rows[7:8])
+        mix_second(0, halo_rows)
 
         for index in range(4, 7):
             weight_ready(m, index)
         sv[m] = dot_nn(lf[m], wf[...])
-        release(m, 4)
 
         def widen(j, carry):
             columns = pl.ds(pl.multiple_of(j * width, width), width)
@@ -508,7 +534,8 @@
             sq[m, :, columns] = (active * active).astype(BF16)
             return carry
 
-        lax.fori_loop(0, hidden // width, widen, 0)
+        lax.fori_loop(0, hidden // width, widen, 0, unroll=True)
+        release(m, 4)
         release(m, 5)
 
         def finish(j, carry):
@@ -532,6 +559,9 @@
         def _():
             result_halo(m).start()
 
+        for index in range(6):
+            store_copy(index, m).start()
+
         return carry
 
     pl.when(is_late)(lambda: transpose_all(True))
@@ -574,7 +604,7 @@
             dsv[m, rows, :] = (gained * proj[m, rows, :] * (1.0 - sieve)).astype(BF16)
             return carry
 
-        lax.fori_loop(0, chunks, open_back, 0)
+        lax.fori_loop(0, chunks, open_back, 0, unroll=True)
         t1[...] = jnp.zeros_like(t1)
         turned_ready(m, 5)
         turned_ready(m, 6)
@@ -586,7 +616,7 @@
             t1[...] += dot_nn(dh[m, :, columns], wp[columns, :])
             return carry
 
-        lax.fori_loop(0, hidden // width, narrow, 0)
+        lax.fori_loop(0, hidden // width, narrow, 0, unroll=True)
         turned_ready(m, 4)
         t2[...] = dot_nn(dsv[m], wf[...])
 
@@ -595,7 +625,7 @@
             return whole * keep_of(position, starts)
 
         eight = lax.broadcasted_iota(jnp.int32, (8, 1), 0)
-        send_de2[m] = second_earlier(pl.ds(0, 8), base + eight)
+        send_de2[m] = second_earlier(pl.ds(0, 8), base + eight)[0:1]
 
         @pl.when(has_left)
         def _():
@@ -628,17 +658,15 @@
             start = pl.multiple_of((i + 1) * RB, RB)
             return second_earlier(pl.ds(start, 8), base + start + eight)[0:1]
 
-        last = lax.fori_loop(
-            0, chunks - 1,
-            lambda i, last: back_second(i, last, following_second(i)),
-            halo2[m, 7:8],
-        )
+        last = halo2[m]
+        for i in range(chunks - 1):
+            last = back_second(i, last, following_second(i))
 
         @pl.when(has_right)
         def _():
             second_copy(m).wait_recv()
 
-        back_second(chunks - 1, last, de2[m, 0:1])
+        back_second(chunks - 1, last, de2[m])
         turned_ready(m, 3)
         t1[...] = dot_nn(datt[m], wo[...])
         open_segment = segment(base, starts)
@@ -677,9 +705,10 @@
             )
 
         nothing = jnp.zeros((8, width), F32)
-        total_a, total_b = lax.fori_loop(0, chunks, back_states_in, (nothing, nothing))
-        sum_back[m, 0:1] = jnp.sum(total_a, axis=0, keepdims=True)
-        sum_back[m, 1:2] = jnp.sum(total_b, axis=0, keepdims=True)
+        total_a, total_b = lax.fori_loop(0, chunks, back_states_in, (nothing, nothing), unroll=True)
+        sum_back[m] = packed(
+            jnp.sum(total_a, axis=0, keepdims=True), jnp.sum(total_b, axis=0, keepdims=True)
+        )
 
         def send_state(k, carry):
             back_state_copy(m, k, me).start()
@@ -694,13 +723,11 @@
             first = segment(k * row_count, starts)
             unbroken = first == segment((k + 1) * row_count - 1, starts)
             joined = jnp.where(first == segment(k * row_count - 1, starts), 1.0, 0.0)
-            passing = jnp.where(unbroken, 1.0, 0.0) * decay_block
-            return (
-                joined * (passing * held[0] + back_states[m, k, 0:1]),
-                joined * (passing * held[1] + back_states[m, k, 1:2]),
-            )
-
-        enter_a, enter_b = lax.fori_loop(0, peers - 1 - me, receive_state, (none, none))
+            passing = jnp.where(unbroken, 1.0, 0.0) * decay_tile
+            return joined * (passing * held + back_states[m, k])
+
+        entered = lax.fori_loop(0, peers - 1 - me, receive_state, jnp.zeros_like(decay_tile))
+        enter_a, enter_b = unpacked(entered, 0), unpacked(entered, 1)
         end_segment = segment(base + row_count - 1, starts)
 
         def back_keys(i, carry):
@@ -717,7 +744,7 @@
             dk[m, rows, :] = (t1[rows, :] + (d_a * vv[m, rows, :] + d_b) * weight).astype(BF16)
             return carry
 
-        lax.fori_loop(0, chunks, back_keys, 0)
+        lax.fori_loop(0, chunks, back_keys, 0, unroll=True)
         for index in range(3):
             turned_ready(m, index)
         t1[...] = dot_nn(dk[m], wk[...])
@@ -732,11 +759,14 @@
             )
             return whole * keep_of(position, starts)
 
-        send_de1[m] = first_earlier(pl.ds(0, 8), base + eight)
+        send_de1[m] = first_earlier(pl.ds(0, 8), base + eight)[0:1]
 
         @pl.when(has_left)
         def _():
             first_copy(m).start()
+
+        for index in range(6, 12):
+            store_copy(index, m).start()
 
         def back_first(i, last, following):
             rows = span_of(i)
@@ -771,17 +801,16 @@
             start = pl.multiple_of((i + 1) * RB, RB)
             return first_earlier(pl.ds(start, 8), base + start + eight)[0:1]
 
-        last = lax.fori_loop(
-            0, chunks - 1,
-            lambda i, last: back_first(i, last, following_first(i)),
-            halo1[m, 7:8],
-        )
+        last = halo1[m, 7:8]
+        for i in range(chunks - 1):
+            last = back_first(i, last, following_first(i))
 
         @pl.when(has_right)
         def _():
             first_copy(m).wait_recv()
 
-        back_first(chunks - 1, last, de1[m, 0:1])
+        back_first(chunks - 1, last, de1[m])
+        store_copy(12, m).start()
 
         return carry
 
@@ -791,40 +820,6 @@
 
     vgs[...] = jnp.sum(vg[...], axis=1)
     vgs[5:6] = vgs[5:6] * (-rate * jnp.exp(-rate))
-    share = vgr.shape[2]
-
-    def part(k):
-        if split_vectors:
-            return vgs.at[:, pl.ds(pl.multiple_of(k * share, share), share)]
-        return vgs
-
-    def vector_copy(k, slot):
-        return remote(part(k), vgr.at[slot], s_vg.at[k], r_vg.at[slot], me_s, k)
-
-    def each_peer(action):
-        def turn(k, carry):
-            @pl.when(k != me)
-            def _():
-                action(k)
-
-            return carry
-
-        lax.fori_loop(0, peers, turn, 0)
-
-    each_peer(lambda k: vector_copy(k, me).start())
-    if split_vectors:
-        vec_out[...] = vgs[:, pl.ds(pl.multiple_of(me * share, share), share)]
-    else:
-        vec_out[...] = vgs[...]
-
-    def collect(k):
-        vector_copy(k, k).wait_recv()
-        vec_out[...] += vgr[k]
-
-    each_peer(collect)
-
-    each_peer(lambda k: vector_copy(k, me).wait_send())
-
     def close(m, carry):
         @pl.when((me_s == 0) & has_right)
         def _():
@@ -850,6 +845,9 @@
         @pl.when(has_prior)
         def _():
             pl.when(m + 1 < batches)(lambda: each_chunk(lambda i: back_copy(m, i).wait_send()))
+
+        for index in range(13):
+            store_copy(index, m).wait()
 
         def ended(k, carry):
             state_copy(m, k, me).wait_send()
@@ -871,10 +869,6 @@
 def relay(sections, peers, x, top, spans, vectors, matrices):
     batches, rows, width = x.shape
     hidden = matrices[4].shape[1]
-    share = width // peers
-    split_vectors = share % 128 == 0
-    if not split_vectors:
-        share = width
     shape = jax.ShapeDtypeStruct
     low = shape((batches, rows, width), BF16)
     square = shape((width, width), BF16)
@@ -886,11 +880,10 @@
         return pltpu.VMEM((batches, rows, width), kind)
 
     return pl.pallas_call(
-        partial(relay_kernel, sections, peers, split_vectors),
+        partial(relay_kernel, sections, peers),
         out_shape=(
-            low, low, shape((VECTORS, share), F32),
-            low, low, low, low, low,
-            low, low, low, low, low, low,
+            low, low, low, low, low, low, low,
+            low, low, low, low, low, low, shape((VECTORS, width), F32),
             shape((peers // 2, batches, rows, width), BF16),
             square, square, square, square, square,
             shape((width, hidden), BF16), shape((hidden, width), BF16),
@@ -898,8 +891,8 @@
         in_specs=[pl.BlockSpec(memory_space=pltpu.SMEM), anywhere, anywhere]
         + [vmem] * 11
         + [anywhere] * 7,
-        out_specs=[vmem] * 14 + [anywhere] * 8,
-        scratch_shapes=[
+        out_specs=[anywhere] * 13 + [vmem] + [anywhere] * 8,
+        scratch_shapes=[narrow(BF16)] * 13 + [
             narrow(BF16), pltpu.VMEM((batches, rows, hidden), BF16),
             pltpu.VMEM((batches, rows, hidden), BF16), pltpu.VMEM((2, 512, 512), BF16),
         ]
@@ -907,26 +900,27 @@
         + [
             narrow(BF16), pltpu.VMEM((batches, 16, width), BF16), narrow(BF16),
             narrow(F32), narrow(F32), narrow(F32), narrow(F32), narrow(F32), narrow(F32),
-            pltpu.VMEM((batches, 8, width), F32), narrow(F32), narrow(F32),
+            pltpu.VMEM((batches, 1, width), F32), narrow(F32), narrow(F32),
             pltpu.VMEM((batches, rows, hidden), BF16),
-            pltpu.VMEM((batches, 8, width), F32), pltpu.VMEM((batches, 8, width), F32),
+            pltpu.VMEM((batches, 8, width), F32), pltpu.VMEM((batches, 1, width), F32),
             pltpu.VMEM((rows, width), F32), pltpu.VMEM((rows, width), F32),
             pltpu.VMEM((batches, rows, 2 * rows), BF16), pltpu.VMEM((batches, rows, 2 * rows), BF16),
             pltpu.VMEM((2 * rows, 2 * width), BF16), pltpu.VMEM((rows, 2 * width), F32),
             pltpu.VMEM((rows, width), F32), pltpu.VMEM((rows, width), F32), pltpu.VMEM((rows, width), F32),
-            pltpu.VMEM((batches, peers, 2, width), F32), pltpu.VMEM((batches, peers, 2, width), F32),
-            pltpu.VMEM((batches, 8, width), F32), pltpu.VMEM((batches, 8, width), F32),
-            pltpu.VMEM((batches, 2, width), F32), pltpu.VMEM((batches, 2, width), F32),
-            pltpu.VMEM((batches, 8, width), F32), pltpu.VMEM((batches, 8, width), F32),
-            pltpu.VMEM((VECTORS, 8, width), F32), pltpu.VMEM((VECTORS, width), F32),
-            pltpu.VMEM((peers, VECTORS, share), F32),
+            pltpu.VMEM((batches, peers, width // 64, 128), F32),
+            pltpu.VMEM((batches, peers, width // 64, 128), F32),
+            pltpu.VMEM((batches, 1, width), F32), pltpu.VMEM((batches, 1, width), F32),
+            pltpu.VMEM((batches, width // 64, 128), F32),
+            pltpu.VMEM((batches, width // 64, 128), F32),
+            pltpu.VMEM((batches, 1, width), F32), pltpu.VMEM((batches, 1, width), F32),
+            pltpu.VMEM((VECTORS, 8, width), F32),
             dma((7,)), dma, dma,
             dma((batches,)), dma((batches, PARTS)), dma((batches,)), dma((batches, peers)),
             dma((batches,)), dma((batches, rows // RB)), dma((batches,)), dma((batches, peers)),
-            dma((batches,)), dma((peers,)),
+            dma((batches,)),
             dma((batches, PARTS)), dma((batches,)), dma((batches, peers)), dma((batches,)),
             dma((batches, rows // RB)), dma((batches,)), dma((batches, peers)), dma((batches,)),
-            dma((peers,)),
+            dma((13, batches)),
             dma((batches, peers // 2)), dma((batches, peers // 2)), dma((batches,)),
             dma((2,)), dma((7,)),
         ],
@@ -942,17 +936,18 @@
     return (wk, wv, wg, wo, wh, wp, wf)
 
 
-def sum_kernel(peers, *refs):
+def sum_kernel(peers, split_vectors, *refs):
     left_in, right_in = refs[0:5], refs[5:10]
-    lh_in, dp_in, wh_in, wp_in = refs[10:14]
-    outs, wh_out, wp_out = refs[14:19], refs[19], refs[20]
+    lh_in, dp_in, wh_in, wp_in, vgs = refs[10:15]
+    outs_hbm, wh_hbm, wp_hbm, vec_out = refs[15:19]
     (
         lefts, rights, whole, own, pair_out, going_right, going_left,
         lh, dp, wh, wp, act, wide, hid_out, hid_in, proj_out, proj_in,
         left_sem, right_sem, lh_sem, dp_sem, wh_sem, wp_sem,
         s_pair, r_pair, s_right, r_right, s_left, r_left, s_hid, r_hid, s_proj, r_proj,
         s_ahead, s_behind, r_rows,
-    ) = refs[21:]
+        outs, wh_out, wp_out, vgr, s_vg, r_vg, outs_sem, wh_out_sem, wp_out_sem,
+    ) = refs[19:]
     count = len(left_in)
     me_s = lax.axis_index("section")
     me = lax.axis_index("dp")
@@ -971,16 +966,17 @@
     def greet(index):
         pl.semaphore_signal(barrier, inc=1, device_id=(me_s, index), device_id_type=MESH)
 
-    greet(sibling)
-
-    @pl.when(has_right)
-    def _():
-        greet(after)
-
-    @pl.when(has_left)
-    def _():
-        greet(before)
-
+    def each_peer(action):
+        def turn(k, carry):
+            @pl.when(k != me)
+            def _():
+                action(k)
+
+            return carry
+
+        lax.fori_loop(0, peers, turn, 0)
+
+    each_peer(greet)
     for w in range(count):
         pltpu.make_async_copy(left_in[w], lefts.at[w], left_sem.at[w]).start()
         pltpu.make_async_copy(right_in[w], rights.at[w], right_sem.at[w]).start()
@@ -1005,10 +1001,6 @@
 
     wh_copy(0, 0).start()
     wp_copy(0, 0).start()
-    pl.semaphore_wait(
-        barrier, 1 + jnp.where(has_right, 1, 0) + jnp.where(has_left, 1, 0)
-    )
-
     def remote(source, target, send, receive, index):
         return pltpu.make_async_remote_copy(
             src_ref=source, dst_ref=target, send_sem=send, recv_sem=receive,
@@ -1018,6 +1010,12 @@
     def pair_copy(w):
         return remote(pair_out.at[w], own.at[w], s_pair.at[w], r_pair.at[w], sibling)
 
+    cut = vgr.shape[2]
+
+    def vector_copy(k, slot):
+        part = vgs.at[:, pl.ds(pl.multiple_of(k * cut, cut), cut)] if split_vectors else vgs
+        return remote(part, vgr.at[slot], s_vg.at[k], r_vg.at[slot], k)
+
     def rows_of(block, parity):
         return pl.ds(pl.multiple_of((2 * block + parity) * share, share), share)
 
@@ -1032,7 +1030,6 @@
             return carry
 
         lax.fori_loop(0, blocks, divide, 0)
-        pair_copy(w).start()
 
     def combine(w):
         slot = w % 2
@@ -1116,6 +1113,36 @@
     first = chip * 2 * share
     start = pl.multiple_of(first // group * group, group)
     inside = first - first // group * group
+
+    def hidden_store(j):
+        place = pl.ds(pl.multiple_of(j * columns, columns), columns)
+        return pltpu.make_async_copy(wh_out.at[:, place], wh_hbm.at[:, place], wh_out_sem.at[j])
+
+    def close_hidden(j):
+        hid_copy(j).wait_recv()
+        place = pl.ds(pl.multiple_of(j * columns, columns), columns)
+        wh_out[:, place] += hid_in[:, place].astype(F32)
+        hidden_store(j).start()
+
+    def sum_store(w):
+        return pltpu.make_async_copy(outs.at[w], outs_hbm.at[w], outs_sem.at[w])
+
+    proj_store = pltpu.make_async_copy(wp_out, wp_hbm, wp_out_sem)
+
+    def close_sum(w):
+        outs[w] = own[w, chip].astype(F32)
+
+        @pl.when(has_left)
+        def _():
+            right_copy(own.at[w, 0], w, rounds - 1).wait_recv()
+            outs[w] += going_right[w, rounds - 1].astype(F32)
+
+        @pl.when(has_right)
+        def _():
+            left_copy(own.at[w, 0], w, rounds - 1).wait_recv()
+            outs[w] += going_left[w, rounds - 1].astype(F32)
+
+        sum_store(w).start()
 
     def feed(j):
         slot = j % 2
@@ -1144,6 +1171,7 @@
         wh_out[:, place] = wide[mine, :]
         hid_out[:, place] = wide[other, :].astype(BF16)
         hid_copy(j).start()
+        pl.when(j > 0)(lambda: close_hidden(j - 1))
 
         @pl.when(j == 2 * chip + core)
         def _():
@@ -1157,11 +1185,19 @@
             proj_copy.start()
 
     rounds = chips - 1
+    prepare(0)
+    pl.semaphore_wait(barrier, peers - 1)
+    pair_copy(0).start()
     dp_copy.wait()
     spread(0)
-    prepare(0)
+    each_peer(lambda k: vector_copy(k, me).start())
     prepare(1)
+    pair_copy(1).start()
     combine(0)
+    if split_vectors:
+        vec_out[...] = vgs[:, pl.ds(pl.multiple_of(me * cut, cut), cut)]
+    else:
+        vec_out[...] = vgs[...]
     opening = count * rounds - peers
 
     def step(t, carry):
@@ -1171,6 +1207,7 @@
         @pl.when((r == 1) & (w + 2 < count))
         def _():
             prepare(w + 2)
+            pair_copy(w + 2).start()
 
         @pl.when((r == 1) & (w + 1 < count))
         def _():
@@ -1184,39 +1221,35 @@
         def _():
             feed(t - opening)
 
+        @pl.when((r == rounds - 1) & (w > 0))
+        def _():
+            close_sum(w - 1)
+
         return carry
 
     lax.fori_loop(0, count * rounds, step, 0)
 
-    for w in range(count):
-        outs[w][...] = own[w, chip].astype(F32)
-
-        @pl.when(has_left)
-        def _():
-            right_copy(own.at[w, 0], w, rounds - 1).wait_recv()
-            outs[w][...] += going_right[w, rounds - 1].astype(F32)
-
-        @pl.when(has_right)
-        def _():
-            left_copy(own.at[w, 0], w, rounds - 1).wait_recv()
-            outs[w][...] += going_left[w, rounds - 1].astype(F32)
-
-    def gather_hidden(j, carry):
-        hid_copy(j).wait_recv()
-        place = pl.ds(pl.multiple_of(j * columns, columns), columns)
-        wh_out[:, place] += hid_in[:, place].astype(F32)
-        return carry
-
-    lax.fori_loop(0, peers, gather_hidden, 0)
+    close_hidden(peers - 1)
     proj_copy.wait_recv()
     wp_out[...] += proj_in[...].astype(F32)
+    proj_store.start()
+
+    def collect(k):
+        vector_copy(k, k).wait_recv()
+        vec_out[...] += vgr[k]
+
+    each_peer(collect)
+    close_sum(count - 1)
+    each_peer(lambda k: vector_copy(k, me).wait_send())
 
     def sent_hidden(j, carry):
         hid_copy(j).wait_send()
+        hidden_store(j).wait()
         return carry
 
     lax.fori_loop(0, peers, sent_hidden, 0)
     proj_copy.wait_send()
+    proj_store.wait()
 
     def sent_rows(origin, carry):
         @pl.when(has_right & (origin <= chip))
@@ -1233,6 +1266,7 @@
 
     def sent(w, carry):
         pair_copy(w).wait_send()
+        sum_store(w).wait()
 
         def sent_round(r, inner):
             @pl.when(has_right & (chip <= r))
@@ -1251,7 +1285,7 @@
     lax.fori_loop(0, count, sent, 0)
 
 
-def gradient_sums(peers, lefts, rights, lh, dp, wh, wp):
+def gradient_sums(peers, lefts, rights, lh, dp, wh, wp, vgs):
     count = len(lefts)
     rows, width = lefts[0].shape
     hidden = wh.shape[1]
@@ -1266,12 +1300,16 @@
     dma = pltpu.SemaphoreType.DMA
     blocks = pltpu.VMEM((count, chips, share, width), BF16)
     slots = pltpu.VMEM((count, chips - 1, share, width), BF16)
+    split_vectors = share % 128 == 0
+    cut = share if split_vectors else width
     return pl.pallas_call(
-        partial(sum_kernel, peers),
-        out_shape=(shape((share, width), F32),) * count
-        + (shape((share, hidden), F32), shape((columns, width), F32)),
-        in_specs=[anywhere] * (2 * count + 4),
-        out_specs=[vmem] * (count + 2),
+        partial(sum_kernel, peers, split_vectors),
+        out_shape=(
+            shape((count, share, width), F32), shape((share, hidden), F32),
+            shape((columns, width), F32), shape((VECTORS, cut), F32),
+        ),
+        in_specs=[anywhere] * (2 * count + 4) + [vmem],
+        out_specs=[anywhere] * 3 + [vmem],
         scratch_shapes=[
             pltpu.VMEM((count, rows, width), BF16), pltpu.VMEM((count, rows, width), BF16),
             pltpu.VMEM((2, width, width), F32),
@@ -1287,12 +1325,61 @@
             dma((count, chips - 1)), dma((count, chips - 1)),
             dma((peers,)), dma((peers,)), dma, dma,
             dma((chips,)), dma((chips,)), dma((chips,)),
+            pltpu.VMEM((count, share, width), F32), pltpu.VMEM((share, hidden), F32),
+            pltpu.VMEM((columns, width), F32), pltpu.VMEM((peers, VECTORS, cut), F32),
+            dma((peers,)), dma((peers,)), dma((count,)), dma((peers,)), dma,
         ],
         compiler_params=pltpu.CompilerParams(
             collective_id=1, has_side_effects=True, vmem_limit_bytes=63 * 2**20
         ),
         name="gradient_sums",
-    )(*lefts, *rights, lh, dp, wh, wp)
+    )(*lefts, *rights, lh, dp, wh, wp, vgs)
+
+
+def deliver_kernel(count, vectors, *refs):
+    vec, sources = refs[0], refs[1:6]
+    targets = refs[6 : 6 + count]
+    rows = refs[6 + count : 6 + count + vectors]
+    buffers = refs[6 + count + vectors : -2]
+    in_sem, out_sem = refs[-2:]
+    pieces = list(sources[:-1]) + [sources[-1].at[w] for w in range(count - 4)]
+    enter = [
+        pltpu.make_async_copy(piece, buffer, in_sem.at[index])
+        for index, (piece, buffer) in enumerate(zip(pieces, buffers))
+    ]
+    leave = [
+        pltpu.make_async_copy(buffer, target, out_sem.at[index])
+        for index, (buffer, target) in enumerate(zip(buffers, targets))
+    ]
+    for copy in enter:
+        copy.start()
+    for index, row in enumerate(rows):
+        row[...] = vec[index : index + 1, :]
+    for first, second in zip(enter, leave):
+        first.wait()
+        second.start()
+    for copy in leave:
+        copy.wait()
+
+
+def deliver(vec, hidden, project, out, back, squares, vectors):
+    shapes = [(out.shape, BF16), (back.shape, BF16), (hidden.shape, F32), (project.shape, F32)]
+    shapes += [(squares.shape[1:], F32)] * squares.shape[0]
+    count = len(shapes)
+    anywhere = pl.BlockSpec(memory_space=pl.ANY)
+    vmem = pl.BlockSpec(memory_space=pltpu.VMEM)
+    dma = pltpu.SemaphoreType.DMA
+    found = pl.pallas_call(
+        partial(deliver_kernel, count, vectors),
+        out_shape=tuple(jax.ShapeDtypeStruct(*kind) for kind in shapes)
+        + (jax.ShapeDtypeStruct((1, vec.shape[1]), F32),) * vectors,
+        in_specs=[vmem] + [anywhere] * 5,
+        out_specs=[anywhere] * count + [vmem] * vectors,
+        scratch_shapes=[pltpu.VMEM(*kind) for kind in shapes] + [dma((count,)), dma((count,))],
+        compiler_params=pltpu.CompilerParams(vmem_limit_bytes=40 * 2**20),
+        name="deliver",
+    )(vec, out, back, hidden, project, squares)
+    return found[:count], found[count:]
 
 
 def per_device(x, top, spans, *parameters):
@@ -1305,28 +1392,25 @@
     vectors = (gain1, bias1, mix_k, mix_v, mix_g, log_rate, extra, gain2, bias2, mix_h, mix_f)
     matrices = tuple(w[0] for w in (wk, wv, wg, wo, wh, wp, wf))
     found = relay(sections, peers, x, top, spans, vectors, matrices)
-    out, back, vec = found[0:3]
+    out, back, lk, lv, lg, lgt, lf, dk, dv, dg, datt, dsv, dproj = found[0:13]
+    vgs, lh = found[13], found[14].reshape(-1, x.shape[2])
     flat = (x.shape[0] * x.shape[1], x.shape[2])
-    lk, lv, lg, lgt, lf, dk, dv, dg, datt, dsv, dproj = (
-        part.reshape(flat) for part in found[3:14]
+    squares, d_wh, d_wp, vec = gradient_sums(
+        peers,
+        [part.reshape(flat) for part in (lf, lgt, lg, lk, lv)],
+        [part.reshape(flat) for part in (dsv, datt, dg, dk, dv)],
+        lh, dproj.reshape(flat), matrices[4], matrices[5], vgs,
     )
-    lh = found[14].reshape(-1, x.shape[2])
     share = x.shape[2] // peers
     if vec.shape[1] != share:
         vec = lax.dynamic_slice_in_dim(vec, lax.axis_index("dp") * share, share, 1)
-    summed = gradient_sums(
-        peers, (lf, lgt, lg, lk, lv), (dsv, datt, dg, dk, dv), lh, dproj, matrices[4], matrices[5]
-    )
-    d_wf, d_wo, d_wg, d_wk, d_wv, d_wh, d_wp = (part[None] for part in summed)
-
-    def row(index):
-        return vec[index : index + 1]
-
+    moved, rows = deliver(vec, d_wh, d_wp, out, back, squares, 11)
+    out, back, d_wh, d_wp, d_wf, d_wo, d_wg, d_wk, d_wv = (part[None] for part in moved)
     return (
-        out[None], back[None],
-        row(0), row(1), row(2), row(3), row(4), row(5), row(6),
+        out, back,
+        rows[0], rows[1], rows[2], rows[3], rows[4], rows[5], rows[6],
         d_wk, d_wv, d_wg, d_wo,
-        row(7), row(8), row(9), row(10),
+        rows[7], rows[8], rows[9], rows[10],
         d_wh, d_wp, d_wf,
     )
 

time: 287 us -> 271 us (0.944)
  Pallas kernels: 274 us -> 263 us
  local copies, waits for them, and re-layouts: 12 us -> 6.66 us
    pallas_call x2 -> x3, Pallas kernels: 274 us -> 263 us  [the longest x1 152 us: relay(): pl.pallas_call(partial(relay_kernel, sections, peers), out_shape=(low, lo...]
    unnamed x25 -> x12, local copies, waits for them, and re-layouts: 10.5 us -> 6.66 us
where the time goes in v5:
time: 271 us
  Pallas kernels  263 us (97%)
  local copies, waits for them, and re-layouts  6.66 us (2%)
    pallas_call x1, Pallas kernels, relay(): pl.pallas_call(partial(relay_kernel, sections, peers), out_shape=(low, lo...  152 us
    pallas_call x1, Pallas kernels, gradient_sums(): pl.pallas_call(partial(sum_kernel, peers, split_vectors), out_shape=(shap...  106 us
    unnamed x12, local copies, waits for them, and re-layouts  6.66 us

profile of v5, /device:TPU:0, one launch (start us, length us, event | category | flops | bytes accessed | tf_op | source)
XLA Modules:
  0.0 270.6 jit_solution(9518212959532530842)
XLA Ops:
  0.7 152.4 %relay.1 = (bf16[2,128,1024]{2,1,0:T(8,128)(2,1)}, bf16[2,128,1024]{2,1,0:T(8,128)(2,1)}, bf16[2,128,1024]{2,1,0:T(8,128)(2,1)}, bf16[2,128,1024]{2,1,0:T(8,128)...) custom-call(s32[2,5]{1,0:T(2,128)} %refs_0_.1, ...), custom_call_target="tpu_custom_call" | custom-call | tf_op jit(solution)/shard_map/relay/pallas_call | solution.py:882
  153.1 0.0 copy-start.3
  153.1 106.2 %gradient_sums.1 = (f32[5,128,1024]{2,1,0:T(8,128)}, f32[128,4096]{1,0:T(8,128)}, f32[512,1024]{1,0:T(8,128)}, f32[16,128]{1,0:T(8,128)}) custom-call(bf16[256,1024]{1,0:T(8,128)(2,1)} %bitcast.42, bf16[256,1024]{1,0:T(8,128)(2,1)} %bitcast.41, bf16[256,1024]{1,0:T(8,128)(2,1)} %bitcast.40, bf16[256,1024]{1,0:T(8,128)(2,1)} %bitcast.38, ...), custom_call_target="tpu_custom_call" | custom-call | tf_op jit(solution)/shard_map/gradient_sums/pallas_call | solution.py:1305
  259.3 0.0 copy-done.3
  259.3 0.0 copy-start
  259.3 1.7 copy-done
  261.0 0.0 copy-start.1
  261.0 1.6 copy-done.1
  262.6 0.0 copy-start.2
  262.6 1.6 copy-done.2
  264.2 0.0 copy-start.4
  264.2 1.0 copy-done.4
  265.3 0.0 copy-start.5
  265.3 0.7 copy-done.5
  266.0 4.4 %deliver.1 = (bf16[2,128,1024]{2,1,0:T(8,128)(2,1)}, bf16[2,128,1024]{2,1,0:T(8,128)(2,1)}, f32[128,4096]{1,0:T(8,128)}, f32[512,1024]{1,0:T(8,128)}, f32[128,10...) custom-call(f32[16,128]{1,0:T(8,128)S(1)} %copy-done.5, ...), custom_call_target="tpu_custom_call" | custom-call | tf_op jit(solution)/shard_map/deliver/pallas_call | solution.py:1372
Async XLA Ops:
  153.1 106.2 %copy-start.3 = (bf16[2,128,1024]{2,1,0:T(8,128)(2,1)S(1)}, bf16[2,128,1024]{2,1,0:T(8,128)(2,1)}, u32[]{:S(2)}) copy-start(bf16[2,128,1024]{2,1,0:T(8,128)(2,1)} %get-tuple-element.73.refs_1_) | copy-start | bytes 1572868
  259.3 1.7 copy-start
  261.0 1.6 copy-start.1
  262.6 1.6 copy-start.2
  264.2 1.0 copy-start.4
  265.3 0.7 copy-start.5

commit v6 on v5

--- a/solution.py
+++ b/solution.py
@@ -62,17 +62,18 @@
         gain1, bias1, mix_k, mix_v, mix_g, log_rate, extra, gain2, bias2, mix_h, mix_f,
         wk_in, wv_in, wg_in, wo_in, wh_in, wp_in, wf_in,
         out_hbm, back_hbm, lk_hbm, lv_hbm, lg_hbm, lgt_hbm, lf_hbm,
-        dk_hbm, dv_hbm, dg_hbm, datt_hbm, dsv_hbm, dproj_hbm, vgs, lh_all,
+        dk_hbm, dv_hbm, dg_hbm, datt_hbm, dsv_hbm, dproj_hbm, vgs, lh_all, near,
         wk_t, wv_t, wg_t, wo_t, wf_t, wp_t, wh_t,
         out, back, lk, lv, lg, lgt, lf, dk, dv, dg, datt, dsv, dproj,
         lh, sq, dh, turned,
         wk, wv, wg, wo, wh, wp, wf,
-        xs, hx, dys, kk, vv, sg, sa, sb, mid, hmid, proj, sv, act, halo1, halo2,
+        xs, hx, dys, kk, vv, sg, sa, sb, mid, hmid, proj, sv, act,
         e0, e1, low_mask, up_mask, split, acc, t1, t2, t3,
         states, back_states, de2, de1, sum_row, sum_back, send_de2, send_de1, vg,
+        sp1, gp1, sd1, sp2, gp2, sd2, fo, iv,
         w_sem, x_sem, top_sem, s_h0, s_x, s_hx, s_st, s_mid, s_dy, s_de2, s_bst, s_de1,
         r_x, r_hx, r_st, r_mid, r_dy, r_de2, r_bst, r_de1, store_sem,
-        s_lh, r_lh, own_sem, turn_sem, back_sem,
+        s_lh, r_lh, own_sem, s_near, r_near, turn_sem, back_sem,
     ) = refs
     me_s = lax.axis_index("section")
     me = lax.axis_index("dp")
@@ -137,6 +138,7 @@
         pltpu.make_async_copy(top_in, dys, top_sem).start()
 
     rate = jnp.exp(log_rate[...])
+    boost = jnp.exp(extra[...])
     decay_block = jnp.exp(-rate * row_count)
     grow_block = jnp.exp(rate * row_count)
 
@@ -266,18 +268,19 @@
     def state_copy(m, k, slot):
         return remote(sum_row.at[m], states.at[m, slot], s_st.at[m, k], r_st.at[m, slot], me_s, k)
 
-    def back_copy(m, i):
-        rows = pl.ds(pl.multiple_of(i * RB, RB), RB)
+    pieces = (
+        (0, row_count // 2), (row_count // 2, row_count // 2 - 16), (row_count - 16, 16)
+    )
+
+    def back_copy(m, index):
+        rows = pl.ds(*pieces[index])
         return remote(
-            back.at[m, rows], dys.at[m, rows], s_dy.at[m, i], r_dy.at[m, i], below, me
+            back.at[m, rows], dys.at[m, rows], s_dy.at[m, index], r_dy.at[m, index], below, me
         )
 
-    def each_chunk(action):
-        def turn(i, carry):
-            action(i)
-            return carry
-
-        lax.fori_loop(0, chunks, turn, 0)
+    def each_piece(action):
+        for index in range(len(pieces)):
+            action(index)
 
     def second_copy(m):
         return remote(send_de2.at[m], de2.at[m], s_de2.at[m], r_de2.at[m], me_s, left)
@@ -297,6 +300,8 @@
         return remote(
             lh.at[m], lh_all.at[slot, m], s_lh.at[m, k], r_lh.at[m, slot], me_s, 2 * k + core
         )
+
+    is_late = 2 * me_s >= sections
 
     def own_copy(m):
         return pltpu.make_async_copy(lh.at[m], lh_all.at[chip, m], own_sem.at[m])
@@ -311,22 +316,47 @@
 
         lax.fori_loop(0, chips, turn, 0)
 
-    def start_gather(m):
-        own_copy(m).start()
-        each_chip(lambda k: gather_copy(m, k, chip).start())
-
-    def start_gathers(early):
+    ahead = jnp.minimum(me + 2, peers - 1)
+    behind = jnp.maximum(me - 2, 0)
+    has_ahead = chip + 1 < chips
+    has_behind = chip > 0
+
+    def near_copy(m, way):
+        return remote(
+            dproj.at[m], near.at[way, m], s_near.at[way, m], r_near.at[way, m],
+            me_s, behind if way else ahead,
+        )
+
+    def send_near(m):
+        pl.when(has_ahead)(lambda: near_copy(m, 0).start())
+        pl.when(has_behind)(lambda: near_copy(m, 1).start())
+
+    def end_near(m):
+        @pl.when(has_ahead)
+        def _():
+            near_copy(m, 0).wait_send()
+            near_copy(m, 1).wait_recv()
+
+        @pl.when(has_behind)
+        def _():
+            near_copy(m, 1).wait_send()
+            near_copy(m, 0).wait_recv()
+
+    def start_gathers():
         for m in range(batches):
-            in_gap = me_s + 1 + m < sections
-
-            @pl.when(in_gap if early else jnp.logical_not(in_gap))
+            own_copy(m).start()
+
+            @pl.when(jnp.logical_not(is_late))
             def _(m=m):
-                start_gather(m)
+                each_chip(lambda k: gather_copy(m, k, chip).start())
 
     def end_gather(m):
         own_copy(m).wait()
-        each_chip(lambda k: gather_copy(m, k, chip).wait_send())
-        each_chip(lambda k: gather_copy(m, k, k).wait_recv())
+
+        @pl.when(jnp.logical_not(is_late))
+        def _():
+            each_chip(lambda k: gather_copy(m, k, chip).wait_send())
+            each_chip(lambda k: gather_copy(m, k, k).wait_recv())
 
     @pl.when((me_s == 0) & has_right)
     def _():
@@ -377,7 +407,6 @@
         source, target = returns[index]
         return pltpu.make_async_copy(source, target, back_sem.at[index])
 
-    is_late = 2 * me_s >= sections
 
     def release(m, index):
         @pl.when(is_late & (m == batches - 1))
@@ -392,6 +421,19 @@
     def span_of(i):
         return pl.ds(pl.multiple_of(i * RB, RB), RB)
 
+    def split_sums():
+        def turn(i, carry):
+            rows = span_of(i)
+            low = pl.ds(pl.multiple_of(row_count + i * RB, RB), RB)
+            for source, place in ((t1, pl.ds(0, width)), (t2, pl.ds(width, width))):
+                value = source[rows, :]
+                high = value.astype(BF16)
+                split[rows, place] = high
+                split[low, place] = (value - high.astype(F32)).astype(BF16)
+            return carry
+
+        lax.fori_loop(0, chunks, turn, 0, unroll=True)
+
     def forward(m, carry):
         starts = starts_of(m)
 
@@ -405,21 +447,22 @@
 
         halo_rows, _ = normalise(hx[m].astype(F32))
         halo_rows = halo_rows * gain1[...] + bias1[...]
-        halo1[m] = halo_rows[8:16]
 
         def mix_in(i, last):
             rows = span_of(i)
-            normed, _ = normalise(xs[m, rows, :].astype(F32))
-            normed = normed * gain1[...] + bias1[...]
+            spare, spread = normalise(xs[m, rows, :].astype(F32))
+            sp1[m, rows, :] = spare
+            sd1[m, rows, :] = spread
+            normed = spare * gain1[...] + bias1[...]
             earlier = moved_down(normed, last) * keep_of(column(i), starts)
             gap = normed - earlier
+            gp1[m, rows, :] = gap.astype(BF16)
             lk[m, rows, :] = (earlier + gap * mix_k[...]).astype(BF16)
             lv[m, rows, :] = (earlier + gap * mix_v[...]).astype(BF16)
             lg[m, rows, :] = (earlier + gap * mix_g[...]).astype(BF16)
             return normed[RB - 1 : RB]
 
         lax.fori_loop(0, chunks, mix_in, halo_rows[15:16], unroll=True)
-
         weight_ready(m, 0)
         weight_ready(m, 1)
         kk[m] = dot_nn(lk[m], wk[...])
@@ -430,15 +473,12 @@
 
         def spread_in(i, totals):
             rows = span_of(i)
-            weight = jnp.exp(kk[m, rows, :]) * e1[rows, :]
+            plain = jnp.exp(kk[m, rows, :])
+            kk[m, rows, :] = plain
+            weight = plain * e1[rows, :]
             weighted = weight * vv[m, rows, :]
-            high_a = weighted.astype(BF16)
-            high_b = weight.astype(BF16)
-            split[rows, 0:width] = high_a
-            split[rows, width:] = high_b
-            low = pl.ds(pl.multiple_of(row_count + i * RB, RB), RB)
-            split[low, 0:width] = (weighted - high_a.astype(F32)).astype(BF16)
-            split[low, width:] = (weight - high_b.astype(F32)).astype(BF16)
+            t1[rows, :] = weighted
+            t2[rows, :] = weight
             chosen = segment(column(i), starts) == end_segment
             return (
                 totals[0] + fold(jnp.where(chosen, weighted, 0.0)),
@@ -459,7 +499,9 @@
 
         weight_ready(m, 2)
         sg[m] = dot_nn(lg[m], wg[...])
+        split_sums()
         acc[...] = dot_nn(low_mask[m], split[...])
+        sg[m] = sigmoid(sg[m])
         release(m, 2)
 
         def receive_state(k, held):
@@ -485,11 +527,12 @@
             state_b = grown * acc[rows, width:] + held * enter_b
             sa[m, rows, :] = state_a
             sb[m, rows, :] = state_b
-            present = jnp.exp(extra[...] + kk[m, rows, :])
-            gate = sigmoid(sg[m, rows, :])
-            sg[m, rows, :] = gate
-            found = (state_a + present * vv[m, rows, :]) / (state_b + present)
-            lgt[m, rows, :] = (gate * found).astype(BF16)
+            present = boost * kk[m, rows, :]
+            inverse = 1.0 / (state_b + present)
+            found = (state_a + present * vv[m, rows, :]) * inverse
+            iv[m, rows, :] = inverse
+            fo[m, rows, :] = found
+            lgt[m, rows, :] = (sg[m, rows, :] * found).astype(BF16)
             return carry
 
         lax.fori_loop(0, chunks, mix_states, 0, unroll=True)
@@ -502,26 +545,30 @@
         def _():
             middle_halo(m).start()
 
-        def mix_second(i, last):
-            rows = span_of(i)
-            normed, _ = normalise(mid[m, rows, :])
-            normed = normed * gain2[...] + bias2[...]
-            earlier = moved_down(normed, last) * keep_of(column(i), starts)
+        def mix_second(start, size, last):
+            rows = pl.ds(start, size)
+            spare, spread = normalise(mid[m, rows, :])
+            sp2[m, rows, :] = spare
+            sd2[m, rows, :] = spread
+            normed = spare * gain2[...] + bias2[...]
+            position = base + start + lax.broadcasted_iota(jnp.int32, (size, 1), 0)
+            earlier = moved_down(normed, last) * keep_of(position, starts)
             gap = normed - earlier
+            gp2[m, rows, :] = gap.astype(BF16)
             lh[m, rows, :] = (earlier + gap * mix_h[...]).astype(BF16)
             lf[m, rows, :] = (earlier + gap * mix_f[...]).astype(BF16)
-            return normed[RB - 1 : RB]
-
-        lax.fori_loop(0, chunks, mix_second, none, unroll=True)
+            return normed[size - 1 : size]
+
+        last = none
+        for start in range(0, row_count, RB):
+            last = mix_second(start, RB, last)
 
         @pl.when(has_left)
         def _():
             middle_halo(m).wait_recv()
 
         halo_rows, _ = normalise(hmid[m])
-        halo_rows = halo_rows * gain2[...] + bias2[...]
-        halo2[m] = halo_rows
-        mix_second(0, halo_rows)
+        mix_second(0, 16, halo_rows * gain2[...] + bias2[...])
 
         for index in range(4, 7):
             weight_ready(m, index)
@@ -573,7 +620,7 @@
         for index in range(7):
             return_copy(index).start()
 
-    start_gathers(True)
+    start_gathers()
 
     def add_vector(index, value):
         vg[index] += fold(value)
@@ -593,7 +640,7 @@
 
         @pl.when(has_next)
         def _():
-            each_chunk(lambda i: back_copy(m, i).wait_recv())
+            each_piece(lambda i: back_copy(m, i).wait_recv())
 
         def open_back(i, carry):
             rows = span_of(i)
@@ -631,12 +678,12 @@
         def _():
             second_copy(m).start()
 
-        def back_second(i, last, following):
-            rows = span_of(i)
-            spare, spread = normalise(mid[m, rows, :])
-            normed = spare * gain2[...] + bias2[...]
-            kept = keep_of(column(i), starts)
-            gap = normed - moved_down(normed, last) * kept
+        def back_second(start, size, following):
+            rows = pl.ds(start, size)
+            spare, spread = sp2[m, rows, :], sd2[m, rows, :]
+            gap = gp2[m, rows, :].astype(F32)
+            position = base + start + lax.broadcasted_iota(jnp.int32, (size, 1), 0)
+            kept = keep_of(position, starts)
             from_h = t1[rows, :]
             from_f = t2[rows, :]
             add_vector(9, from_h * gap)
@@ -652,52 +699,31 @@
             d_mid = dys[m, rows, :].astype(F32) + spread * (scaled - mean_one - spare * mean_two)
             t3[rows, :] = d_mid
             datt[m, rows, :] = d_mid.astype(BF16)
-            return normed[RB - 1 : RB]
-
-        def following_second(i):
-            start = pl.multiple_of((i + 1) * RB, RB)
-            return second_earlier(pl.ds(start, 8), base + start + eight)[0:1]
-
-        last = halo2[m]
-        for i in range(chunks - 1):
-            last = back_second(i, last, following_second(i))
+
+        for start, size in pieces[:-1]:
+            end = start + size
+            back_second(start, size, second_earlier(pl.ds(end, 8), base + end + eight)[0:1])
 
         @pl.when(has_right)
         def _():
             second_copy(m).wait_recv()
 
-        back_second(chunks - 1, last, de2[m])
+        back_second(*pieces[-1], de2[m])
         turned_ready(m, 3)
         t1[...] = dot_nn(datt[m], wo[...])
         open_segment = segment(base, starts)
 
         def back_states_in(i, totals):
             rows = span_of(i)
-            d_gated = t1[rows, :]
-            gate = sg[m, rows, :]
-            keys = kk[m, rows, :]
-            values = vv[m, rows, :]
-            present = jnp.exp(extra[...] + keys)
-            inverse = 1.0 / (sb[m, rows, :] + present)
-            found = (sa[m, rows, :] + present * values) * inverse
-            d_found = d_gated * gate
-            dg[m, rows, :] = (d_found * found * (1.0 - gate)).astype(BF16)
-            d_a = d_found * inverse
-            d_b = -d_a * found
-            d_key = (d_a * values + d_b) * present
-            add_vector(6, d_key)
-            t1[rows, :] = d_key
-            t2[rows, :] = d_a * present
+            d_found = t1[rows, :] * sg[m, rows, :]
+            d_a = d_found * iv[m, rows, :]
+            d_b = -d_a * fo[m, rows, :]
             falling = e0[rows, :]
             scaled_a = d_a * falling
             scaled_b = d_b * falling
-            high_a = scaled_a.astype(BF16)
-            high_b = scaled_b.astype(BF16)
-            split[rows, 0:width] = high_a
-            split[rows, width:] = high_b
-            low = pl.ds(pl.multiple_of(row_count + i * RB, RB), RB)
-            split[low, 0:width] = (scaled_a - high_a.astype(F32)).astype(BF16)
-            split[low, width:] = (scaled_b - high_b.astype(F32)).astype(BF16)
+            t1[rows, :] = scaled_a
+            t2[rows, :] = scaled_b
+            acc[rows, 0:width] = d_found
             chosen = segment(column(i), starts) == open_segment
             return (
                 totals[0] + fold(jnp.where(chosen, scaled_a, 0.0)),
@@ -715,6 +741,21 @@
             return carry
 
         lax.fori_loop(0, me, send_state, 0)
+        split_sums()
+
+        def back_present(i, carry):
+            rows = span_of(i)
+            gate, found = sg[m, rows, :], fo[m, rows, :]
+            d_found = acc[rows, 0:width]
+            dg[m, rows, :] = (d_found * found * (1.0 - gate)).astype(BF16)
+            gained = d_found * iv[m, rows, :] * (boost * kk[m, rows, :])
+            d_key = gained * (vv[m, rows, :] - found)
+            add_vector(6, d_key)
+            t1[rows, :] = d_key
+            t2[rows, :] = gained
+            return carry
+
+        lax.fori_loop(0, chunks, back_present, 0, unroll=True)
         acc[...] = dot_nn(up_mask[m], split[...])
 
         def receive_state(turn, held):
@@ -739,7 +780,7 @@
             d_a = grown * acc[rows, 0:width] + held * enter_a
             d_b = grown * acc[rows, width:] + held * enter_b
             add_vector(5, d_a * sa[m, rows, :] + d_b * sb[m, rows, :])
-            weight = jnp.exp(kk[m, rows, :])
+            weight = kk[m, rows, :]
             dv[m, rows, :] = (t2[rows, :] + d_a * weight).astype(BF16)
             dk[m, rows, :] = (t1[rows, :] + (d_a * vv[m, rows, :] + d_b) * weight).astype(BF16)
             return carry
@@ -765,15 +806,17 @@
         def _():
             first_copy(m).start()
 
+        pl.when(me_s == 0)(lambda: send_near(m))
         for index in range(6, 12):
             store_copy(index, m).start()
 
-        def back_first(i, last, following):
-            rows = span_of(i)
-            spare, spread = normalise(xs[m, rows, :].astype(F32))
-            normed = spare * gain1[...] + bias1[...]
-            kept = keep_of(column(i), starts)
-            gap = normed - moved_down(normed, last) * kept
+        def back_first(index, following):
+            start, size = pieces[index]
+            rows = pl.ds(start, size)
+            spare, spread = sp1[m, rows, :], sd1[m, rows, :]
+            gap = gp1[m, rows, :].astype(F32)
+            position = base + start + lax.broadcasted_iota(jnp.int32, (size, 1), 0)
+            kept = keep_of(position, starts)
             from_k = t1[rows, :]
             from_v = t2[rows, :]
             from_g = acc[rows, 0:width]
@@ -793,30 +836,28 @@
 
             @pl.when(has_prior)
             def _():
-                back_copy(m, i).start()
-
-            return normed[RB - 1 : RB]
-
-        def following_first(i):
-            start = pl.multiple_of((i + 1) * RB, RB)
-            return first_earlier(pl.ds(start, 8), base + start + eight)[0:1]
-
-        last = halo1[m, 7:8]
-        for i in range(chunks - 1):
-            last = back_first(i, last, following_first(i))
+                back_copy(m, index).start()
+
+        for index, (start, size) in enumerate(pieces[:-1]):
+            end = start + size
+            back_first(index, first_earlier(pl.ds(end, 8), base + end + eight)[0:1])
 
         @pl.when(has_right)
         def _():
             first_copy(m).wait_recv()
 
-        back_first(chunks - 1, last, de1[m])
+        back_first(len(pieces) - 1, de1[m])
         store_copy(12, m).start()
-
         return carry
 
     lax.fori_loop(0, batches, backward, 0)
-    pl.when(has_prior)(lambda: each_chunk(lambda i: back_copy(batches - 1, i).wait_send()))
-    start_gathers(False)
+    pl.when(has_prior)(lambda: each_piece(lambda i: back_copy(batches - 1, i).wait_send()))
+
+    @pl.when(me_s > 0)
+    def _():
+        for m in range(batches):
+            send_near(m)
+
 
     vgs[...] = jnp.sum(vg[...], axis=1)
     vgs[5:6] = vgs[5:6] * (-rate * jnp.exp(-rate))
@@ -844,7 +885,7 @@
 
         @pl.when(has_prior)
         def _():
-            pl.when(m + 1 < batches)(lambda: each_chunk(lambda i: back_copy(m, i).wait_send()))
+            pl.when(m + 1 < batches)(lambda: each_piece(lambda i: back_copy(m, i).wait_send()))
 
         for index in range(13):
             store_copy(index, m).wait()
@@ -855,6 +896,7 @@
 
         lax.fori_loop(me + 1, peers, ended, 0)
         end_gather(m)
+        end_near(m)
 
         def ended_back(k, carry):
             back_state_copy(m, k, me).wait_send()
@@ -885,13 +927,14 @@
             low, low, low, low, low, low, low,
             low, low, low, low, low, low, shape((VECTORS, width), F32),
             shape((peers // 2, batches, rows, width), BF16),
+            shape((2, batches, rows, width), BF16),
             square, square, square, square, square,
             shape((width, hidden), BF16), shape((hidden, width), BF16),
         ),
         in_specs=[pl.BlockSpec(memory_space=pltpu.SMEM), anywhere, anywhere]
         + [vmem] * 11
         + [anywhere] * 7,
-        out_specs=[anywhere] * 13 + [vmem] + [anywhere] * 8,
+        out_specs=[anywhere] * 13 + [vmem] + [anywhere] * 9,
         scratch_shapes=[narrow(BF16)] * 13 + [
             narrow(BF16), pltpu.VMEM((batches, rows, hidden), BF16),
             pltpu.VMEM((batches, rows, hidden), BF16), pltpu.VMEM((2, 512, 512), BF16),
@@ -902,7 +945,6 @@
             narrow(F32), narrow(F32), narrow(F32), narrow(F32), narrow(F32), narrow(F32),
             pltpu.VMEM((batches, 1, width), F32), narrow(F32), narrow(F32),
             pltpu.VMEM((batches, rows, hidden), BF16),
-            pltpu.VMEM((batches, 8, width), F32), pltpu.VMEM((batches, 1, width), F32),
             pltpu.VMEM((rows, width), F32), pltpu.VMEM((rows, width), F32),
             pltpu.VMEM((batches, rows, 2 * rows), BF16), pltpu.VMEM((batches, rows, 2 * rows), BF16),
             pltpu.VMEM((2 * rows, 2 * width), BF16), pltpu.VMEM((rows, 2 * width), F32),
@@ -914,14 +956,18 @@
             pltpu.VMEM((batches, width // 64, 128), F32),
             pltpu.VMEM((batches, 1, width), F32), pltpu.VMEM((batches, 1, width), F32),
             pltpu.VMEM((VECTORS, 8, width), F32),
+            narrow(F32), narrow(BF16), pltpu.VMEM((batches, rows, 1), F32),
+            narrow(F32), narrow(BF16), pltpu.VMEM((batches, rows, 1), F32),
+            narrow(F32), narrow(F32),
             dma((7,)), dma, dma,
             dma((batches,)), dma((batches, PARTS)), dma((batches,)), dma((batches, peers)),
-            dma((batches,)), dma((batches, rows // RB)), dma((batches,)), dma((batches, peers)),
+            dma((batches,)), dma((batches, 3)), dma((batches,)), dma((batches, peers)),
             dma((batches,)),
             dma((batches, PARTS)), dma((batches,)), dma((batches, peers)), dma((batches,)),
-            dma((batches, rows // RB)), dma((batches,)), dma((batches, peers)), dma((batches,)),
+            dma((batches, 3)), dma((batches,)), dma((batches, peers)), dma((batches,)),
             dma((13, batches)),
             dma((batches, peers // 2)), dma((batches, peers // 2)), dma((batches,)),
+            dma((2, batches)), dma((2, batches)),
             dma((2,)), dma((7,)),
         ],
         compiler_params=pltpu.CompilerParams(
@@ -936,10 +982,10 @@
     return (wk, wv, wg, wo, wh, wp, wf)
 
 
-def sum_kernel(peers, split_vectors, *refs):
+def sum_kernel(sections, peers, split_vectors, *refs):
     left_in, right_in = refs[0:5], refs[5:10]
-    lh_in, dp_in, wh_in, wp_in, vgs = refs[10:15]
-    outs_hbm, wh_hbm, wp_hbm, vec_out = refs[15:19]
+    lh_in, dp_in, near_in, wh_in, wp_in, vgs = refs[10:16]
+    outs_hbm, wh_hbm, wp_hbm, vec_out = refs[16:20]
     (
         lefts, rights, whole, own, pair_out, going_right, going_left,
         lh, dp, wh, wp, act, wide, hid_out, hid_in, proj_out, proj_in,
@@ -947,7 +993,8 @@
         s_pair, r_pair, s_right, r_right, s_left, r_left, s_hid, r_hid, s_proj, r_proj,
         s_ahead, s_behind, r_rows,
         outs, wh_out, wp_out, vgr, s_vg, r_vg, outs_sem, wh_out_sem, wp_out_sem,
-    ) = refs[19:]
+        near_sem,
+    ) = refs[20:]
     count = len(left_in)
     me_s = lax.axis_index("section")
     me = lax.axis_index("dp")
@@ -980,12 +1027,23 @@
     for w in range(count):
         pltpu.make_async_copy(left_in[w], lefts.at[w], left_sem.at[w]).start()
         pltpu.make_async_copy(right_in[w], rights.at[w], right_sem.at[w]).start()
+    is_late = 2 * me_s >= sections
     lh_copy = pltpu.make_async_copy(lh_in, lh, lh_sem)
     rows = dp_in.shape[0]
     own_rows = pl.ds(pl.multiple_of(chip * rows, rows), rows)
     dp_copy = pltpu.make_async_copy(dp_in, dp.at[own_rows], dp_sem)
     dp_copy.start()
-    lh_copy.start()
+
+    def near_load(way):
+        origin = jnp.minimum(chip + 1, chips - 1) if way else jnp.maximum(chip - 1, 0)
+        place = pl.ds(pl.multiple_of(origin * rows, rows), rows)
+        return pltpu.make_async_copy(near_in.at[way], dp.at[place], near_sem.at[way])
+
+    pl.when(has_left)(lambda: near_load(0).start())
+    pl.when(has_right)(lambda: near_load(1).start())
+    lh_own = pltpu.make_async_copy(lh_in.at[own_rows], lh.at[own_rows], lh_sem)
+    pl.when(is_late)(lh_own.start)
+    pl.when(jnp.logical_not(is_late))(lh_copy.start)
 
     def wh_copy(j, slot):
         return pltpu.make_async_copy(
@@ -1051,16 +1109,22 @@
 
     from_end = chips - 1 - chip
 
+    def launch(w):
+        def turn(r, carry):
+            @pl.when(has_right & (chip == 0))
+            def _():
+                right_copy(own.at[w, chips - 1 - r], w, r).start()
+
+            @pl.when(has_left & (from_end == 0))
+            def _():
+                left_copy(own.at[w, r], w, r).start()
+
+            return carry
+
+        lax.fori_loop(0, rounds, turn, 0)
+
     def travel(w, r):
         prior = jnp.maximum(r - 1, 0)
-
-        @pl.when(has_right & (chip == 0))
-        def _():
-            right_copy(own.at[w, chips - 1 - r], w, r).start()
-
-        @pl.when(has_left & (from_end == 0))
-        def _():
-            left_copy(own.at[w, r], w, r).start()
 
         @pl.when(has_right & (chip > 0) & (chip <= r))
         def _():
@@ -1080,27 +1144,29 @@
             ).astype(BF16)
             left_copy(slot, w, r).start()
 
-    def rows_copy(origin, send, index):
-        block = dp.at[pl.ds(pl.multiple_of(origin * rows, rows), rows)]
-        return remote(block, block, send.at[origin], r_rows.at[origin], index)
-
-    def each_origin(low, high):
+    def rows_copy(kind, origin, send, index):
+        block = (lh if kind else dp).at[pl.ds(pl.multiple_of(origin * rows, rows), rows)]
+        return remote(block, block, send.at[kind, origin], r_rows.at[kind, origin], index)
+
+    def each_origin(kind, low, high):
         def turn(origin, carry):
-            rows_copy(origin, s_ahead, after).wait_recv()
+            rows_copy(kind, origin, s_ahead, after).wait_recv()
             return carry
 
         lax.fori_loop(low, high, turn, 0)
 
-    def spread(r):
+    def spread(kind, r):
+        held = 0 if kind else 1
+
         @pl.when(has_right & (chip >= r))
         def _():
-            pl.when(r > 0)(lambda: rows_copy(chip - r, s_ahead, after).wait_recv())
-            rows_copy(chip - r, s_ahead, after).start()
+            pl.when(r > held)(lambda: rows_copy(kind, chip - r, s_ahead, after).wait_recv())
+            rows_copy(kind, chip - r, s_ahead, after).start()
 
         @pl.when(has_left & (from_end >= r))
         def _():
-            pl.when(r > 0)(lambda: rows_copy(chip + r, s_behind, before).wait_recv())
-            rows_copy(chip + r, s_behind, before).start()
+            pl.when(r > held)(lambda: rows_copy(kind, chip + r, s_behind, before).wait_recv())
+            rows_copy(kind, chip + r, s_behind, before).start()
 
     def hid_copy(j):
         place = pl.ds(pl.multiple_of(j * columns, columns), columns)
@@ -1150,9 +1216,12 @@
 
         @pl.when(j == 0)
         def _():
-            lh_copy.wait()
-            pl.when(chip == 0)(lambda: each_origin(1, chips))
-            pl.when(from_end == 0)(lambda: each_origin(0, chips - 1))
+            dp_copy.wait()
+            pl.when(chip == 0)(lambda: each_origin(0, 2, chips))
+            pl.when(from_end == 0)(lambda: each_origin(0, 0, chips - 2))
+            pl.when(jnp.logical_not(is_late))(lh_copy.wait)
+            pl.when(is_late & (chip == 0))(lambda: each_origin(1, 1, chips))
+            pl.when(is_late & (from_end == 0))(lambda: each_origin(1, 0, chips - 1))
 
         wh_copy(j, slot).wait()
         wp_copy(j, slot).wait()
@@ -1188,12 +1257,20 @@
     prepare(0)
     pl.semaphore_wait(barrier, peers - 1)
     pair_copy(0).start()
-    dp_copy.wait()
-    spread(0)
+    pl.when(has_left)(lambda: near_load(0).wait())
+    pl.when(has_right)(lambda: near_load(1).wait())
+    spread(0, 1)
+
+    @pl.when(is_late)
+    def _():
+        lh_own.wait()
+        spread(1, 0)
+
     each_peer(lambda k: vector_copy(k, me).start())
     prepare(1)
     pair_copy(1).start()
     combine(0)
+    launch(0)
     if split_vectors:
         vec_out[...] = vgs[:, pl.ds(pl.multiple_of(me * cut, cut), cut)]
     else:
@@ -1212,10 +1289,15 @@
         @pl.when((r == 1) & (w + 1 < count))
         def _():
             combine(w + 1)
-
-        @pl.when(t + 1 < rounds)
-        def _():
-            spread(t + 1)
+            launch(w + 1)
+
+        @pl.when(t + 2 < rounds)
+        def _():
+            spread(0, t + 2)
+
+        @pl.when(is_late & (t + 1 < rounds))
+        def _():
+            spread(1, t + 1)
 
         @pl.when(t >= opening)
         def _():
@@ -1252,13 +1334,21 @@
     proj_store.wait()
 
     def sent_rows(origin, carry):
-        @pl.when(has_right & (origin <= chip))
-        def _():
-            rows_copy(origin, s_ahead, after).wait_send()
-
-        @pl.when(has_left & (origin >= chip))
-        def _():
-            rows_copy(origin, s_behind, before).wait_send()
+        @pl.when(has_right & (origin < chip))
+        def _():
+            rows_copy(0, origin, s_ahead, after).wait_send()
+
+        @pl.when(has_left & (origin > chip))
+        def _():
+            rows_copy(0, origin, s_behind, before).wait_send()
+
+        @pl.when(is_late & has_right & (origin <= chip))
+        def _():
+            rows_copy(1, origin, s_ahead, after).wait_send()
+
+        @pl.when(is_late & has_left & (origin >= chip))
+        def _():
+            rows_copy(1, origin, s_behind, before).wait_send()
 
         return carry
 
@@ -1285,7 +1375,7 @@
     lax.fori_loop(0, count, sent, 0)
 
 
-def gradient_sums(peers, lefts, rights, lh, dp, wh, wp, vgs):
+def gradient_sums(sections, peers, lefts, rights, lh, dp, near, wh, wp, vgs):
     count = len(lefts)
     rows, width = lefts[0].shape
     hidden = wh.shape[1]
@@ -1303,12 +1393,12 @@
     split_vectors = share % 128 == 0
     cut = share if split_vectors else width
     return pl.pallas_call(
-        partial(sum_kernel, peers, split_vectors),
+        partial(sum_kernel, sections, peers, split_vectors),
         out_shape=(
             shape((count, share, width), F32), shape((share, hidden), F32),
             shape((columns, width), F32), shape((VECTORS, cut), F32),
         ),
-        in_specs=[anywhere] * (2 * count + 4) + [vmem],
+        in_specs=[anywhere] * (2 * count + 5) + [vmem],
         out_specs=[anywhere] * 3 + [vmem],
         scratch_shapes=[
             pltpu.VMEM((count, rows, width), BF16), pltpu.VMEM((count, rows, width), BF16),
@@ -1324,16 +1414,16 @@
             dma((count, chips - 1)), dma((count, chips - 1)),
             dma((count, chips - 1)), dma((count, chips - 1)),
             dma((peers,)), dma((peers,)), dma, dma,
-            dma((chips,)), dma((chips,)), dma((chips,)),
+            dma((2, chips)), dma((2, chips)), dma((2, chips)),
             pltpu.VMEM((count, share, width), F32), pltpu.VMEM((share, hidden), F32),
             pltpu.VMEM((columns, width), F32), pltpu.VMEM((peers, VECTORS, cut), F32),
-            dma((peers,)), dma((peers,)), dma((count,)), dma((peers,)), dma,
+            dma((peers,)), dma((peers,)), dma((count,)), dma((peers,)), dma, dma((2,)),
         ],
         compiler_params=pltpu.CompilerParams(
             collective_id=1, has_side_effects=True, vmem_limit_bytes=63 * 2**20
         ),
         name="gradient_sums",
-    )(*lefts, *rights, lh, dp, wh, wp, vgs)
+    )(*lefts, *rights, lh, dp, near, wh, wp, vgs)
 
 
 def deliver_kernel(count, vectors, *refs):
@@ -1376,7 +1466,7 @@
         in_specs=[vmem] + [anywhere] * 5,
         out_specs=[anywhere] * count + [vmem] * vectors,
         scratch_shapes=[pltpu.VMEM(*kind) for kind in shapes] + [dma((count,)), dma((count,))],
-        compiler_params=pltpu.CompilerParams(vmem_limit_bytes=40 * 2**20),
+        compiler_params=pltpu.CompilerParams(vmem_limit_bytes=63 * 2**20),
         name="deliver",
     )(vec, out, back, hidden, project, squares)
     return found[:count], found[count:]
@@ -1396,10 +1486,10 @@
     vgs, lh = found[13], found[14].reshape(-1, x.shape[2])
     flat = (x.shape[0] * x.shape[1], x.shape[2])
     squares, d_wh, d_wp, vec = gradient_sums(
-        peers,
+        sections, peers,
         [part.reshape(flat) for part in (lf, lgt, lg, lk, lv)],
         [part.reshape(flat) for part in (dsv, datt, dg, dk, dv)],
-        lh, dproj.reshape(flat), matrices[4], matrices[5], vgs,
+        lh, dproj.reshape(flat), found[15].reshape(2, *flat), matrices[4], matrices[5], vgs,
     )
     share = x.shape[2] // peers
     if vec.shape[1] != share:

time: 271 us -> 261 us (0.963)
  local copies, waits for them, and re-layouts: 6.66 us -> 0 us
  Pallas kernels: 263 us -> 260 us
    pallas_call x1, Pallas kernels: 106 us -> 98.2 us  [gradient_sums(): pl.pallas_call(partial(sum_kernel, sections, peers, split_vectors), out_s...]
    unnamed x12 -> x0, local copies, waits for them, and re-layouts: 6.66 us -> none
    pallas_call x1, Pallas kernels: 4.4 us -> 7.68 us  [deliver(): pl.pallas_call(partial(deliver_kernel, count, vectors), out_shape=tuple((...]
where the time goes in v6:
time: 261 us
  Pallas kernels  260 us (100%)
    pallas_call x1, Pallas kernels, relay(): pl.pallas_call(partial(relay_kernel, sections, peers), out_shape=(low, lo...  154 us
    pallas_call x1, Pallas kernels, gradient_sums(): pl.pallas_call(partial(sum_kernel, sections, peers, split_vectors), out_s...  98.2 us
    pallas_call x1, Pallas kernels, deliver(): pl.pallas_call(partial(deliver_kernel, count, vectors), out_shape=tuple((...  7.68 us

profile of v6, /device:TPU:0, one launch (start us, length us, event | category | flops | bytes accessed | tf_op | source)
XLA Modules:
  0.0 261.2 jit_solution(8934341912830513757)
XLA Ops:
  0.7 154.4 %relay.1 = (bf16[2,128,1024]{2,1,0:T(8,128)(2,1)}, bf16[2,128,1024]{2,1,0:T(8,128)(2,1)}, bf16[2,128,1024]{2,1,0:T(8,128)(2,1)}, bf16[2,128,1024]{2,1,0:T(8,128)...) custom-call(s32[2,5]{1,0:T(2,128)} %refs_0_.1, ...), custom_call_target="tpu_custom_call" | custom-call | tf_op jit(solution)/shard_map/relay/pallas_call | solution.py:924
  155.0 98.2 %gradient_sums.1 = (f32[5,128,1024]{2,1,0:T(8,128)}, f32[128,4096]{1,0:T(8,128)}, f32[512,1024]{1,0:T(8,128)}, f32[16,128]{1,0:T(8,128)}) custom-call(bf16[256,1024]{1,0:T(8,128)(2,1)} %bitcast.44, bf16[256,1024]{1,0:T(8,128)(2,1)} %bitcast.43, bf16[256,1024]{1,0:T(8,128)(2,1)} %bitcast.42, bf16[256,1024]{1,0:T(8,128)(2,1)} %bitcast.40, ...), custom_call_target="tpu_custom_call" | custom-call | tf_op jit(solution)/shard_map/gradient_sums/pallas_call | solution.py:1395
  253.3 7.7 %deliver.1 = (bf16[2,128,1024]{2,1,0:T(8,128)(2,1)}, bf16[2,128,1024]{2,1,0:T(8,128)(2,1)}, f32[128,4096]{1,0:T(8,128)}, f32[512,1024]{1,0:T(8,128)}, f32[128,10...) custom-call(f32[16,128]{1,0:T(8,128)} %get-tuple-element.74.refs_0_,, ...), custom_call_target="tpu_custom_call" | custom-call | tf_op jit(solution)/shard_map/deliver/pallas_call | solution.py:1462

commit v7 on v6

--- a/solution.py
+++ b/solution.py
@@ -10,7 +10,7 @@
 EPS = 1e-05
 MESH = pl.DeviceIdType.MESH
 RB = 64
-PARTS = 1
+SLOTS = 4
 VECTORS = 16
 F32 = jnp.float32
 BF16 = jnp.bfloat16
@@ -243,21 +243,11 @@
     def start_halo(m):
         return remote(x_in.at[m, tail], hx.at[m], s_h0.at[m], r_hx.at[m], me_s, right)
 
-    def part_of(j):
-        return pl.ds(pl.multiple_of(j * (width // PARTS), width // PARTS), width // PARTS)
-
-    def result_copy(m, j):
+    def result_copy(m, i):
+        rows = pl.ds(i * RB, RB)
         return remote(
-            out.at[m, :, part_of(j)], xs.at[m, :, part_of(j)],
-            s_x.at[m, j], r_x.at[m, j], above, me,
+            out.at[m, rows], xs.at[m, rows], s_x.at[m, i], r_x.at[m, i], above, me
         )
-
-    def each_part(action):
-        def turn(j, carry):
-            action(j)
-            return carry
-
-        lax.fori_loop(0, PARTS, turn, 0)
 
     def result_halo(m):
         return remote(out.at[m, tail], hx.at[m], s_hx.at[m], r_hx.at[m], above, right)
@@ -385,7 +375,7 @@
             def place(n, source=source, target=target, tall=tall):
                 down = pl.ds(pl.multiple_of(n % tall * edge, edge), edge)
                 along = pl.ds(pl.multiple_of(n // tall * edge, edge), edge)
-                slot = n % 2
+                slot = n % SLOTS
                 return (
                     source.at[down, along],
                     turned.at[slot],
@@ -394,13 +384,13 @@
 
             def turn(n, carry, place=place):
                 piece, buffer, copy = place(n)
-                pl.when(n >= 2)(copy.wait)
+                pl.when(n >= SLOTS)(copy.wait)
                 buffer[...] = piece[...].T
                 copy.start()
                 return carry
 
             lax.fori_loop(0, blocks, turn, 0)
-            for n in range(blocks - 2, blocks):
+            for n in range(blocks - SLOTS, blocks):
                 place(n)[2].wait()
 
     def return_copy(index):
@@ -437,32 +427,34 @@
     def forward(m, carry):
         starts = starts_of(m)
 
-        @pl.when(has_prior)
-        def _():
-            each_part(lambda j: result_copy(m, j).wait_recv())
-
-        @pl.when(has_left)
-        def _():
-            start_halo(m).wait_recv()
-
-        halo_rows, _ = normalise(hx[m].astype(F32))
-        halo_rows = halo_rows * gain1[...] + bias1[...]
-
-        def mix_in(i, last):
-            rows = span_of(i)
+        none = jnp.zeros((1, width), F32)
+
+        def mix_in(start, size, last):
+            rows = pl.ds(start, size)
             spare, spread = normalise(xs[m, rows, :].astype(F32))
             sp1[m, rows, :] = spare
             sd1[m, rows, :] = spread
             normed = spare * gain1[...] + bias1[...]
-            earlier = moved_down(normed, last) * keep_of(column(i), starts)
+            position = base + start + lax.broadcasted_iota(jnp.int32, (size, 1), 0)
+            earlier = moved_down(normed, last) * keep_of(position, starts)
             gap = normed - earlier
             gp1[m, rows, :] = gap.astype(BF16)
             lk[m, rows, :] = (earlier + gap * mix_k[...]).astype(BF16)
             lv[m, rows, :] = (earlier + gap * mix_v[...]).astype(BF16)
             lg[m, rows, :] = (earlier + gap * mix_g[...]).astype(BF16)
-            return normed[RB - 1 : RB]
-
-        lax.fori_loop(0, chunks, mix_in, halo_rows[15:16], unroll=True)
+            return normed[size - 1 : size]
+
+        last = none
+        for i in range(chunks):
+            pl.when(has_prior)(lambda i=i: result_copy(m, i).wait_recv())
+            last = mix_in(i * RB, RB, last)
+
+        @pl.when(has_left)
+        def _():
+            start_halo(m).wait_recv()
+
+        halo_rows, _ = normalise(hx[m].astype(F32))
+        mix_in(0, 16, (halo_rows * gain1[...] + bias1[...])[15:16])
         weight_ready(m, 0)
         weight_ready(m, 1)
         kk[m] = dot_nn(lk[m], wk[...])
@@ -512,7 +504,6 @@
             passing = jnp.where(unbroken, 1.0, 0.0) * decay_tile
             return passing * held + states[m, k]
 
-        none = jnp.zeros((1, width), F32)
         entered = lax.fori_loop(0, me, receive_state, jnp.zeros_like(decay_tile))
         enter_a, enter_b = unpacked(entered, 0), unpacked(entered, 1)
         prior_segment = segment(base - 1, starts)
@@ -572,7 +563,7 @@
 
         for index in range(4, 7):
             weight_ready(m, index)
-        sv[m] = dot_nn(lf[m], wf[...])
+        sv[m] = sigmoid(dot_nn(lf[m], wf[...]))
 
         def widen(j, carry):
             columns = pl.ds(pl.multiple_of(j * width, width), width)
@@ -585,21 +576,12 @@
         release(m, 4)
         release(m, 5)
 
-        def finish(j, carry):
-            columns = part_of(j)
-            found = dot_nn(sq[m], wp[:, columns])
-            proj[m, :, columns] = found
-            sieve = sigmoid(sv[m, :, columns])
-            sv[m, :, columns] = sieve
-            out[m, :, columns] = (mid[m, :, columns] + sieve * found).astype(BF16)
-
-            @pl.when(has_next)
-            def _():
-                result_copy(m, j).start()
-
-            return carry
-
-        lax.fori_loop(0, PARTS, finish, 0)
+        proj[m] = dot_nn(sq[m], wp[...])
+        for i in range(chunks):
+            rows = pl.ds(i * RB, RB)
+            out[m, rows, :] = (mid[m, rows, :] + sv[m, rows, :] * proj[m, rows, :]).astype(BF16)
+            pl.when(has_next)(lambda i=i: result_copy(m, i).start())
+
         release(m, 6)
 
         @pl.when(has_next & has_right)
@@ -622,8 +604,23 @@
 
     start_gathers()
 
-    def add_vector(index, value):
-        vg[index] += fold(value)
+    def add_vectors(n, carry):
+        m, i = n // chunks, n % chunks
+        rows = span_of(i)
+        gap = gp2[m, rows, :].astype(F32)
+        found = {
+            9: mid[m, rows, :] * gap, 10: proj[m, rows, :] * gap,
+            7: sv[m, rows, :] * sp2[m, rows, :], 8: sv[m, rows, :],
+            5: sa[m, rows, :], 6: iv[m, rows, :],
+        }
+        gap = gp1[m, rows, :].astype(F32)
+        found.update({
+            2: kk[m, rows, :] * gap, 3: vv[m, rows, :] * gap, 4: sg[m, rows, :] * gap,
+            0: fo[m, rows, :] * sp1[m, rows, :], 1: fo[m, rows, :],
+        })
+        for index in sorted(found):
+            vg[index] += fold(found[index])
+        return carry
 
     @pl.when(me_s == sections - 1)
     def _():
@@ -638,21 +635,14 @@
         starts = starts_of(m)
         none = jnp.zeros((1, width), F32)
 
-        @pl.when(has_next)
-        def _():
-            each_piece(lambda i: back_copy(m, i).wait_recv())
-
-        def open_back(i, carry):
-            rows = span_of(i)
-            incoming = dys[m, rows, :].astype(F32)
+        for index, (start, size) in enumerate(pieces):
+            pl.when(has_next)(lambda index=index: back_copy(m, index).wait_recv())
+            rows = pl.ds(start, size)
             sieve = sv[m, rows, :]
-            gained = incoming * sieve
+            gained = dys[m, rows, :].astype(F32) * sieve
             dproj[m, rows, :] = gained.astype(BF16)
             dsv[m, rows, :] = (gained * proj[m, rows, :] * (1.0 - sieve)).astype(BF16)
-            return carry
-
-        lax.fori_loop(0, chunks, open_back, 0, unroll=True)
-        t1[...] = jnp.zeros_like(t1)
+
         turned_ready(m, 5)
         turned_ready(m, 6)
 
@@ -660,15 +650,16 @@
             columns = pl.ds(pl.multiple_of(j * width, width), width)
             grown = dot_nn(dproj[m], wh[:, columns])
             dh[m, :, columns] = (grown * 2.0 * act[m, :, columns].astype(F32)).astype(BF16)
-            t1[...] += dot_nn(dh[m, :, columns], wp[columns, :])
             return carry
 
         lax.fori_loop(0, hidden // width, narrow, 0, unroll=True)
+        pl.when(has_right)(lambda: middle_halo(m).wait_send())
+        mid[m] = dot_nn(dh[m], wp[...])
         turned_ready(m, 4)
-        t2[...] = dot_nn(dsv[m], wf[...])
+        proj[m] = dot_nn(dsv[m], wf[...])
 
         def second_earlier(rows, position):
-            whole = t1[rows, :] * (1.0 - mix_h[...]) + t2[rows, :] * (1.0 - mix_f[...])
+            whole = mid[m, rows, :] * (1.0 - mix_h[...]) + proj[m, rows, :] * (1.0 - mix_f[...])
             return whole * keep_of(position, starts)
 
         eight = lax.broadcasted_iota(jnp.int32, (8, 1), 0)
@@ -681,18 +672,14 @@
         def back_second(start, size, following):
             rows = pl.ds(start, size)
             spare, spread = sp2[m, rows, :], sd2[m, rows, :]
-            gap = gp2[m, rows, :].astype(F32)
             position = base + start + lax.broadcasted_iota(jnp.int32, (size, 1), 0)
             kept = keep_of(position, starts)
-            from_h = t1[rows, :]
-            from_f = t2[rows, :]
-            add_vector(9, from_h * gap)
-            add_vector(10, from_f * gap)
+            from_h = mid[m, rows, :]
+            from_f = proj[m, rows, :]
             straight = from_h * mix_h[...] + from_f * mix_f[...]
             earlier = (from_h + from_f - straight) * kept
             d_normed = straight + moved_up(earlier, following)
-            add_vector(7, d_normed * spare)
-            add_vector(8, d_normed)
+            sv[m, rows, :] = d_normed
             scaled = d_normed * gain2[...]
             mean_one = jnp.mean(scaled, axis=-1, keepdims=True)
             mean_two = jnp.mean(scaled * spare, axis=-1, keepdims=True)
@@ -750,8 +737,7 @@
             dg[m, rows, :] = (d_found * found * (1.0 - gate)).astype(BF16)
             gained = d_found * iv[m, rows, :] * (boost * kk[m, rows, :])
             d_key = gained * (vv[m, rows, :] - found)
-            add_vector(6, d_key)
-            t1[rows, :] = d_key
+            iv[m, rows, :] = d_key
             t2[rows, :] = gained
             return carry
 
@@ -779,24 +765,24 @@
             held = rising * chosen
             d_a = grown * acc[rows, 0:width] + held * enter_a
             d_b = grown * acc[rows, width:] + held * enter_b
-            add_vector(5, d_a * sa[m, rows, :] + d_b * sb[m, rows, :])
+            sa[m, rows, :] = d_a * sa[m, rows, :] + d_b * sb[m, rows, :]
             weight = kk[m, rows, :]
             dv[m, rows, :] = (t2[rows, :] + d_a * weight).astype(BF16)
-            dk[m, rows, :] = (t1[rows, :] + (d_a * vv[m, rows, :] + d_b) * weight).astype(BF16)
+            dk[m, rows, :] = (iv[m, rows, :] + (d_a * vv[m, rows, :] + d_b) * weight).astype(BF16)
             return carry
 
         lax.fori_loop(0, chunks, back_keys, 0, unroll=True)
         for index in range(3):
             turned_ready(m, index)
-        t1[...] = dot_nn(dk[m], wk[...])
-        t2[...] = dot_nn(dv[m], wv[...])
-        acc[:, 0:width] = dot_nn(dg[m], wg[...])
+        kk[m] = dot_nn(dk[m], wk[...])
+        vv[m] = dot_nn(dv[m], wv[...])
+        sg[m] = dot_nn(dg[m], wg[...])
 
         def first_earlier(rows, position):
             whole = (
-                t1[rows, :] * (1.0 - mix_k[...])
-                + t2[rows, :] * (1.0 - mix_v[...])
-                + acc[rows, 0:width] * (1.0 - mix_g[...])
+                kk[m, rows, :] * (1.0 - mix_k[...])
+                + vv[m, rows, :] * (1.0 - mix_v[...])
+                + sg[m, rows, :] * (1.0 - mix_g[...])
             )
             return whole * keep_of(position, starts)
 
@@ -814,20 +800,15 @@
             start, size = pieces[index]
             rows = pl.ds(start, size)
             spare, spread = sp1[m, rows, :], sd1[m, rows, :]
-            gap = gp1[m, rows, :].astype(F32)
             position = base + start + lax.broadcasted_iota(jnp.int32, (size, 1), 0)
             kept = keep_of(position, starts)
-            from_k = t1[rows, :]
-            from_v = t2[rows, :]
-            from_g = acc[rows, 0:width]
-            add_vector(2, from_k * gap)
-            add_vector(3, from_v * gap)
-            add_vector(4, from_g * gap)
+            from_k = kk[m, rows, :]
+            from_v = vv[m, rows, :]
+            from_g = sg[m, rows, :]
             straight = from_k * mix_k[...] + from_v * mix_v[...] + from_g * mix_g[...]
             earlier = (from_k + from_v + from_g - straight) * kept
             d_normed = straight + moved_up(earlier, following)
-            add_vector(0, d_normed * spare)
-            add_vector(1, d_normed)
+            fo[m, rows, :] = d_normed
             scaled = d_normed * gain1[...]
             mean_one = jnp.mean(scaled, axis=-1, keepdims=True)
             mean_two = jnp.mean(scaled * spare, axis=-1, keepdims=True)
@@ -859,6 +840,7 @@
             send_near(m)
 
 
+    lax.fori_loop(0, batches * chunks, add_vectors, 0)
     vgs[...] = jnp.sum(vg[...], axis=1)
     vgs[5:6] = vgs[5:6] * (-rate * jnp.exp(-rate))
     def close(m, carry):
@@ -868,15 +850,12 @@
 
         @pl.when(has_next)
         def _():
-            each_part(lambda j: result_copy(m, j).wait_send())
+            for i in range(chunks):
+                result_copy(m, i).wait_send()
 
         @pl.when(has_next & has_right)
         def _():
             result_halo(m).wait_send()
-
-        @pl.when(has_right)
-        def _():
-            middle_halo(m).wait_send()
 
         @pl.when(has_left)
         def _():
@@ -937,7 +916,7 @@
         out_specs=[anywhere] * 13 + [vmem] + [anywhere] * 9,
         scratch_shapes=[narrow(BF16)] * 13 + [
             narrow(BF16), pltpu.VMEM((batches, rows, hidden), BF16),
-            pltpu.VMEM((batches, rows, hidden), BF16), pltpu.VMEM((2, 512, 512), BF16),
+            pltpu.VMEM((batches, rows, hidden), BF16), pltpu.VMEM((SLOTS, 512, 512), BF16),
         ]
         + [pltpu.VMEM(matrix.shape, BF16) for matrix in matrices_order(matrices)]
         + [
@@ -960,15 +939,15 @@
             narrow(F32), narrow(BF16), pltpu.VMEM((batches, rows, 1), F32),
             narrow(F32), narrow(F32),
             dma((7,)), dma, dma,
-            dma((batches,)), dma((batches, PARTS)), dma((batches,)), dma((batches, peers)),
+            dma((batches,)), dma((batches, rows // RB)), dma((batches,)), dma((batches, peers)),
             dma((batches,)), dma((batches, 3)), dma((batches,)), dma((batches, peers)),
             dma((batches,)),
-            dma((batches, PARTS)), dma((batches,)), dma((batches, peers)), dma((batches,)),
+            dma((batches, rows // RB)), dma((batches,)), dma((batches, peers)), dma((batches,)),
             dma((batches, 3)), dma((batches,)), dma((batches, peers)), dma((batches,)),
             dma((13, batches)),
             dma((batches, peers // 2)), dma((batches, peers // 2)), dma((batches,)),
             dma((2, batches)), dma((2, batches)),
-            dma((2,)), dma((7,)),
+            dma((SLOTS,)), dma((7,)),
         ],
         compiler_params=pltpu.CompilerParams(
             collective_id=0, has_side_effects=True, vmem_limit_bytes=63 * 2**20

time: 261 us -> 258 us (0.989)
  Pallas kernels: 260 us -> 256 us
    pallas_call x1, Pallas kernels: 154 us -> 150 us  [relay(): pl.pallas_call(partial(relay_kernel, sections, peers), out_shape=(low, lo...]
where the time goes in v7:
time: 258 us; the launch traced here: 257 us
  Pallas kernels  256 us (99%)
    pallas_call x1, Pallas kernels, relay(): pl.pallas_call(partial(relay_kernel, sections, peers), out_shape=(low, lo...  150 us
    pallas_call x1, Pallas kernels, gradient_sums(): pl.pallas_call(partial(sum_kernel, sections, peers, split_vectors), out_s...  98.2 us
    pallas_call x1, Pallas kernels, deliver(): pl.pallas_call(partial(deliver_kernel, count, vectors), out_shape=tuple((...  7.68 us

profile of v7, /device:TPU:0, one launch (start us, length us, event | category | flops | bytes accessed | tf_op | source)
XLA Modules:
  0.0 257.3 jit_solution(796466358146521031)
XLA Ops:
  0.7 150.5 %relay.1 = (bf16[2,128,1024]{2,1,0:T(8,128)(2,1)}, bf16[2,128,1024]{2,1,0:T(8,128)(2,1)}, bf16[2,128,1024]{2,1,0:T(8,128)(2,1)}, bf16[2,128,1024]{2,1,0:T(8,128)...) custom-call(s32[2,5]{1,0:T(2,128)} %refs_0_.1, ...), custom_call_target="tpu_custom_call" | custom-call | tf_op jit(solution)/shard_map/relay/pallas_call | solution.py:903
  151.2 98.2 %gradient_sums.1 = (f32[5,128,1024]{2,1,0:T(8,128)}, f32[128,4096]{1,0:T(8,128)}, f32[512,1024]{1,0:T(8,128)}, f32[16,128]{1,0:T(8,128)}) custom-call(bf16[256,1024]{1,0:T(8,128)(2,1)} %bitcast.44, bf16[256,1024]{1,0:T(8,128)(2,1)} %bitcast.43, bf16[256,1024]{1,0:T(8,128)(2,1)} %bitcast.42, bf16[256,1024]{1,0:T(8,128)(2,1)} %bitcast.40, ...), custom_call_target="tpu_custom_call" | custom-call | tf_op jit(solution)/shard_map/gradient_sums/pallas_call | solution.py:1374
  249.4 7.7 %deliver.1 = (bf16[2,128,1024]{2,1,0:T(8,128)(2,1)}, bf16[2,128,1024]{2,1,0:T(8,128)(2,1)}, f32[128,4096]{1,0:T(8,128)}, f32[512,1024]{1,0:T(8,128)}, f32[128,10...) custom-call(f32[16,128]{1,0:T(8,128)} %get-tuple-element.74.refs_0_,, ...), custom_call_target="tpu_custom_call" | custom-call | tf_op jit(solution)/shard_map/deliver/pallas_call | solution.py:1441

commit v8 on v7

--- a/solution.py
+++ b/solution.py
@@ -10,7 +10,6 @@
 EPS = 1e-05
 MESH = pl.DeviceIdType.MESH
 RB = 64
-SLOTS = 4
 VECTORS = 16
 F32 = jnp.float32
 BF16 = jnp.bfloat16
@@ -213,7 +212,6 @@
         + jnp.where(has_next & has_right, 1, 0)
         + jnp.where(has_prior & has_left, 1, 0)
     )
-    pl.semaphore_wait(barrier, greeted)
     for copy in weight_copies[2:7]:
         copy.start()
 
@@ -348,11 +346,6 @@
             each_chip(lambda k: gather_copy(m, k, chip).wait_send())
             each_chip(lambda k: gather_copy(m, k, k).wait_recv())
 
-    @pl.when((me_s == 0) & has_right)
-    def _():
-        for m in range(batches):
-            start_halo(m).start()
-
     @pl.when(me_s == 0)
     def _():
         pltpu.make_async_copy(x_in, xs, x_sem).wait()
@@ -363,7 +356,7 @@
     returns = (
         (wk_t, wk), (wv_t, wv), (wg_t, wg), (wo_t, wo), (wf_t, wf), (wp_t, wh), (wh_t, wp)
     )
-    edge = turned.shape[1]
+    slots, edge = turned.shape[0], turned.shape[1]
 
     def transpose_all(fresh):
         for index, (source, target) in enumerate(turns):
@@ -375,7 +368,7 @@
             def place(n, source=source, target=target, tall=tall):
                 down = pl.ds(pl.multiple_of(n % tall * edge, edge), edge)
                 along = pl.ds(pl.multiple_of(n // tall * edge, edge), edge)
-                slot = n % SLOTS
+                slot = n % slots
                 return (
                     source.at[down, along],
                     turned.at[slot],
@@ -384,13 +377,13 @@
 
             def turn(n, carry, place=place):
                 piece, buffer, copy = place(n)
-                pl.when(n >= SLOTS)(copy.wait)
+                pl.when(n >= slots)(copy.wait)
                 buffer[...] = piece[...].T
                 copy.start()
                 return carry
 
             lax.fori_loop(0, blocks, turn, 0)
-            for n in range(blocks - SLOTS, blocks):
+            for n in range(blocks - slots, blocks):
                 place(n)[2].wait()
 
     def return_copy(index):
@@ -399,14 +392,12 @@
 
 
     def release(m, index):
-        @pl.when(is_late & (m == batches - 1))
-        def _():
-            return_copy(index).start()
+        if m == batches - 1:
+            pl.when(is_late)(lambda: return_copy(index).start())
 
     def weight_ready(m, index, fresh=True):
-        @pl.when((m == 0) & jnp.logical_not(is_late))
-        def _():
-            weight_copies[index].wait()
+        if m == 0:
+            pl.when(jnp.logical_not(is_late))(lambda: weight_copies[index].wait())
 
     def span_of(i):
         return pl.ds(pl.multiple_of(i * RB, RB), RB)
@@ -448,6 +439,14 @@
         for i in range(chunks):
             pl.when(has_prior)(lambda i=i: result_copy(m, i).wait_recv())
             last = mix_in(i * RB, RB, last)
+
+        if m == 0:
+            pl.semaphore_wait(barrier, greeted)
+
+            @pl.when((me_s == 0) & has_right)
+            def _():
+                for n in range(batches):
+                    start_halo(n).start()
 
         @pl.when(has_left)
         def _():
@@ -594,7 +593,8 @@
         return carry
 
     pl.when(is_late)(lambda: transpose_all(True))
-    lax.fori_loop(0, batches, forward, 0)
+    for m in range(batches):
+        forward(m, 0)
 
     @pl.when(jnp.logical_not(is_late))
     def _():
@@ -627,8 +627,7 @@
         pltpu.make_async_copy(top_in, dys, top_sem).wait()
 
     def turned_ready(m, index):
-        @pl.when(m == 0)
-        def _():
+        if m == 0:
             return_copy(index).wait()
 
     def backward(m, carry):
@@ -831,7 +830,8 @@
         store_copy(12, m).start()
         return carry
 
-    lax.fori_loop(0, batches, backward, 0)
+    for m in range(batches):
+        backward(m, 0)
     pl.when(has_prior)(lambda: each_piece(lambda i: back_copy(batches - 1, i).wait_send()))
 
     @pl.when(me_s > 0)
@@ -890,6 +890,7 @@
 def relay(sections, peers, x, top, spans, vectors, matrices):
     batches, rows, width = x.shape
     hidden = matrices[4].shape[1]
+    slots = 4 if peers <= 8 else 2
     shape = jax.ShapeDtypeStruct
     low = shape((batches, rows, width), BF16)
     square = shape((width, width), BF16)
@@ -916,7 +917,7 @@
         out_specs=[anywhere] * 13 + [vmem] + [anywhere] * 9,
         scratch_shapes=[narrow(BF16)] * 13 + [
             narrow(BF16), pltpu.VMEM((batches, rows, hidden), BF16),
-            pltpu.VMEM((batches, rows, hidden), BF16), pltpu.VMEM((SLOTS, 512, 512), BF16),
+            pltpu.VMEM((batches, rows, hidden), BF16), pltpu.VMEM((slots, 512, 512), BF16),
         ]
         + [pltpu.VMEM(matrix.shape, BF16) for matrix in matrices_order(matrices)]
         + [
@@ -947,7 +948,7 @@
             dma((13, batches)),
             dma((batches, peers // 2)), dma((batches, peers // 2)), dma((batches,)),
             dma((2, batches)), dma((2, batches)),
-            dma((SLOTS,)), dma((7,)),
+            dma((slots,)), dma((7,)),
         ],
         compiler_params=pltpu.CompilerParams(
             collective_id=0, has_side_effects=True, vmem_limit_bytes=63 * 2**20
@@ -971,7 +972,7 @@
         left_sem, right_sem, lh_sem, dp_sem, wh_sem, wp_sem,
         s_pair, r_pair, s_right, r_right, s_left, r_left, s_hid, r_hid, s_proj, r_proj,
         s_ahead, s_behind, r_rows,
-        outs, wh_out, wp_out, vgr, s_vg, r_vg, outs_sem, wh_out_sem, wp_out_sem,
+        total, wh_out, wp_out, vgr, s_vg, r_vg, outs_sem, wh_out_sem, wp_out_sem,
         near_sem,
     ) = refs[20:]
     count = len(left_in)
@@ -1161,32 +1162,33 @@
 
     def hidden_store(j):
         place = pl.ds(pl.multiple_of(j * columns, columns), columns)
-        return pltpu.make_async_copy(wh_out.at[:, place], wh_hbm.at[:, place], wh_out_sem.at[j])
+        return pltpu.make_async_copy(hid_in.at[:, place], wh_hbm.at[:, place], wh_out_sem.at[j])
 
     def close_hidden(j):
         hid_copy(j).wait_recv()
         place = pl.ds(pl.multiple_of(j * columns, columns), columns)
-        wh_out[:, place] += hid_in[:, place].astype(F32)
+        hid_in[:, place] = (wh_out[:, place] + hid_in[:, place].astype(F32)).astype(BF16)
         hidden_store(j).start()
 
     def sum_store(w):
-        return pltpu.make_async_copy(outs.at[w], outs_hbm.at[w], outs_sem.at[w])
-
-    proj_store = pltpu.make_async_copy(wp_out, wp_hbm, wp_out_sem)
+        return pltpu.make_async_copy(own.at[w, chip], outs_hbm.at[w], outs_sem.at[w])
+
+    proj_store = pltpu.make_async_copy(proj_in, wp_hbm, wp_out_sem)
 
     def close_sum(w):
-        outs[w] = own[w, chip].astype(F32)
+        total[...] = own[w, chip].astype(F32)
 
         @pl.when(has_left)
         def _():
             right_copy(own.at[w, 0], w, rounds - 1).wait_recv()
-            outs[w] += going_right[w, rounds - 1].astype(F32)
+            total[...] += going_right[w, rounds - 1].astype(F32)
 
         @pl.when(has_right)
         def _():
             left_copy(own.at[w, 0], w, rounds - 1).wait_recv()
-            outs[w] += going_left[w, rounds - 1].astype(F32)
-
+            total[...] += going_left[w, rounds - 1].astype(F32)
+
+        own[w, chip] = total[...].astype(BF16)
         sum_store(w).start()
 
     def feed(j):
@@ -1292,7 +1294,7 @@
 
     close_hidden(peers - 1)
     proj_copy.wait_recv()
-    wp_out[...] += proj_in[...].astype(F32)
+    proj_in[...] = (wp_out[...] + proj_in[...].astype(F32)).astype(BF16)
     proj_store.start()
 
     def collect(k):
@@ -1374,8 +1376,8 @@
     return pl.pallas_call(
         partial(sum_kernel, sections, peers, split_vectors),
         out_shape=(
-            shape((count, share, width), F32), shape((share, hidden), F32),
-            shape((columns, width), F32), shape((VECTORS, cut), F32),
+            shape((count, share, width), BF16), shape((share, hidden), BF16),
+            shape((columns, width), BF16), shape((VECTORS, cut), F32),
         ),
         in_specs=[anywhere] * (2 * count + 5) + [vmem],
         out_specs=[anywhere] * 3 + [vmem],
@@ -1394,7 +1396,7 @@
             dma((count, chips - 1)), dma((count, chips - 1)),
             dma((peers,)), dma((peers,)), dma, dma,
             dma((2, chips)), dma((2, chips)), dma((2, chips)),
-            pltpu.VMEM((count, share, width), F32), pltpu.VMEM((share, hidden), F32),
+            pltpu.VMEM((share, width), F32), pltpu.VMEM((share, hidden), F32),
             pltpu.VMEM((columns, width), F32), pltpu.VMEM((peers, VECTORS, cut), F32),
             dma((peers,)), dma((peers,)), dma((count,)), dma((peers,)), dma, dma((2,)),
         ],
@@ -1409,7 +1411,8 @@
     vec, sources = refs[0], refs[1:6]
     targets = refs[6 : 6 + count]
     rows = refs[6 + count : 6 + count + vectors]
-    buffers = refs[6 + count + vectors : -2]
+    buffers = refs[6 + count + vectors : 6 + 2 * count + vectors]
+    wide = refs[6 + 2 * count + vectors : -2]
     in_sem, out_sem = refs[-2:]
     pieces = list(sources[:-1]) + [sources[-1].at[w] for w in range(count - 4)]
     enter = [
@@ -1418,14 +1421,16 @@
     ]
     leave = [
         pltpu.make_async_copy(buffer, target, out_sem.at[index])
-        for index, (buffer, target) in enumerate(zip(buffers, targets))
+        for index, (buffer, target) in enumerate(zip(buffers[:2] + wide, targets))
     ]
     for copy in enter:
         copy.start()
     for index, row in enumerate(rows):
         row[...] = vec[index : index + 1, :]
-    for first, second in zip(enter, leave):
+    for index, (first, second) in enumerate(zip(enter, leave)):
         first.wait()
+        if index >= 2:
+            wide[index - 2][...] = buffers[index][...].astype(F32)
         second.start()
     for copy in leave:
         copy.wait()
@@ -1444,7 +1449,9 @@
         + (jax.ShapeDtypeStruct((1, vec.shape[1]), F32),) * vectors,
         in_specs=[vmem] + [anywhere] * 5,
         out_specs=[anywhere] * count + [vmem] * vectors,
-        scratch_shapes=[pltpu.VMEM(*kind) for kind in shapes] + [dma((count,)), dma((count,))],
+        scratch_shapes=[pltpu.VMEM(kind[0], BF16) for kind in shapes]
+        + [pltpu.VMEM(*kind) for kind in shapes[2:]]
+        + [dma((count,)), dma((count,))],
         compiler_params=pltpu.CompilerParams(vmem_limit_bytes=63 * 2**20),
         name="deliver",
     )(vec, out, back, hidden, project, squares)

time: 258 us -> 252 us (0.977)
  Pallas kernels: 256 us -> 251 us
    pallas_call x1, Pallas kernels: 150 us -> 147 us  [relay(): pl.pallas_call(partial(relay_kernel, sections, peers), out_shape=(low, lo...]
where the time goes in v8:
time: 252 us
  Pallas kernels  251 us (100%)
    pallas_call x1, Pallas kernels, relay(): pl.pallas_call(partial(relay_kernel, sections, peers), out_shape=(low, lo...  147 us
    pallas_call x1, Pallas kernels, gradient_sums(): pl.pallas_call(partial(sum_kernel, sections, peers, split_vectors), out_s...  98.2 us
    pallas_call x1, Pallas kernels, deliver(): pl.pallas_call(partial(deliver_kernel, count, vectors), out_shape=tuple((...  5.91 us

profile of v8, /device:TPU:0, one launch (start us, length us, event | category | flops | bytes accessed | tf_op | source)
XLA Modules:
  0.0 252.2 jit_solution(17986965500506253326)
XLA Ops:
  0.7 147.2 %relay.1 = (bf16[2,128,1024]{2,1,0:T(8,128)(2,1)}, bf16[2,128,1024]{2,1,0:T(8,128)(2,1)}, bf16[2,128,1024]{2,1,0:T(8,128)(2,1)}, bf16[2,128,1024]{2,1,0:T(8,128)...) custom-call(s32[2,5]{1,0:T(2,128)} %refs_0_.1, ...), custom_call_target="tpu_custom_call" | custom-call | tf_op jit(solution)/shard_map/relay/pallas_call | solution.py:904
  147.9 98.2 %gradient_sums.1 = (bf16[5,128,1024]{2,1,0:T(8,128)(2,1)}, bf16[128,4096]{1,0:T(8,128)(2,1)}, bf16[512,1024]{1,0:T(8,128)(2,1)}, f32[16,128]{1,0:T(8,128)}) custom-call(bf16[256,1024]{1,0:T(8,128)(2,1)} %bitcast.44, bf16[256,1024]{1,0:T(8,128)(2,1)} %bitcast.43, bf16[256,1024]{1,0:T(8,128)(2,1)} %bitcast.42, bf16[256,1024]{1,0:T(8,128)(2,1)} %bitcast.40, ...), custom_call_target="tpu_custom_call" | custom-call | tf_op jit(solution)/shard_map/gradient_sums/pallas_call | solution.py:1376
  246.1 5.9 %deliver.1 = (bf16[2,128,1024]{2,1,0:T(8,128)(2,1)}, bf16[2,128,1024]{2,1,0:T(8,128)(2,1)}, f32[128,4096]{1,0:T(8,128)}, f32[512,1024]{1,0:T(8,128)}, f32[128,10...) custom-call(f32[16,128]{1,0:T(8,128)} %get-tuple-element.74.refs_0_,, ...), custom_call_target="tpu_custom_call" | custom-call | tf_op jit(solution)/shard_map/deliver/pallas_call | solution.py:1446
